TPU v7x, 32 devices: a whole 2x2x4 slice. The times are simulated.
32 devices in a mesh: parts: 2 (over y), expert: 4 (over z), replica: 4 (over x, core).
Axes of the slice: x: 2, y: 2, z: 4, core: 2. Of those that a mesh axis runs over, the one named last changes fastest.
Arguments:
- tokens: bfloat16 [4096, 2048], P(('parts', 'expert', 'replica')), parts along dimension 0, may hold values from -6 to 6
- out_grad: bfloat16 [4096, 2048], P(('parts', 'expert', 'replica')), parts along dimension 0, may hold values from -4 to 4
- expert_ids: int32 [4096, 2], P(('parts', 'expert', 'replica')), parts along dimension 0, may hold values from 0 to 3, all different within a row; in each aligned block of 128 rows (0 to 127, 128 to 255, ...) at most 128 rows name the same one
- gates: bfloat16 [4096, 2], P(('parts', 'expert', 'replica')), parts along dimension 0, may hold values from 0.099609375 to 1
- gate_weight: bfloat16 [4, 2048, 1024], P('expert', None, 'replica'), may hold values from -0.125 to 0.125
- up_weight: bfloat16 [4, 2048, 1024], P('expert', None, 'replica'), may hold values from -0.125 to 0.125
- down_weight: bfloat16 [4, 2048, 1024], P('expert', None, 'replica'), may hold values from -0.125 to 0.125
Outputs:
- token_grad: bfloat16 [4096, 2048], P(('parts', 'expert', 'replica')), parts along dimension 0
- gate_grad: bfloat16 [4096, 2], P(('parts', 'expert', 'replica')), parts along dimension 0
- gate_weight_grad: bfloat16 [8, 2048, 1024], P(('parts', 'expert'), None, 'replica'), parts along dimension 0
- up_weight_grad: bfloat16 [8, 2048, 1024], P(('parts', 'expert'), None, 'replica'), parts along dimension 0
- down_weight_grad: bfloat16 [8, 2048, 1024], P(('parts', 'expert'), None, 'replica'), parts along dimension 0
There are 2 independent parts, one for each index of `parts`. A program takes and returns all parts, laid end to end along the dimension named above; an argument that names none is the same for every part. Nothing has to cross between parts.
Inputs may be any that keep to these rules, and one draw needn't show every extreme that they name: `expert_ids`: among the 128 rows of one device (aligned blocks), no expert is named by more than 128 rows, and in some blocks one expert is named by exactly 128 rows; each row names two different experts; busy experts carry several times the mean load.
All inputs are finite; a program needn't handle non-finite values.
Results may differ from a plain program's by a relative error of at most 0.009.
Values may be sent and summed in bfloat16 or wider, within the bound.
No kernel may reach another device: no remote copies, remote signals or barrier semaphores. Data moves between devices by JAX's collectives and lax.ppermute only.
A program may use at most 128 MiB of HBM per device.

v0:
```python
import functools

import jax
import jax.numpy as jnp
from jax import lax
from jax.experimental import pallas as pl
from jax.experimental.pallas import tpu as pltpu
from jax.sharding import PartitionSpec as P

row_block = 256


def swiglu_backward(rows_in, rows_grad, rows_scaled, rows_gate, weight_g, weight_u, weight_d):
    pre_gate = jnp.dot(rows_in, weight_g, preferred_element_type=jnp.float32)
    pre_up = jnp.dot(rows_in, weight_u, preferred_element_type=jnp.float32)
    back_proj = jnp.dot(rows_grad, weight_d, preferred_element_type=jnp.float32)
    sigmoid_g = jax.nn.sigmoid(pre_gate)
    activated = pre_gate * sigmoid_g
    hidden_act = activated * pre_up
    gate_part = jnp.sum(back_proj * hidden_act, axis=1)
    grad_hidden = rows_gate[:, None] * back_proj
    grad_gate_pre = (
        grad_hidden * pre_up * sigmoid_g * (1.0 + pre_gate * (1.0 - sigmoid_g))
    ).astype(jnp.bfloat16)
    grad_up_pre = (grad_hidden * activated).astype(jnp.bfloat16)
    hidden_rounded = hidden_act.astype(jnp.bfloat16)
    contract_last = (((1,), (1,)), ((), ()))
    contract_first = (((0,), (0,)), ((), ()))
    input_grad = lax.dot_general(
        grad_gate_pre, weight_g, contract_last, preferred_element_type=jnp.float32
    )
    input_grad = input_grad + lax.dot_general(
        grad_up_pre, weight_u, contract_last, preferred_element_type=jnp.float32
    )
    add_gate = lax.dot_general(
        rows_in, grad_gate_pre, contract_first, preferred_element_type=jnp.float32
    )
    add_up = lax.dot_general(
        rows_in, grad_up_pre, contract_first, preferred_element_type=jnp.float32
    )
    add_down = lax.dot_general(
        rows_scaled, hidden_rounded, contract_first, preferred_element_type=jnp.float32
    )
    return (input_grad, gate_part, add_gate, add_up, add_down)


def hidden_part(state_now, pieces, first, row_data):
    gate_piece = pieces[0][0]
    up_piece = pieces[1][0]
    down_piece = pieces[2][0]
    rows_in, rows_grad, rows_scaled, rows_gate, block_total = row_data
    grad_g, grad_u, grad_d, input_acc, gate_acc = state_now
    packed = rows_in.shape[0]
    block_limit = packed // row_block

    def make_branch(block_count):
        row_total = block_count * row_block

        def branch(unused):
            input_grad, gate_part, add_g, add_u, add_d = swiglu_backward(
                rows_in[:row_total],
                rows_grad[:row_total],
                rows_scaled[:row_total],
                rows_gate[:row_total],
                gate_piece,
                up_piece,
                down_piece,
            )
            spare = packed - row_total
            input_grad = jnp.pad(input_grad, ((0, spare), (0, 0)))
            gate_part = jnp.pad(gate_part, ((0, spare),))
            return (input_grad, gate_part, add_g, add_u, add_d)

        return branch

    branches = [make_branch(count) for count in range(1, block_limit + 1)]
    which = jnp.clip(block_total - 1, 0, block_limit - 1)
    input_grad, gate_part, add_g, add_u, add_d = lax.switch(which, branches, 0)
    grad_g = lax.dynamic_update_slice_in_dim(grad_g, add_g, first, 1)
    grad_u = lax.dynamic_update_slice_in_dim(grad_u, add_u, first, 1)
    grad_d = lax.dynamic_update_slice_in_dim(grad_d, add_d, first, 1)
    return (grad_g, grad_u, grad_d, input_acc + input_grad, gate_acc + gate_part)


def general_body(tokens, out_grad, expert_ids, gates, gate_weight, up_weight, down_weight):
    tok_rows, feature_width = tokens.shape
    owners = lax.axis_size("expert")
    capacity = min(tok_rows, max(2, 6 * tok_rows // owners))
    slot_count = 2 * tok_rows
    flat_ids = expert_ids.reshape(-1)
    onehot = (flat_ids[:, None] == jnp.arange(owners, dtype=jnp.int32)[None, :]).astype(jnp.int32)
    before = jnp.cumsum(onehot, axis=0) - onehot
    position = jnp.sum(before * onehot, axis=1)
    target = flat_ids * capacity + position
    source = (
        jnp.full((owners * capacity,), slot_count, jnp.int32)
        .at[target]
        .set(jnp.arange(slot_count, dtype=jnp.int32))
    )
    in_ext = jnp.concatenate([tokens, jnp.zeros((1, feature_width), jnp.bfloat16)])
    grad_ext = jnp.concatenate([out_grad, jnp.zeros((1, feature_width), jnp.bfloat16)])
    gate_ext = jnp.concatenate([gates.reshape(-1), jnp.zeros((1,), jnp.bfloat16)])
    send_in = in_ext[source // 2].reshape(owners, capacity, feature_width)
    send_grad = grad_ext[source // 2].reshape(owners, capacity, feature_width)
    send_gate = gate_ext[source].reshape(owners, capacity)
    recv_in, recv_grad, recv_gate = (
        lax.all_to_all(send_in, "expert", split_axis=0, concat_axis=0, tiled=True),
        lax.all_to_all(send_grad, "expert", split_axis=0, concat_axis=0, tiled=True),
        lax.all_to_all(send_gate, "expert", split_axis=0, concat_axis=0, tiled=True),
    )
    recv_slots = owners * capacity
    live_rows = (recv_gate.reshape(-1) > 0).astype(jnp.int32)
    packed_pos = jnp.cumsum(live_rows) - live_rows
    live_total = jnp.sum(live_rows)
    packed = (recv_slots + row_block - 1) // row_block * row_block
    unpack = jnp.where(live_rows > 0, packed_pos, packed)
    pack_index = (
        jnp.full((packed,), recv_slots, jnp.int32)
        .at[unpack]
        .set(jnp.arange(recv_slots, dtype=jnp.int32), mode="drop")
    )
    rows_in = jnp.concatenate(
        [recv_in.reshape(recv_slots, feature_width), jnp.zeros((1, feature_width), jnp.bfloat16)]
    )[pack_index]
    rows_grad = jnp.concatenate(
        [recv_grad.reshape(recv_slots, feature_width), jnp.zeros((1, feature_width), jnp.bfloat16)]
    )[pack_index]
    rows_gate = jnp.concatenate([recv_gate.reshape(-1), jnp.zeros((1,), jnp.bfloat16)])[
        pack_index
    ].astype(jnp.float32)
    rows_scaled = (rows_gate[:, None] * rows_grad.astype(jnp.float32)).astype(jnp.bfloat16)
    block_total = (live_total + row_block - 1) // row_block
    row_data = (rows_in, rows_grad, rows_scaled, rows_gate, block_total)
    hidden_units = gate_weight.shape[2] * lax.axis_size("replica")
    zero_grad = jnp.zeros((feature_width, hidden_units), jnp.float32)
    start_state = (
        zero_grad,
        zero_grad,
        zero_grad,
        jnp.zeros((packed, feature_width), jnp.float32),
        jnp.zeros((packed,), jnp.float32),
    )
    complete = (
        lax.all_gather(gate_weight, "replica", axis=2, tiled=True),
        lax.all_gather(up_weight, "replica", axis=2, tiled=True),
        lax.all_gather(down_weight, "replica", axis=2, tiled=True),
    )
    final = hidden_part(start_state, complete, 0, row_data)
    grad_g, grad_u, grad_d, input_acc, gate_acc = final
    packed_grad = jnp.concatenate(
        [input_acc.astype(jnp.bfloat16), jnp.zeros((1, feature_width), jnp.bfloat16)]
    )
    packed_gate = jnp.concatenate([gate_acc.astype(jnp.bfloat16), jnp.zeros((1,), jnp.bfloat16)])
    back_grad = packed_grad[unpack].reshape(owners, capacity, feature_width)
    back_gate = packed_gate[unpack].reshape(owners, capacity)
    ret_grad, ret_gate = (
        lax.all_to_all(back_grad, "expert", split_axis=0, concat_axis=0, tiled=True),
        lax.all_to_all(back_gate, "expert", split_axis=0, concat_axis=0, tiled=True),
    )
    slot_grad = ret_grad.reshape(recv_slots, feature_width)[target].reshape(
        tok_rows, 2, feature_width
    )
    token_grad = slot_grad.astype(jnp.float32).sum(axis=1).astype(jnp.bfloat16)
    gate_grad = ret_gate.reshape(-1)[target].reshape(tok_rows, 2)
    shares = (
        lax.psum_scatter(
            grad_g.astype(jnp.bfloat16), "replica", scatter_dimension=1, tiled=True
        ).astype(jnp.float32),
        lax.psum_scatter(
            grad_u.astype(jnp.bfloat16), "replica", scatter_dimension=1, tiled=True
        ).astype(jnp.float32),
        lax.psum_scatter(
            grad_d.astype(jnp.bfloat16), "replica", scatter_dimension=1, tiled=True
        ).astype(jnp.float32),
    )
    return (
        token_grad,
        gate_grad,
        shares[0].astype(jnp.bfloat16)[None],
        shares[1].astype(jnp.bfloat16)[None],
        shares[2].astype(jnp.bfloat16)[None],
    )


swap_x = [(0, 2), (1, 3), (2, 0), (3, 1)]
swap_core = [(0, 1), (1, 0), (2, 3), (3, 2)]
swap_part = [(0, 1), (1, 0)]


def slot_kernel(slots, lane_ref, part_ref, *rest):
    ins, grads, rest = rest[:slots], rest[slots : 2 * slots], rest[2 * slots :]
    own, near, far, far_near = rest[:3], rest[3], rest[4:8], rest[8:12]
    near_ref, far_ref, hidden_send, hidden_keep, scaled_ref = rest[12:17]
    backs, rest = rest[17 : 17 + slots], rest[17 + slots :]
    held, held_down, rows_in, rows_grad, acts, sems = rest
    features = held.shape[0]
    width = held.shape[1] // 8
    half, quarter = features // 2, features // 4
    copies = [[] for _ in range(4)]
    first = pl.multiple_of(part_ref[0] * half, half)
    second = pl.multiple_of(half - part_ref[0] * half, half)
    count = 0
    for share, (group, lines) in enumerate(
        ((own, None), (near, None), (far, (first, second)), (far_near, (first, second)))
    ):
        for kind in range(3):
            target = held_down if kind == 2 else held
            column = share * width if kind == 2 else (2 * share + kind) * width
            columns = pl.ds(column, width)
            if share == 0:
                pairs = [(own[kind], target.at[:, columns])]
            elif share == 1:
                pairs = [(near.at[kind], target.at[:, columns])]
            else:
                pairs = [
                    (group[2 * side + kind // 2].at[kind % 2], target.at[pl.ds(line, half), columns])
                    for side, line in enumerate(lines)
                ]
            for source, place in pairs:
                copies[share].append(pltpu.make_async_copy(source, place, sems.at[count]))
                count += 1
    for group in copies:
        for copy in group:
            copy.start()
    height = ins[0].shape[0]
    gates = []
    for slot, (in_ref, grad_ref) in enumerate(zip(ins, grads)):
        lines = slice(slot * height, (slot + 1) * height)
        rows_in[lines, :] = in_ref[...]
        rows_grad[lines, :] = grad_ref[:, :features]
        lanes = grad_ref[:, features:].astype(jnp.float32)
        gates.append(jnp.sum(lanes * lane_ref[...], axis=1, keepdims=True))
    gate = jnp.concatenate(gates)
    scaled_ref[...] = (gate * rows_grad[...].astype(jnp.float32)).astype(jnp.bfloat16)
    gate_sum = jnp.zeros(gate.shape, jnp.float32)
    for share in range(4):
        for copy in copies[share]:
            copy.wait()
        both = slice(2 * share * width, 2 * (share + 1) * width)
        pre = jnp.dot(rows_in[...], held[:, both], preferred_element_type=jnp.float32)
        pre_gate, pre_up = pre[:, :width], pre[:, width:]
        back_proj = jnp.dot(
            rows_grad[...],
            held_down[:, share * width : (share + 1) * width],
            preferred_element_type=jnp.float32,
        )
        sigmoid_g = jax.nn.sigmoid(pre_gate)
        activated = pre_gate * sigmoid_g
        hidden_act = activated * pre_up
        gate_sum = gate_sum + jnp.sum(back_proj * hidden_act, axis=1, keepdims=True)
        grad_hidden = gate * back_proj
        grad_gate = (
            grad_hidden * pre_up * sigmoid_g * (1.0 + pre_gate * (1.0 - sigmoid_g))
        ).astype(jnp.bfloat16)
        grad_up = (grad_hidden * activated).astype(jnp.bfloat16)
        acts[:, 2 * share * width : (2 * share + 1) * width] = grad_gate
        acts[:, (2 * share + 1) * width : 2 * (share + 1) * width] = grad_up
        hidden = hidden_send if share % 2 else hidden_keep
        pick = share // 2
        hidden[:, pick * width : (pick + 1) * width] = hidden_act.astype(jnp.bfloat16)
    near_ref[...] = acts[:, : 4 * width]
    far_ref[...] = acts[:, 4 * width :]
    for piece in range(4):
        lines = slice(piece * quarter, (piece + 1) * quarter)
        part = lax.dot_general(
            acts[...],
            held[lines, :],
            (((1,), (1,)), ((), ())),
            preferred_element_type=jnp.float32,
        ).astype(jnp.bfloat16)
        for slot, back in enumerate(backs):
            back[:, lines] = part[slot * height : (slot + 1) * height]
    for slot, back in enumerate(backs):
        back[:, features:] = jnp.broadcast_to(
            gate_sum[slot * height : (slot + 1) * height], (height, 128)
        ).astype(jnp.bfloat16)


def slot_compute(ins, grads, lane, part, weights):
    slots = len(ins)
    height = ins[0].shape[0]
    rows = slots * height
    features, width = weights[0].shape
    bf = jnp.bfloat16
    shapes = [(rows, c) for c in (4 * width, 4 * width, 2 * width, 2 * width, features)]
    shapes += [(height, features + 128)] * slots
    vmem = pl.BlockSpec(memory_space=pltpu.VMEM)
    out = pl.pallas_call(
        functools.partial(slot_kernel, slots),
        out_shape=[jax.ShapeDtypeStruct(shape, bf) for shape in shapes],
        in_specs=[vmem, pl.BlockSpec(memory_space=pltpu.SMEM)]
        + [vmem] * (2 * slots)
        + [pl.BlockSpec(memory_space=pl.ANY)] * 12,
        out_specs=[vmem] * len(shapes),
        scratch_shapes=[
            pltpu.VMEM((features, 8 * width), bf),
            pltpu.VMEM((features, 4 * width), bf),
            pltpu.VMEM((rows, features), bf),
            pltpu.VMEM((rows, features), bf),
            pltpu.VMEM((rows, 8 * width), bf),
            pltpu.SemaphoreType.DMA((18,)),
        ],
        compiler_params=pltpu.CompilerParams(vmem_limit_bytes=48 * 1024 * 1024),
        cost_estimate=pl.CostEstimate(
            flops=rows * features, bytes_accessed=2 * rows * features, transcendentals=0
        ),
    )(lane, part, *ins, *grads, *weights)
    return (*out[:5], out[5:])


def tied(*values):
    return lax.optimization_barrier(values)


def over_z(value, pairs):
    return lax.ppermute(value, "expert", pairs)


def over_x(value):
    return lax.ppermute(value, "replica", swap_x)


def over_core(value):
    return lax.ppermute(value, "replica", swap_core)


def over_parts(value):
    return lax.ppermute(value, "parts", swap_part)


def apart(step):
    return [(i, i ^ step) for i in range(4)]


def outer(lhs, rhs):
    return lax.dot_general(lhs, rhs, (((0,), (0,)), ((), ())), preferred_element_type=jnp.float32)


def fast_body(tokens, out_grad, expert_ids, gates, gate_weight, up_weight, down_weight):
    z = lax.axis_index("expert")
    y = lax.axis_index("parts")
    rows, features = tokens.shape
    bf, f32 = jnp.bfloat16, jnp.float32
    half = features // 2
    own = [gate_weight[0], up_weight[0], down_weight[0]]
    width = own[0].shape[1]
    halves = [lax.dynamic_slice_in_dim(w, y * half, half, 0) for w in own]
    pieces = [jnp.stack(halves[:2]), halves[2][None]]
    lanes = jnp.arange(128, dtype=jnp.int32)[None, :]
    gate_lanes = sum(
        jnp.where(expert_ids[:, k : k + 1] == lanes, gates[:, k : k + 1], 0) for k in range(2)
    ).astype(bf)
    lane = (lanes == z).astype(f32)
    wide_grad = jnp.concatenate([out_grad, gate_lanes], axis=1)
    part_index = jnp.reshape(y, (1,)).astype(jnp.int32)

    in_two, in_one = over_z(tokens, apart(2)), over_z(tokens, apart(1))
    across_0 = over_x(pieces[0])
    in_two, in_one, across_0, wide_grad, tokens_x, piece_1, stacked = tied(
        in_two, in_one, across_0, wide_grad, tokens, pieces[1], jnp.stack(own)
    )

    grad_two, grad_one = over_z(wide_grad, apart(2)), over_z(wide_grad, apart(1))
    across_1 = over_x(piece_1)
    other_0 = over_parts(across_0)
    near = over_core(stacked)
    across_1, near, tokens_x = tied(across_1, near, tokens_x)
    other_1 = over_parts(across_1)
    far_a = over_x(tokens_x)
    in_bc = jnp.concatenate([in_one, in_two])
    two = jnp.concatenate([in_two, grad_two], axis=1)
    two, grad_one, in_bc, far_a, across_0, across_1, other_0, other_1 = tied(
        two, grad_one, in_bc, far_a, across_0, across_1, other_0, other_1
    )

    three = over_z(two, apart(1))
    far_bc = over_x(in_bc)
    far_weights = [across_0, across_1, other_0, other_1]
    weights = [*own, near, *far_weights, *[over_core(w) for w in far_weights]]
    acts_abc, crossing_abc, send_abc, keep_abc, scaled_abc, backs = slot_compute(
        [tokens, in_one, in_two], [wide_grad, grad_one, grad_two], lane, part_index, weights
    )
    three, far_bc, crossing_abc, back_a, back_b, back_c = tied(three, far_bc, crossing_abc, *backs)

    in_d, grad_d = three[:, :features], three[:, features:]
    far_d = over_x(in_d)
    back_one = over_z(back_b, apart(1))
    acts_d, crossing_d, send_d, keep_d, scaled_d, (back_d,) = slot_compute(
        [in_d], [grad_d], lane, part_index, weights
    )
    far_d, back_one, acts_d, crossing_d, send_d, keep_d, scaled_d, back_d, back_c = tied(
        far_d, back_one, acts_d, crossing_d, send_d, keep_d, scaled_d, back_d, back_c
    )

    acts_far = over_x(jnp.concatenate([crossing_abc, crossing_d]))
    back_two = over_z(back_c, apart(2))
    scaled = jnp.concatenate([scaled_abc, scaled_d])
    send = outer(scaled, jnp.concatenate([send_abc, send_d])).astype(bf)
    keep = outer(scaled, jnp.concatenate([keep_abc, keep_d])).astype(bf)
    both = keep.astype(f32) + over_core(send).astype(f32)
    acts = jnp.concatenate([acts_abc, acts_d])
    rows_near = jnp.concatenate([tokens, in_bc, in_d])
    part_keep = outer(rows_near, acts[:, : 2 * width]).astype(bf)
    part_send = outer(rows_near, acts[:, 2 * width :]).astype(bf)
    rows_far = jnp.concatenate([far_a, far_bc, far_d])
    crossing, both = both[:, width:].astype(bf), both[:, :width]
    acts_far, back_two, crossing, both, part_keep, part_send, rows_far, back_d = tied(
        acts_far, back_two, crossing, both, part_keep, part_send, rows_far, back_d
    )

    down_far = over_x(crossing)
    back_three = over_z(back_d, apart(3))
    part_send = part_send.astype(f32) + outer(rows_far, acts_far[:, 2 * width :])
    part_keep = part_keep.astype(f32) + outer(rows_far, acts_far[:, : 2 * width])
    pair = (part_keep + over_core(part_send.astype(bf)).astype(f32)).astype(bf)
    gate_out, up_out = pair[:, :width], pair[:, width:]
    back_three, down_far, gate_out, up_out = tied(back_three, down_far, gate_out, up_out)
    returned = [back_a, back_one, back_two, back_three]
    down = (both + down_far.astype(f32)).astype(bf)
    token_grad = sum(r[:, :features].astype(f32) for r in returned).astype(bf)
    gate_grad = sum(
        jnp.where(expert_ids == (z ^ step), r[:, features : features + 1].astype(f32), 0.0)
        for step, r in enumerate(returned)
    ).astype(bf)
    return token_grad, gate_grad, gate_out[None], up_out[None], down[None]


def body(*args):
    sizes = tuple(lax.axis_size(name) for name in ("parts", "expert", "replica"))
    if sizes == (2, 4, 4):
        return fast_body(*args)
    return general_body(*args)


def solution(mesh):
    in_specs = (
        P(("parts", "expert", "replica"), None),
        P(("parts", "expert", "replica"), None),
        P(("parts", "expert", "replica"), None),
        P(("parts", "expert", "replica"), None),
        P("expert", None, "replica"),
        P("expert", None, "replica"),
        P("expert", None, "replica"),
    )
    out_specs = (
        P(("parts", "expert", "replica"), None),
        P(("parts", "expert", "replica"), None),
        P(("parts", "expert"), None, "replica"),
        P(("parts", "expert"), None, "replica"),
        P(("parts", "expert"), None, "replica"),
    )
    return jax.shard_map(body, mesh=mesh, in_specs=in_specs, out_specs=out_specs, check_vma=False)
```

profile of v0, /device:TPU:12, one launch (start us, length us, event | category | flops | bytes accessed | tf_op | source)
XLA Modules:
  0.0 174.5 jit_solution(5691953830692100744)
XLA Ops:
  0.6 2.7 %collective-permute-start = (bf16[128,2048]{1,0:T(8,128)(2,1)}, bf16[128,2048]{1,0:T(8,128)(2,1)S(1)}, u32[]{:S(2)}, u32[]{:S(2)}) collective-permute-start(bf16[128,2048]{1,0:T(8,128)(2,1)} %rest_0_.1), channel_id=1, source_target_pairs={{0,8},{4,12},{8,0},{12,4},{1,9},{5,13},{9,1},{13,5},{2,10},{6,14},... | collective-permute-start | bytes 1572872 | tf_op jit(solution)/shard_map/ppermute | solution.py:316
  3.3 0.4 collective-permute-start.1
  3.8 1.4 constant_dynamic-slice_fusion.1
  5.3 1.6 collective-permute-start.2
  6.9 0.3 pad_maximum_fusion
  7.3 0.1 fusion.17
  7.5 0.5 copy-done.24
  8.0 17.9 %collective-permute-done.rest_2_ = bf16[128,2048]{1,0:T(8,128)(2,1)S(1)} collective-permute-done((bf16[128,2048]{1,0:T(8,128)(2,1)}, bf16[128,2048]{1,0:T(8,128)(2,1)S(1)}, u32[]{:S(2)}, u32[]{:S(2)}) %collective-permute-start) | collective-permute-done | bytes 524320 | tf_op jit(solution)/shard_map/ppermute | solution.py:316
  25.9 1.0 collective-permute-done.1.rest_1_
  26.9 2.9 %collective-permute-done.2.rest_10_.rest_6_ = bf16[2,1024,256]{2,1,0:T(8,128)(2,1)} collective-permute-done((bf16[2,1024,256]{2,1,0:T(8,128)(2,1)S(1)}, bf16[2,1024,256]{2,1,0:T(8,128)(2,1)}, u32[]{:S(2)}, u32[]{:S(2)}) %collective-permute-start.2) | collective-permute-done | bytes 1048608 | tf_op jit(solution)/shard_map/ppermute | solution.py:320
  29.8 0.4 collective-permute-start.3
  30.2 1.5 collective-permute-start.5
  31.7 0.5 collective-permute-start.8
  32.2 1.6 collective-permute-start.4
  33.7 1.0 pad_maximum_fusion.5
  34.8 9.4 %collective-permute-done.5.rest_11_.rest_7_ = bf16[1,1024,256]{2,1,0:T(8,128)(2,1)S(1)} collective-permute-done((bf16[1,1024,256]{2,1,0:T(8,128)(2,1)S(1)}, bf16[1,1024,256]{2,1,0:T(8,128)(2,1)S(1)}, u32[]{:S(2)}, u32[]{:S(2)}) %collective-permute-start.5) | collective-permute-done | bytes 524320 | tf_op jit(solution)/shard_map/ppermute | solution.py:320
  44.2 0.5 collective-permute-start.9
  44.7 1.5 collective-permute-start.7
  46.2 8.5 %collective-permute-done.3.rest_5_ = bf16[128,2176]{1,0:T(8,128)(2,1)S(1)} collective-permute-done((bf16[128,2176]{1,0:T(8,128)(2,1)S(1)}, bf16[128,2176]{1,0:T(8,128)(2,1)S(1)}, u32[]{:S(2)}, u32[]{:S(2)}) %collective-permute-start.3) | collective-permute-done | bytes 557088 | tf_op jit(solution)/shard_map/ppermute | solution.py:316
  54.7 1.2 pad_maximum_fusion.3
  55.9 1.5 collective-permute-done.4.rest_4_
  57.4 0.6 collective-permute-done.8.rest_12_.rest_8_
  58.0 10.1 %collective-permute-done.9.rest_13_.rest_9_ = bf16[1,1024,256]{2,1,0:T(8,128)(2,1)S(1)} collective-permute-done((bf16[1,1024,256]{2,1,0:T(8,128)(2,1)S(1)}, bf16[1,1024,256]{2,1,0:T(8,128)(2,1)S(1)}, u32[]{:S(2)}, u32[]{:S(2)}) %collective-permute-start.9) | collective-permute-done | bytes 524320 | tf_op jit(solution)/shard_map/ppermute | solution.py:328
  68.1 1.6 collective-permute-start.10
  69.7 0.5 collective-permute-start.12
  70.2 0.5 collective-permute-start.11
  70.8 1.6 collective-permute-done.13.rest_15_.rest_11_
  72.3 0.1 collective-permute-start.15
  72.5 2.9 %collective-permute-done.15.rest_17_.rest_13_ = bf16[1,1024,256]{2,1,0:T(8,128)(2,1)S(1)} collective-permute-done((bf16[1,1024,256]{2,1,0:T(8,128)(2,1)S(1)}, bf16[1,1024,256]{2,1,0:T(8,128)(2,1)S(1)}, u32[]{:S(2)}, u32[]{:S(2)}) %collective-permute-start.15) | collective-permute-done | bytes 524320 | tf_op jit(solution)/shard_map/ppermute | solution.py:324
  75.4 1.0 copy-done.5
  76.4 14.4 %shard_map.110 = (bf16[384,1024]{1,0:T(8,128)(2,1)}, bf16[384,1024]{1,0:T(8,128)(2,1)}, bf16[384,512]{1,0:T(8,128)(2,1)S(1)}, bf16[384,512]{1,0:T(8,128)(2,1)S(1...) custom-call(f32[1,128]{1,0:T(1,128)S(1)} %compare_convert_fusion.lan, ...), custom_call_target="tpu_custom_call" | custom-call | flops 786432 | bytes 1572864 | tf_op jit(solution)/shard_map/pallas_call | solution.py:288
  90.9 5.2 %collective-permute-done.11 = bf16[256,2048]{1,0:T(8,128)(2,1)} collective-permute-done((bf16[256,2048]{1,0:T(8,128)(2,1)}, bf16[256,2048]{1,0:T(8,128)(2,1)}, u32[]{:S(2)}, u32[]{:S(2)}) %collective-permute-start.11) | collective-permute-done | bytes 1048608 | tf_op jit(solution)/shard_map/ppermute | solution.py:320
  96.1 0.5 collective-permute-start.17
  96.6 1.1 slice.72.rest_0_
  97.7 0.6 collective-permute-start.16
  98.3 1.1 slice.73.rest_1_
  99.4 0.2 constant_dynamic-update-slice_fusion.1
  99.5 7.9 %shard_map.111 = (bf16[128,1024]{1,0:T(8,128)(2,1)S(1)}, bf16[128,1024]{1,0:T(8,128)(2,1)S(1)}, bf16[128,512]{1,0:T(8,128)(2,1)S(1)}, bf16[128,512]{1,0:T(8,128)...) custom-call(f32[1,128]{1,0:T(1,128)S(1)} %compare_convert_fusion.lane_ref, s32[1]{0:T(128)} %bitcast.4.part_ref, ...), custom_call_target="tpu_custom_call" | custom-call | flops 262144 | bytes 524288 | tf_op jit(solution)/shard_map/pallas_call | solution.py:288
  107.4 3.6 %collective-permute-done.16 = bf16[128,2048]{1,0:T(8,128)(2,1)S(1)} collective-permute-done((bf16[128,2048]{1,0:T(8,128)(2,1)S(1)}, bf16[128,2048]{1,0:T(8,128)(2,1)S(1)}, u32[]{:S(2)}, u32[]{:S(2)}) %collective-permute-start.16) | collective-permute-done | bytes 524320 | tf_op jit(solution)/shard_map/ppermute | solution.py:320
  111.1 1.3 convolution_convert_fusion.2
  112.4 0.3 copy-done.11
  112.8 1.0 copy-done.18
  113.9 0.6 collective-permute-start.18
  114.5 2.6 %collective-permute-start.19 = (bf16[128,2176]{1,0:T(8,128)(2,1)S(1)}, bf16[128,2176]{1,0:T(8,128)(2,1)S(1)}, u32[]{:S(2)}, u32[]{:S(2)}) collective-permute-start(bf16[128,2176]{1,0:T(8,128)(2,1)S(1)} %get-tuple-element.98), channel_id=1, source_target_pairs={{0,8},{4,12},{8,0},{12,4},{1,9},{5,13},{9,1},{13,5},{2,10},{6,14},... | collective-permute-start | bytes 1671176 | tf_op jit(solution)/shard_map/ppermute | solution.py:316
  117.1 2.5 %convolution_convert_fusion = bf16[2048,512]{1,0:T(8,128)(2,1)S(1)} fusion(bf16[128,2048]{1,0:T(8,128)(2,1)S(1)} %slice.72.rest_0_, bf16[256,2048]{1,0:T(8,128)(2,1)} %pad_maximum_fusion.5, bf16[128,2048]{1,0:T(8,128)(2,1)S(1)} %copy-done.5, bf16[512,1024]{1,0:T(8,128)(2,1)S(1)} %constant_dynamic-update-slice_fusion.2), kind=kOutput, calls=%fused_computation.4 | convolution fusion | flops 1081081856 | bytes 4718592 | tf_op jit(solution)/shard_map/dot_general | solution.py:336
  119.7 4.0 %convolution_convert_fusion.1 = bf16[2048,512]{1,0:T(8,128)(2,1)} fusion(bf16[128,2048]{1,0:T(8,128)(2,1)S(1)} %slice.72.rest_0_, bf16[256,2048]{1,0:T(8,128)(2,1)} %pad_maximum_fusion.5, bf16[128,2048]{1,0:T(8,128)(2,1)S(1)} %copy-done.5, bf16[512,1024]{1,0:T(8,128)(2,1)S(1)} %constant_dynamic-update-slice_fusion.2), kind=kOutput, calls=%fused_computation.5 | convolution fusion | flops 1081081856 | bytes 4718592 | tf_op jit(solution)/shard_map/dot_general | solution.py:336
  123.6 1.5 pad_maximum_fusion.2
  125.2 0.3 copy-done.12
  125.5 1.3 convert_add_fusion
  126.9 2.0 %copy-done.6 = f32[2048,512]{1,0:T(8,128)} copy-done((f32[2048,512]{1,0:T(8,128)}, f32[2048,512]{1,0:T(8,128)S(1)}, u32[]{:S(2)}) %copy-start.6) | copy-done | bytes 4194328
  128.8 0.1 slice.118
  129.0 11.2 %collective-permute-done.19 = bf16[128,2176]{1,0:T(8,128)(2,1)S(1)} collective-permute-done((bf16[128,2176]{1,0:T(8,128)(2,1)S(1)}, bf16[128,2176]{1,0:T(8,128)(2,1)S(1)}, u32[]{:S(2)}, u32[]{:S(2)}) %collective-permute-start.19) | collective-permute-done | bytes 557088 | tf_op jit(solution)/shard_map/ppermute | solution.py:316
  140.2 2.8 %add_convert_fusion.1 = bf16[2048,512]{1,0:T(8,128)(2,1)} fusion(bf16[2048,512]{1,0:T(8,128)(2,1)S(1)} %convolution_convert_fusion, bf16[512,2048]{1,0:T(8,128)(2,1)S(1)} %pad_maximum_fusion.2, bf16[512,1024]{1,0:T(8,128)(2,1)S(1)} %collective-permute-done.18), kind=kOutput, calls=%fused_computation.1 | convolution fusion | flops 1076887552 | bytes 6815744 | tf_op jit(solution)/shard_map/dot_general | solution.py:336
  143.1 0.1 convert_reduce_fusion.2
  143.2 1.6 collective-permute-start.22
  144.8 0.4 collective-permute-start.21
  145.2 0.9 convert_reduce_fusion.1
  146.0 3.1 %fusion.13 = f32[2048,512]{1,0:T(8,128)S(1)} fusion(bf16[512,2048]{1,0:T(8,128)(2,1)} %copy-done.10, bf16[512,1024]{1,0:T(8,128)(2,1)} %copy-done.29), kind=kOutput, calls=%fused_computation.29 | convolution fusion | flops 1073741824 | bytes 6815744 | tf_op jit(solution)/shard_map/dot_general | solution.py:336
  149.2 2.5 %add_convert_fusion = bf16[2048,512]{1,0:T(8,128)(2,1)S(1)} fusion(bf16[2048,512]{1,0:T(8,128)(2,1)} %collective-permute-done.23, f32[2048,512]{1,0:T(8,128)S(1)} %fusion.13, bf16[2048,512]{1,0:T(8,128)(2,1)S(1)} %copy-done.15), kind=kLoop, calls=%fused_computation | loop fusion | flops 5242880 | bytes 10485760 | tf_op jit(solution)/shard_map/convert_element_type | solution.py:415
  151.7 1.5 fusion.26
  153.1 18.3 %collective-permute-done.21 = bf16[128,2176]{1,0:T(8,128)(2,1)S(1)} collective-permute-done((bf16[128,2176]{1,0:T(8,128)(2,1)S(1)}, bf16[128,2176]{1,0:T(8,128)(2,1)S(1)}, u32[]{:S(2)}, u32[]{:S(2)}) %collective-permute-start.21) | collective-permute-done | bytes 557088 | tf_op jit(solution)/shard_map/ppermute | solution.py:316
  171.6 1.1 add_convert_fusion.3
  172.7 1.3 fusion
  173.9 0.5 fusion.21
  (87 shorter events, 0.8 us)
Async XLA Ops:
  0.6 25.3 %collective-permute-start = (bf16[128,2048]{1,0:T(8,128)(2,1)}, bf16[128,2048]{1,0:T(8,128)(2,1)S(1)}, u32[]{:S(2)}, u32[]{:S(2)}) collective-permute-start(bf16[128,2048]{1,0:T(8,128)(2,1)} %rest_0_.1), channel_id=1, source_target_pairs={{0,8},{4,12},{8,0},{12,4},{1,9},{5,13},{9,1},{13,5},{2,10},{6,14},... | collective-permute-start | bytes 1572872 | tf_op jit(solution)/shard_map/ppermute | solution.py:316
  3.3 23.6 %collective-permute-start.1 = (bf16[128,2048]{1,0:T(8,128)(2,1)}, bf16[128,2048]{1,0:T(8,128)(2,1)S(1)}, u32[]{:S(2)}, u32[]{:S(2)}) collective-permute-start(bf16[128,2048]{1,0:T(8,128)(2,1)} %rest_0_.1), channel_id=1, source_target_pairs={{0,4},{4,0},{8,12},{12,8},{1,5},{5,1},{9,13},{13,9},{2,6},{6,2},{1... | collective-permute-start | bytes 1572872 | tf_op jit(solution)/shard_map/ppermute | solution.py:316
  3.7 3.1 %copy-start.30 = (s32[128,2]{0,1:T(2,128)S(1)}, s32[128,2]{0,1:T(2,128)}, u32[]{:S(2)}) copy-start(s32[128,2]{0,1:T(2,128)} %param.9) | copy-start | bytes 3076
  3.7 3.1 %copy-start.31 = (bf16[128,2]{0,1:T(2,128)(2,1)S(1)}, bf16[128,2]{0,1:T(2,128)(2,1)}, u32[]{:S(2)}) copy-start(bf16[128,2]{0,1:T(2,128)(2,1)} %param.10) | copy-start | bytes 1540
  3.7 3.1 %copy-start = (bf16[1,2048,256]{2,1,0:T(8,128)(2,1)S(1)}, bf16[1,2048,256]{2,1,0:T(8,128)(2,1)}, u32[]{:S(2)}) copy-start(bf16[1,2048,256]{2,1,0:T(8,128)(2,1)} %param.11) | copy-start | bytes 3145732
  3.7 3.1 %copy-start.7 = (bf16[1,2048,256]{2,1,0:T(8,128)(2,1)S(1)}, bf16[1,2048,256]{2,1,0:T(8,128)(2,1)}, u32[]{:S(2)}) copy-start(bf16[1,2048,256]{2,1,0:T(8,128)(2,1)} %param.12) | copy-start | bytes 3145732
  3.7 3.2 %copy-start.8 = (bf16[1,2048,256]{2,1,0:T(8,128)(2,1)S(1)}, bf16[1,2048,256]{2,1,0:T(8,128)(2,1)}, u32[]{:S(2)}) copy-start(bf16[1,2048,256]{2,1,0:T(8,128)(2,1)} %param.13) | copy-start | bytes 3145732
  5.3 24.5 %collective-permute-start.2 = (bf16[2,1024,256]{2,1,0:T(8,128)(2,1)S(1)}, bf16[2,1024,256]{2,1,0:T(8,128)(2,1)}, u32[]{:S(2)}, u32[]{:S(2)}) collective-permute-start(bf16[2,1024,256]{2,1,0:T(8,128)(2,1)S(1)} %pad_maximum_fusion.4), channel_id=1, source_target_pairs={{0,2},{1,3},{2,0},{3,1},{4,6},{5,7},{6,4},{7,5},{8,10},{9,11},{10,... | collective-permute-start | bytes 3145736 | tf_op jit(solution)/shard_map/ppermute | solution.py:320
  6.9 1.0 copy-start.24
  7.4 37.3 %copy-start.4 = (bf16[128,2048]{1,0:T(8,128)(2,1)S(1)}, bf16[128,2048]{1,0:T(8,128)(2,1)}, u32[]{:S(2)}) copy-start(bf16[128,2048]{1,0:T(8,128)(2,1)} %rest_0_.1) | copy-start | bytes 1572868
  8.0 47.9 %copy-start.13 = (bf16[128,2176]{1,0:T(8,128)(2,1)}, bf16[128,2176]{1,0:T(8,128)(2,1)S(1)}, u32[]{:S(2)}) copy-start(bf16[128,2176]{1,0:T(8,128)(2,1)S(1)} %pad_maximum_fusion.9.rest_3_) | copy-start | bytes 1671172
  29.8 14.4 %collective-permute-start.6 = (bf16[3,2048,256]{2,1,0:T(8,128)(2,1)S(1)}, bf16[3,2048,256]{2,1,0:T(8,128)(2,1)S(1)}, u32[]{:S(2)}, u32[]{:S(2)}) collective-permute-start(bf16[3,2048,256]{2,1,0:T(8,128)(2,1)S(1)} %pad_maximum_fusion), channel_id=1, source_target_pairs={{0,1},{1,0},{2,3},{3,2},{4,5},{5,4},{6,7},{7,6},{8,9},{9,8},{10,11... | collective-permute-start | bytes 9437192 | tf_op jit(solution)/shard_map/ppermute | solution.py:324
  29.8 24.9 %collective-permute-start.3 = (bf16[128,2176]{1,0:T(8,128)(2,1)S(1)}, bf16[128,2176]{1,0:T(8,128)(2,1)S(1)}, u32[]{:S(2)}, u32[]{:S(2)}) collective-permute-start(bf16[128,2176]{1,0:T(8,128)(2,1)S(1)} %pad_maximum_fusion.9.rest_3_), channel_id=1, source_target_pairs={{0,8},{4,12},{8,0},{12,4},{1,9},{5,13},{9,1},{13,5},{2,10},{6,14},... | collective-permute-start | bytes 1671176 | tf_op jit(solution)/shard_map/ppermute | solution.py:316
  30.2 14.1 %collective-permute-start.5 = (bf16[1,1024,256]{2,1,0:T(8,128)(2,1)S(1)}, bf16[1,1024,256]{2,1,0:T(8,128)(2,1)S(1)}, u32[]{:S(2)}, u32[]{:S(2)}) collective-permute-start(bf16[1,1024,256]{2,1,0:T(8,128)(2,1)S(1)} %constant_dynamic-slice_fusion), channel_id=1, source_target_pairs={{0,2},{1,3},{2,0},{3,1},{4,6},{5,7},{6,4},{7,5},{8,10},{9,11},{10,... | collective-permute-start | bytes 1572872 | tf_op jit(solution)/shard_map/ppermute | solution.py:320
  31.7 26.3 %collective-permute-start.8 = (bf16[2,1024,256]{2,1,0:T(8,128)(2,1)}, bf16[2,1024,256]{2,1,0:T(8,128)(2,1)}, u32[]{:S(2)}, u32[]{:S(2)}) collective-permute-start(bf16[2,1024,256]{2,1,0:T(8,128)(2,1)} %collective-permute-done.2.rest_10_.rest_6_), channel_id=1, source_target_pairs={{0,16},{16,0},{1,17},{17,1},{2,18},{18,2},{3,19},{19,3},{4,20},{20... | collective-permute-start | bytes 3145736 | tf_op jit(solution)/shard_map/ppermute | solution.py:328
  32.2 25.2 %collective-permute-start.4 = (bf16[128,2176]{1,0:T(8,128)(2,1)S(1)}, bf16[128,2176]{1,0:T(8,128)(2,1)S(1)}, u32[]{:S(2)}, u32[]{:S(2)}) collective-permute-start(bf16[128,2176]{1,0:T(8,128)(2,1)S(1)} %pad_maximum_fusion.9.rest_3_), channel_id=1, source_target_pairs={{0,4},{4,0},{8,12},{12,8},{1,5},{5,1},{9,13},{13,9},{2,6},{6,2},{1... | collective-permute-start | bytes 1671176 | tf_op jit(solution)/shard_map/ppermute | solution.py:316
  44.2 28.1 %copy-start.9 = (bf16[3,2048,256]{2,1,0:T(8,128)(2,1)}, bf16[3,2048,256]{2,1,0:T(8,128)(2,1)S(1)}, u32[]{:S(2)}) copy-start(bf16[3,2048,256]{2,1,0:T(8,128)(2,1)S(1)} %collective-permute-done.6.rest_9_.rest_5_) | copy-start | bytes 9437188
  44.2 23.9 %collective-permute-start.9 = (bf16[1,1024,256]{2,1,0:T(8,128)(2,1)S(1)}, bf16[1,1024,256]{2,1,0:T(8,128)(2,1)S(1)}, u32[]{:S(2)}, u32[]{:S(2)}) collective-permute-start(bf16[1,1024,256]{2,1,0:T(8,128)(2,1)S(1)} %collective-permute-done.5.rest_11_.rest_7_), channel_id=1, source_target_pairs={{0,16},{16,0},{1,17},{17,1},{2,18},{18,2},{3,19},{19,3},{4,20},{20... | collective-permute-start | bytes 1572872 | tf_op jit(solution)/shard_map/ppermute | solution.py:328
  44.7 23.4 %collective-permute-start.7 = (bf16[128,2048]{1,0:T(8,128)(2,1)S(1)}, bf16[128,2048]{1,0:T(8,128)(2,1)S(1)}, u32[]{:S(2)}, u32[]{:S(2)}) collective-permute-start(bf16[128,2048]{1,0:T(8,128)(2,1)S(1)} %copy-done.4), channel_id=1, source_target_pairs={{0,2},{1,3},{2,0},{3,1},{4,6},{5,7},{6,4},{7,5},{8,10},{9,11},{10,... | collective-permute-start | bytes 1572872 | tf_op jit(solution)/shard_map/ppermute | solution.py:320
  54.7 17.6 %copy-start.14 = (bf16[128,2176]{1,0:T(8,128)(2,1)}, bf16[128,2176]{1,0:T(8,128)(2,1)S(1)}, u32[]{:S(2)}) copy-start(bf16[128,2176]{1,0:T(8,128)(2,1)S(1)} %collective-permute-done.3.rest_5_) | copy-start | bytes 1671172
  57.4 15.0 %copy-start.19 = (bf16[128,2176]{1,0:T(8,128)(2,1)}, bf16[128,2176]{1,0:T(8,128)(2,1)S(1)}, u32[]{:S(2)}) copy-start(bf16[128,2176]{1,0:T(8,128)(2,1)S(1)} %collective-permute-done.4.rest_4_) | copy-start | bytes 1671172
  68.1 2.6 %copy-start.25 = (bf16[128,2048]{1,0:T(8,128)(2,1)}, bf16[128,2048]{1,0:T(8,128)(2,1)S(1)}, u32[]{:S(2)}) copy-start(bf16[128,2048]{1,0:T(8,128)(2,1)S(1)} %collective-permute-done.7) | copy-start | bytes 1572868
  68.1 28.0 %collective-permute-start.10 = (bf16[128,4224]{1,0:T(8,128)(2,1)}, bf16[128,4224]{1,0:T(8,128)(2,1)}, u32[]{:S(2)}, u32[]{:S(2)}) collective-permute-start(bf16[128,4224]{1,0:T(8,128)(2,1)} %pad_maximum_fusion.3), channel_id=1, source_target_pairs={{0,4},{4,0},{8,12},{12,8},{1,5},{5,1},{9,13},{13,9},{2,6},{6,2},{1... | collective-permute-start | bytes 3244040 | tf_op jit(solution)/shard_map/ppermute | solution.py:316
  69.7 2.6 %collective-permute-start.13 = (bf16[1,1024,256]{2,1,0:T(8,128)(2,1)S(1)}, bf16[1,1024,256]{2,1,0:T(8,128)(2,1)S(1)}, u32[]{:S(2)}, u32[]{:S(2)}) collective-permute-start(bf16[1,1024,256]{2,1,0:T(8,128)(2,1)S(1)} %collective-permute-done.5.rest_11_.rest_7_), channel_id=1, source_target_pairs={{0,1},{1,0},{2,3},{3,2},{4,5},{5,4},{6,7},{7,6},{8,9},{9,8},{10,11... | collective-permute-start | bytes 1572872 | tf_op jit(solution)/shard_map/ppermute | solution.py:324
  69.7 5.7 %collective-permute-start.12 = (bf16[2,1024,256]{2,1,0:T(8,128)(2,1)}, bf16[2,1024,256]{2,1,0:T(8,128)(2,1)}, u32[]{:S(2)}, u32[]{:S(2)}) collective-permute-start(bf16[2,1024,256]{2,1,0:T(8,128)(2,1)} %collective-permute-done.2.rest_10_.rest_6_), channel_id=1, source_target_pairs={{0,1},{1,0},{2,3},{3,2},{4,5},{5,4},{6,7},{7,6},{8,9},{9,8},{10,11... | collective-permute-start | bytes 3145736 | tf_op jit(solution)/shard_map/ppermute | solution.py:324
  70.2 5.2 %collective-permute-start.14 = (bf16[2,1024,256]{2,1,0:T(8,128)(2,1)}, bf16[2,1024,256]{2,1,0:T(8,128)(2,1)}, u32[]{:S(2)}, u32[]{:S(2)}) collective-permute-start(bf16[2,1024,256]{2,1,0:T(8,128)(2,1)} %collective-permute-done.8.rest_12_.rest_8_), channel_id=1, source_target_pairs={{0,1},{1,0},{2,3},{3,2},{4,5},{5,4},{6,7},{7,6},{8,9},{9,8},{10,11... | collective-permute-start | bytes 3145736 | tf_op jit(solution)/shard_map/ppermute | solution.py:324
  70.2 25.9 %collective-permute-start.11 = (bf16[256,2048]{1,0:T(8,128)(2,1)}, bf16[256,2048]{1,0:T(8,128)(2,1)}, u32[]{:S(2)}, u32[]{:S(2)}) collective-permute-start(bf16[256,2048]{1,0:T(8,128)(2,1)} %pad_maximum_fusion.5), channel_id=1, source_target_pairs={{0,2},{1,3},{2,0},{3,1},{4,6},{5,7},{6,4},{7,5},{8,10},{9,11},{10,... | collective-permute-start | bytes 3145736 | tf_op jit(solution)/shard_map/ppermute | solution.py:320
  72.3 3.0 %collective-permute-start.15 = (bf16[1,1024,256]{2,1,0:T(8,128)(2,1)S(1)}, bf16[1,1024,256]{2,1,0:T(8,128)(2,1)S(1)}, u32[]{:S(2)}, u32[]{:S(2)}) collective-permute-start(bf16[1,1024,256]{2,1,0:T(8,128)(2,1)S(1)} %collective-permute-done.9.rest_13_.rest_9_), channel_id=1, source_target_pairs={{0,1},{1,0},{2,3},{3,2},{4,5},{5,4},{6,7},{7,6},{8,9},{9,8},{10,11... | collective-permute-start | bytes 1572872 | tf_op jit(solution)/shard_map/ppermute | solution.py:324
  75.4 1.0 copy-start.5
  90.8 6.8 %copy-start.2 = (bf16[128,2176]{1,0:T(8,128)(2,1)}, bf16[128,2176]{1,0:T(8,128)(2,1)S(1)}, u32[]{:S(2)}) copy-start(bf16[128,2176]{1,0:T(8,128)(2,1)S(1)} %get-tuple-element.85) | copy-start | bytes 1671172
  90.9 8.5 %copy-start.16 = (bf16[384,2048]{1,0:T(8,128)(2,1)S(1)}, bf16[384,2048]{1,0:T(8,128)(2,1)}, u32[]{:S(2)}) copy-start(bf16[384,2048]{1,0:T(8,128)(2,1)} %get-tuple-element.99) | copy-start | bytes 4718596
  96.1 14.9 %collective-permute-start.17 = (bf16[128,2176]{1,0:T(8,128)(2,1)S(1)}, bf16[128,2176]{1,0:T(8,128)(2,1)S(1)}, u32[]{:S(2)}, u32[]{:S(2)}) collective-permute-start(bf16[128,2176]{1,0:T(8,128)(2,1)S(1)} %get-tuple-element.87), channel_id=1, source_target_pairs={{0,4},{4,0},{8,12},{12,8},{1,5},{5,1},{9,13},{13,9},{2,6},{6,2},{1... | collective-permute-start | bytes 1671176 | tf_op jit(solution)/shard_map/ppermute | solution.py:316
  97.6 1.9 %copy-start.1 = (bf16[1,2048,256]{2,1,0:T(8,128)(2,1)S(1)}, bf16[1,2048,256]{2,1,0:T(8,128)(2,1)}, u32[]{:S(2)}) copy-start(bf16[1,2048,256]{2,1,0:T(8,128)(2,1)} %param.11) | copy-start | bytes 3145732
  97.7 13.3 %collective-permute-start.16 = (bf16[128,2048]{1,0:T(8,128)(2,1)S(1)}, bf16[128,2048]{1,0:T(8,128)(2,1)S(1)}, u32[]{:S(2)}, u32[]{:S(2)}) collective-permute-start(bf16[128,2048]{1,0:T(8,128)(2,1)S(1)} %slice.72.rest_0_), channel_id=1, source_target_pairs={{0,2},{1,3},{2,0},{3,1},{4,6},{5,7},{6,4},{7,5},{8,10},{9,11},{10,... | collective-permute-start | bytes 1572872 | tf_op jit(solution)/shard_map/ppermute | solution.py:320
  111.0 1.4 copy-start.27
  111.0 1.4 copy-start.20
  111.1 1.6 copy-start.11
  111.1 1.7 copy-start.17
  112.7 1.2 copy-start.18
  112.7 12.5 %collective-permute-start.20 = (bf16[2048,512]{1,0:T(8,128)(2,1)S(1)}, bf16[2048,512]{1,0:T(8,128)(2,1)S(1)}, u32[]{:S(2)}, u32[]{:S(2)}) collective-permute-start(bf16[2048,512]{1,0:T(8,128)(2,1)S(1)} %convolution_convert_fusion.2), channel_id=1, source_target_pairs={{0,1},{1,0},{2,3},{3,2},{4,5},{5,4},{6,7},{7,6},{8,9},{9,8},{10,11... | collective-permute-start | bytes 6291464 | tf_op jit(solution)/shard_map/ppermute | solution.py:324
  113.9 26.3 %collective-permute-start.18 = (bf16[512,1024]{1,0:T(8,128)(2,1)S(1)}, bf16[512,1024]{1,0:T(8,128)(2,1)S(1)}, u32[]{:S(2)}, u32[]{:S(2)}) collective-permute-start(bf16[512,1024]{1,0:T(8,128)(2,1)S(1)} %pad_maximum_fusion.6), channel_id=1, source_target_pairs={{0,2},{1,3},{2,0},{3,1},{4,6},{5,7},{6,4},{7,5},{8,10},{9,11},{10,... | collective-permute-start | bytes 3145736 | tf_op jit(solution)/shard_map/ppermute | solution.py:320
  114.5 25.7 %collective-permute-start.19 = (bf16[128,2176]{1,0:T(8,128)(2,1)S(1)}, bf16[128,2176]{1,0:T(8,128)(2,1)S(1)}, u32[]{:S(2)}, u32[]{:S(2)}) collective-permute-start(bf16[128,2176]{1,0:T(8,128)(2,1)S(1)} %get-tuple-element.98), channel_id=1, source_target_pairs={{0,8},{4,12},{8,0},{12,4},{1,9},{5,13},{9,1},{13,5},{2,10},{6,14},... | collective-permute-start | bytes 1671176 | tf_op jit(solution)/shard_map/ppermute | solution.py:316
  119.6 4.0 %copy-start.26 = (bf16[128,2048]{1,0:T(8,128)(2,1)S(1)}, bf16[128,2048]{1,0:T(8,128)(2,1)}, u32[]{:S(2)}) copy-start(bf16[128,2048]{1,0:T(8,128)(2,1)} %copy-done.25) | copy-start | bytes 1572868
  119.6 4.0 %copy-start.28 = (bf16[128,2048]{1,0:T(8,128)(2,1)S(1)}, bf16[128,2048]{1,0:T(8,128)(2,1)}, u32[]{:S(2)}) copy-start(bf16[128,2048]{1,0:T(8,128)(2,1)} %copy-done.27) | copy-start | bytes 1572868
  123.6 1.9 %copy-start.12 = (bf16[512,2048]{1,0:T(8,128)(2,1)S(1)}, bf16[512,2048]{1,0:T(8,128)(2,1)}, u32[]{:S(2)}) copy-start(bf16[512,2048]{1,0:T(8,128)(2,1)} %copy-done.11) | copy-start | bytes 6291460
  125.2 15.1 %copy-start.10 = (bf16[512,2048]{1,0:T(8,128)(2,1)}, bf16[512,2048]{1,0:T(8,128)(2,1)S(1)}, u32[]{:S(2)}) copy-start(bf16[512,2048]{1,0:T(8,128)(2,1)S(1)} %pad_maximum_fusion.2) | copy-start | bytes 6291460
  126.9 2.0 %copy-start.6 = (f32[2048,512]{1,0:T(8,128)}, f32[2048,512]{1,0:T(8,128)S(1)}, u32[]{:S(2)}) copy-start(f32[2048,512]{1,0:T(8,128)S(1)} %convert_add_fusion) | copy-start | bytes 12582916
  129.0 14.0 %copy-start.3 = (bf16[128,2176]{1,0:T(8,128)(2,1)S(1)}, bf16[128,2176]{1,0:T(8,128)(2,1)}, u32[]{:S(2)}) copy-start(bf16[128,2176]{1,0:T(8,128)(2,1)} %copy-done.2) | copy-start | bytes 1671172
  129.0 14.2 %copy-start.21 = (bf16[128,2176]{1,0:T(8,128)(2,1)S(1)}, bf16[128,2176]{1,0:T(8,128)(2,1)}, u32[]{:S(2)}) copy-start(bf16[128,2176]{1,0:T(8,128)(2,1)} %copy-done.20) | copy-start | bytes 1671172
  140.2 2.8 %copy-start.22 = (bf16[128,2176]{1,0:T(8,128)(2,1)}, bf16[128,2176]{1,0:T(8,128)(2,1)S(1)}, u32[]{:S(2)}) copy-start(bf16[128,2176]{1,0:T(8,128)(2,1)S(1)} %collective-permute-done.19) | copy-start | bytes 1671172
  140.2 2.8 %copy-start.29 = (bf16[512,1024]{1,0:T(8,128)(2,1)}, bf16[512,1024]{1,0:T(8,128)(2,1)S(1)}, u32[]{:S(2)}) copy-start(bf16[512,1024]{1,0:T(8,128)(2,1)S(1)} %collective-permute-done.18) | copy-start | bytes 3145732
  143.0 6.2 %collective-permute-start.23 = (bf16[2048,512]{1,0:T(8,128)(2,1)}, bf16[2048,512]{1,0:T(8,128)(2,1)}, u32[]{:S(2)}, u32[]{:S(2)}) collective-permute-start(bf16[2048,512]{1,0:T(8,128)(2,1)} %add_convert_fusion.1), channel_id=1, source_target_pairs={{0,1},{1,0},{2,3},{3,2},{4,5},{5,4},{6,7},{7,6},{8,9},{9,8},{10,11... | collective-permute-start | bytes 6291464 | tf_op jit(solution)/shard_map/ppermute | solution.py:324
  143.2 28.2 %collective-permute-start.22 = (bf16[2048,256]{1,0:T(8,128)(2,1)S(1)}, bf16[2048,256]{1,0:T(8,128)(2,1)S(1)}, u32[]{:S(2)}, u32[]{:S(2)}) collective-permute-start(bf16[2048,256]{1,0:T(8,128)(2,1)S(1)} %slice.118), channel_id=1, source_target_pairs={{0,2},{1,3},{2,0},{3,1},{4,6},{5,7},{6,4},{7,5},{8,10},{9,11},{10,... | collective-permute-start | bytes 3145736 | tf_op jit(solution)/shard_map/ppermute | solution.py:320
  144.8 26.7 %collective-permute-start.21 = (bf16[128,2176]{1,0:T(8,128)(2,1)S(1)}, bf16[128,2176]{1,0:T(8,128)(2,1)S(1)}, u32[]{:S(2)}, u32[]{:S(2)}) collective-permute-start(bf16[128,2176]{1,0:T(8,128)(2,1)S(1)} %get-tuple-element.112), channel_id=1, source_target_pairs={{0,12},{4,8},{8,4},{12,0},{1,13},{5,9},{9,5},{13,1},{2,14},{6,10},... | collective-permute-start | bytes 1671176 | tf_op jit(solution)/shard_map/ppermute | solution.py:316
  146.0 3.1 %copy-start.15 = (bf16[2048,512]{1,0:T(8,128)(2,1)S(1)}, bf16[2048,512]{1,0:T(8,128)(2,1)}, u32[]{:S(2)}) copy-start(bf16[2048,512]{1,0:T(8,128)(2,1)} %convolution_convert_fusion.1) | copy-start | bytes 6291460
  151.7 19.9 %copy-start.23 = (bf16[128,2176]{1,0:T(8,128)(2,1)S(1)}, bf16[128,2176]{1,0:T(8,128)(2,1)}, u32[]{:S(2)}) copy-start(bf16[128,2176]{1,0:T(8,128)(2,1)} %copy-done.22) | copy-start | bytes 1671172
  153.1 19.5 %slice-start = ((f32[2048,512]{1,0:T(8,128)}), f32[2048,256]{1,0:T(8,128)S(1)}, s32[]{:S(2)}) async-start(f32[2048,512]{1,0:T(8,128)} %copy-done.6), calls=%async_computation | async-start | bytes 4194304 | tf_op jit(solution)/shard_map/slice | solution.py:406
where the time goes:
time: 176 us; the launch traced here: 174 us
  waiting for transfers between devices  94.8 us (54%)
  Pallas kernels  22.3 us (13%)
  starting transfers between devices  19.5 us (11%)
  matrix products  15 us (9%)
  other arithmetic  11 us (6%)
  local copies, waits for them, and re-layouts  10.8 us (6%)
    ppermute x8, waiting for transfers between devices, over_z(): return lax.ppermute(value, 'expert', pairs)  58.4 us
    pallas_call x2, Pallas kernels, slot_compute(): pl.pallas_call(functools.partial(slot_kernel, slots), out_shape=[jax.Shap...  22.3 us
    ppermute x7, waiting for transfers between devices, over_x(): return lax.ppermute(value, 'replica', swap_x)  21.2 us
    dot_general x6, matrix products, outer(): lax.dot_general(lhs, rhs, (((0,), (0,)), ((), ())), preferred_element_typ...  15 us
    ppermute x2, waiting for transfers between devices, over_parts(): return lax.ppermute(value, 'parts', swap_part)  10.7 us
    ppermute x8, starting transfers between devices, over_z(): return lax.ppermute(value, 'expert', pairs)  10 us
    ppermute x7, starting transfers between devices, over_x(): return lax.ppermute(value, 'replica', swap_x)  7.83 us
    unnamed x66, local copies, waits for them, and re-layouts  5.53 us
  transfers between devices with their start and end apart: 24, of which 14 were waited for; matrix products, arithmetic and copies ran while one was open for 14% of the time, Pallas kernels for 13%

commit v1 on v0

--- a/solution.py
+++ b/solution.py
@@ -189,9 +189,9 @@
 
 def slot_kernel(slots, lane_ref, part_ref, *rest):
     ins, grads, rest = rest[:slots], rest[slots : 2 * slots], rest[2 * slots :]
-    own, near, far, far_near = rest[:3], rest[3], rest[4:8], rest[8:12]
-    near_ref, far_ref, hidden_send, hidden_keep, scaled_ref = rest[12:17]
-    backs, rest = rest[17 : 17 + slots], rest[17 + slots :]
+    own, near, far, far_near = rest[:3], rest[3], rest[4:10], rest[10:16]
+    near_ref, far_ref, hidden_send, hidden_keep, scaled_ref = rest[16:21]
+    backs, rest = rest[21 : 21 + slots], rest[21 + slots :]
     held, held_down, rows_in, rows_grad, acts, sems = rest
     features = held.shape[0]
     width = held.shape[1] // 8
@@ -213,7 +213,7 @@
                 pairs = [(near.at[kind], target.at[:, columns])]
             else:
                 pairs = [
-                    (group[2 * side + kind // 2].at[kind % 2], target.at[pl.ds(line, half), columns])
+                    (group[3 * side + kind], target.at[pl.ds(line, half), columns])
                     for side, line in enumerate(lines)
                 ]
             for source, place in pairs:
@@ -290,7 +290,7 @@
         out_shape=[jax.ShapeDtypeStruct(shape, bf) for shape in shapes],
         in_specs=[vmem, pl.BlockSpec(memory_space=pltpu.SMEM)]
         + [vmem] * (2 * slots)
-        + [pl.BlockSpec(memory_space=pl.ANY)] * 12,
+        + [pl.BlockSpec(memory_space=pl.ANY)] * 16,
         out_specs=[vmem] * len(shapes),
         scratch_shapes=[
             pltpu.VMEM((features, 8 * width), bf),
@@ -345,7 +345,6 @@
     own = [gate_weight[0], up_weight[0], down_weight[0]]
     width = own[0].shape[1]
     halves = [lax.dynamic_slice_in_dim(w, y * half, half, 0) for w in own]
-    pieces = [jnp.stack(halves[:2]), halves[2][None]]
     lanes = jnp.arange(128, dtype=jnp.int32)[None, :]
     gate_lanes = sum(
         jnp.where(expert_ids[:, k : k + 1] == lanes, gates[:, k : k + 1], 0) for k in range(2)
@@ -355,27 +354,27 @@
     part_index = jnp.reshape(y, (1,)).astype(jnp.int32)
 
     in_two, in_one = over_z(tokens, apart(2)), over_z(tokens, apart(1))
-    across_0 = over_x(pieces[0])
-    in_two, in_one, across_0, wide_grad, tokens_x, piece_1, stacked = tied(
-        in_two, in_one, across_0, wide_grad, tokens, pieces[1], jnp.stack(own)
+    across = [over_x(w) for w in halves[:2]]
+    other = [over_parts(across[0])]
+    in_two, in_one, across[0], across[1], other[0], wide_grad, tokens_x, half_down, stacked = tied(
+        in_two, in_one, *across, *other, wide_grad, tokens, halves[2], jnp.stack(own)
     )
 
     grad_two, grad_one = over_z(wide_grad, apart(2)), over_z(wide_grad, apart(1))
-    across_1 = over_x(piece_1)
-    other_0 = over_parts(across_0)
+    across.append(over_x(half_down))
+    other.append(over_parts(across[1]))
     near = over_core(stacked)
-    across_1, near, tokens_x = tied(across_1, near, tokens_x)
-    other_1 = over_parts(across_1)
+    across[2], near, tokens_x = tied(across[2], near, tokens_x)
+    other.append(over_parts(across[2]))
     far_a = over_x(tokens_x)
     in_bc = jnp.concatenate([in_one, in_two])
     two = jnp.concatenate([in_two, grad_two], axis=1)
-    two, grad_one, in_bc, far_a, across_0, across_1, other_0, other_1 = tied(
-        two, grad_one, in_bc, far_a, across_0, across_1, other_0, other_1
+    two, grad_one, in_bc, far_a, *far_weights = tied(
+        two, grad_one, in_bc, far_a, *across, *other
     )
 
     three = over_z(two, apart(1))
     far_bc = over_x(in_bc)
-    far_weights = [across_0, across_1, other_0, other_1]
     weights = [*own, near, *far_weights, *[over_core(w) for w in far_weights]]
     acts_abc, crossing_abc, send_abc, keep_abc, scaled_abc, backs = slot_compute(
         [tokens, in_one, in_two], [wide_grad, grad_one, grad_two], lane, part_index, weights
@@ -383,40 +382,44 @@
     three, far_bc, crossing_abc, back_a, back_b, back_c = tied(three, far_bc, crossing_abc, *backs)
 
     in_d, grad_d = three[:, :features], three[:, features:]
-    far_d = over_x(in_d)
-    back_one = over_z(back_b, apart(1))
+    cut = features * 11 // 16
+    far_acts_abc = over_x(crossing_abc)
+    back_two_low = over_z(back_c[:, :cut], apart(2))
+    far_d = over_z(far_bc[rows:], apart(1))
     acts_d, crossing_d, send_d, keep_d, scaled_d, (back_d,) = slot_compute(
         [in_d], [grad_d], lane, part_index, weights
     )
-    far_d, back_one, acts_d, crossing_d, send_d, keep_d, scaled_d, back_d, back_c = tied(
-        far_d, back_one, acts_d, crossing_d, send_d, keep_d, scaled_d, back_d, back_c
-    )
-
-    acts_far = over_x(jnp.concatenate([crossing_abc, crossing_d]))
-    back_two = over_z(back_c, apart(2))
+    (far_acts_abc, back_two_low, far_d, acts_d, crossing_d, send_d, keep_d, scaled_d, back_d,
+     back_b, back_c) = tied(
+        far_acts_abc, back_two_low, far_d, acts_d, crossing_d, send_d, keep_d, scaled_d, back_d,
+        back_b, back_c,
+    )
+
+    far_acts_d = over_x(crossing_d)
+    back_two_high = over_z(back_c[:, cut:], apart(2))
     scaled = jnp.concatenate([scaled_abc, scaled_d])
     send = outer(scaled, jnp.concatenate([send_abc, send_d])).astype(bf)
     keep = outer(scaled, jnp.concatenate([keep_abc, keep_d])).astype(bf)
     both = keep.astype(f32) + over_core(send).astype(f32)
-    acts = jnp.concatenate([acts_abc, acts_d])
-    rows_near = jnp.concatenate([tokens, in_bc, in_d])
-    part_keep = outer(rows_near, acts[:, : 2 * width]).astype(bf)
-    part_send = outer(rows_near, acts[:, 2 * width :]).astype(bf)
-    rows_far = jnp.concatenate([far_a, far_bc, far_d])
-    crossing, both = both[:, width:].astype(bf), both[:, :width]
-    acts_far, back_two, crossing, both, part_keep, part_send, rows_far, back_d = tied(
-        acts_far, back_two, crossing, both, part_keep, part_send, rows_far, back_d
+    crossing, both = both[:, width:].astype(bf), both[:, :width].astype(bf)
+    far_acts_d, back_two_high, crossing, both, back_b, back_d = tied(
+        far_acts_d, back_two_high, crossing, both, back_b, back_d
     )
 
     down_far = over_x(crossing)
     back_three = over_z(back_d, apart(3))
-    part_send = part_send.astype(f32) + outer(rows_far, acts_far[:, 2 * width :])
-    part_keep = part_keep.astype(f32) + outer(rows_far, acts_far[:, : 2 * width])
-    pair = (part_keep + over_core(part_send.astype(bf)).astype(f32)).astype(bf)
+    back_one = over_z(back_b, apart(1))
+    acts = jnp.concatenate([acts_abc, acts_d, far_acts_abc, far_acts_d])
+    every_row = jnp.concatenate([tokens, in_bc, in_d, far_a, far_bc, far_d])
+    send = over_core(outer(every_row, acts[:, 2 * width :]).astype(bf))
+    pair = (outer(every_row, acts[:, : 2 * width]) + send.astype(f32)).astype(bf)
     gate_out, up_out = pair[:, :width], pair[:, width:]
-    back_three, down_far, gate_out, up_out = tied(back_three, down_far, gate_out, up_out)
+    back_one, back_three, down_far, gate_out, up_out = tied(
+        back_one, back_three, down_far, gate_out, up_out
+    )
+    back_two = jnp.concatenate([back_two_low, back_two_high], axis=1)
     returned = [back_a, back_one, back_two, back_three]
-    down = (both + down_far.astype(f32)).astype(bf)
+    down = (both.astype(f32) + down_far.astype(f32)).astype(bf)
     token_grad = sum(r[:, :features].astype(f32) for r in returned).astype(bf)
     gate_grad = sum(
         jnp.where(expert_ids == (z ^ step), r[:, features : features + 1].astype(f32), 0.0)

time: 176 us -> 166 us (0.943)
  waiting for transfers between devices: 94.8 us -> 68.8 us
  local copies, waits for them, and re-layouts: 10.8 us -> 20.6 us
  starting transfers between devices: 19.5 us -> 26.9 us
  Pallas kernels: 22.3 us -> 25.5 us
  matrix products: 15 us -> 12 us
  other arithmetic: 11 us -> 8.3 us
    ppermute x8 -> x10, waiting for transfers between devices: 58.4 us -> 38 us  [over_z(): return lax.ppermute(value, 'expert', pairs)]
    ppermute x2 -> x3, waiting for transfers between devices: 10.7 us -> 1.84 us  [over_parts(): return lax.ppermute(value, 'parts', swap_part)]
    unnamed x66 -> x69, local copies, waits for them, and re-layouts: 5.53 us -> 13.5 us
    ppermute x7 -> x8, waiting for transfers between devices: 21.2 us -> 27.9 us  [over_x(): return lax.ppermute(value, 'replica', swap_x)]
    ppermute x8 -> x10, starting transfers between devices: 10 us -> 15 us  [over_z(): return lax.ppermute(value, 'expert', pairs)]
    ppermute x7 -> x9, waiting for transfers between devices: 4.47 us -> 1.05 us  [over_core(): return lax.ppermute(value, 'replica', swap_core)]
    pallas_call x2, Pallas kernels: 22.3 us -> 25.5 us  [slot_compute(): pl.pallas_call(functools.partial(slot_kernel, slots), out_shape=[jax.Shap...]
    dot_general x6 -> x4, matrix products: 15 us -> 12 us  [outer(): lax.dot_general(lhs, rhs, (((0,), (0,)), ((), ())), preferred_element_typ...]
  transfers between devices with their start and end apart: 24 -> 30, of which waited for: 14 -> 14; matrix products, arithmetic and copies ran while one was open for 14% -> 15% of each run, Pallas kernels for 13% -> 16%
where the time goes in v1:
time: 166 us; the launch traced here: 163 us
  waiting for transfers between devices  68.8 us (41%)
  starting transfers between devices  26.9 us (16%)
  Pallas kernels  25.5 us (15%)
  local copies, waits for them, and re-layouts  20.6 us (12%)
  matrix products  12 us (7%)
  other arithmetic  8.3 us (5%)
    ppermute x10, waiting for transfers between devices, over_z(): return lax.ppermute(value, 'expert', pairs)  38 us
    ppermute x8, waiting for transfers between devices, over_x(): return lax.ppermute(value, 'replica', swap_x)  27.9 us
    pallas_call x2, Pallas kernels, slot_compute(): pl.pallas_call(functools.partial(slot_kernel, slots), out_shape=[jax.Shap...  25.5 us
    ppermute x10, starting transfers between devices, over_z(): return lax.ppermute(value, 'expert', pairs)  15 us
    unnamed x69, local copies, waits for them, and re-layouts  13.5 us
    dot_general x4, matrix products, outer(): lax.dot_general(lhs, rhs, (((0,), (0,)), ((), ())), preferred_element_typ...  12 us
    ppermute x8, starting transfers between devices, over_x(): return lax.ppermute(value, 'replica', swap_x)  8.77 us
  transfers between devices with their start and end apart: 30, of which 14 were waited for; matrix products, arithmetic and copies ran while one was open for 15% of the time, Pallas kernels for 16%

profile of v1, /device:TPU:12, one launch (start us, length us, event | category | flops | bytes accessed | tf_op | source)
XLA Modules:
  0.0 163.2 jit_solution(5864098757288188240)
XLA Ops:
  0.7 2.7 %collective-permute-start = (bf16[128,2048]{1,0:T(8,128)(2,1)}, bf16[128,2048]{1,0:T(8,128)(2,1)S(1)}, u32[]{:S(2)}, u32[]{:S(2)}) collective-permute-start(bf16[128,2048]{1,0:T(8,128)(2,1)} %rest_0_.1), channel_id=1, source_target_pairs={{0,8},{4,12},{8,0},{12,4},{1,9},{5,13},{9,1},{13,5},{2,10},{6,14},... | collective-permute-start | bytes 1572872 | tf_op jit(solution)/shard_map/ppermute | solution.py:316
  3.3 0.4 collective-permute-start.1
  3.8 1.2 dynamic-slice_bitcast_fusion.2
  5.0 1.6 collective-permute-start.2
  6.5 1.1 dynamic-slice_bitcast_fusion.1
  7.6 0.6 collective-permute-start.3
  8.3 1.7 %pad_maximum_fusion = bf16[3,2048,256]{2,1,0:T(8,128)(2,1)S(1)} fusion(bf16[1,2048,256]{2,1,0:T(8,128)(2,1)} %param.13, bf16[1,2048,256]{2,1,0:T(8,128)(2,1)S(1)} %copy-done.10, bf16[1,2048,256]{2,1,0:T(8,128)(2,1)S(1)} %copy-done.9), kind=kLoop, calls=%fused_computation.2 | loop fusion | flops 3145728 | bytes 6291456 | tf_op jit(solution)/shard_map/stack | solution.py:360
  10.0 9.9 %collective-permute-done.2.rest_10_.rest_6_ = bf16[1024,256]{1,0:T(8,128)(2,1)S(1)} collective-permute-done((bf16[1024,256]{1,0:T(8,128)(2,1)S(1)}, bf16[1024,256]{1,0:T(8,128)(2,1)S(1)}, u32[]{:S(2)}, u32[]{:S(2)}) %collective-permute-start.2) | collective-permute-done | bytes 524320 | tf_op jit(solution)/shard_map/ppermute | solution.py:320
  19.9 0.5 collective-permute-start.4
  20.7 8.7 %collective-permute-done.3.rest_11_.rest_7_ = bf16[1024,256]{1,0:T(8,128)(2,1)S(1)} collective-permute-done((bf16[1024,256]{1,0:T(8,128)(2,1)S(1)}, bf16[1024,256]{1,0:T(8,128)(2,1)S(1)}, u32[]{:S(2)}, u32[]{:S(2)}) %collective-permute-start.3) | collective-permute-done | bytes 524320 | tf_op jit(solution)/shard_map/ppermute | solution.py:320
  29.4 0.9 collective-permute-done.4.rest_13_.rest_9_
  30.3 0.4 collective-permute-start.5
  30.7 1.5 collective-permute-start.7
  32.2 1.6 collective-permute-start.6
  33.8 0.5 collective-permute-start.10
  34.3 2.1 %pad_maximum_fusion.2 = bf16[256,2048]{1,0:T(8,128)(2,1)} fusion(bf16[128,2048]{1,0:T(8,128)(2,1)S(1)} %collective-permute-done.rest_2_, bf16[128,2048]{1,0:T(8,128)(2,1)} %copy-done.7), kind=kLoop, calls=%fused_computation.11 | loop fusion | flops 2097152 | bytes 2097152 | tf_op jit(solution)/shard_map/concatenate | solution.py:370
  36.4 8.4 %collective-permute-done.7.rest_12_.rest_8_ = bf16[1024,256]{1,0:T(8,128)(2,1)S(1)} collective-permute-done((bf16[1024,256]{1,0:T(8,128)(2,1)S(1)}, bf16[1024,256]{1,0:T(8,128)(2,1)S(1)}, u32[]{:S(2)}, u32[]{:S(2)}) %collective-permute-start.7) | collective-permute-done | bytes 524320 | tf_op jit(solution)/shard_map/ppermute | solution.py:320
  44.8 0.8 collective-permute-start.11
  45.6 1.2 collective-permute-start.9
  46.8 8.5 %collective-permute-done.5.rest_5_ = bf16[128,2176]{1,0:T(8,128)(2,1)S(1)} collective-permute-done((bf16[128,2176]{1,0:T(8,128)(2,1)S(1)}, bf16[128,2176]{1,0:T(8,128)(2,1)S(1)}, u32[]{:S(2)}, u32[]{:S(2)}) %collective-permute-start.5) | collective-permute-done | bytes 557088 | tf_op jit(solution)/shard_map/ppermute | solution.py:316
  55.3 1.1 pad_maximum_fusion.1
  56.4 1.3 collective-permute-done.6.rest_4_
  57.7 0.9 collective-permute-done.11.rest_15_.rest_11_
  58.6 2.4 %collective-permute-start.12 = (bf16[128,4224]{1,0:T(8,128)(2,1)}, bf16[128,4224]{1,0:T(8,128)(2,1)}, u32[]{:S(2)}, u32[]{:S(2)}) collective-permute-start(bf16[128,4224]{1,0:T(8,128)(2,1)} %pad_maximum_fusion.1), channel_id=1, source_target_pairs={{0,4},{4,0},{8,12},{12,8},{1,5},{5,1},{9,13},{13,9},{2,6},{6,2},{1... | collective-permute-start | bytes 3244040 | tf_op jit(solution)/shard_map/ppermute | solution.py:316
  61.0 0.5 collective-permute-start.15
  61.5 1.4 collective-permute-start.13
  62.9 0.8 copy-done
  64.0 0.3 collective-permute-start.18
  64.5 0.3 copy-done.3
  64.8 0.8 copy-done.15
  65.9 1.1 constant_dynamic-update-slice_fusion.7
  67.0 0.8 collective-permute-done.19.rest_21_.rest_17_
  67.8 1.0 copy-done.1
  68.9 1.0 copy-done.6
  69.9 1.0 copy-done.8
  71.0 15.6 %shard_map.110 = (bf16[384,1024]{1,0:T(8,128)(2,1)}, bf16[384,1024]{1,0:T(8,128)(2,1)}, bf16[384,512]{1,0:T(8,128)(2,1)S(1)}, bf16[384,512]{1,0:T(8,128)(2,1)S(1...) custom-call(f32[1,128]{1,0:T(1,128)S(1)} %compare_convert_fusion.lan, ...), custom_call_target="tpu_custom_call" | custom-call | flops 786432 | bytes 1572864 | tf_op jit(solution)/shard_map/pallas_call | solution.py:288
  86.6 0.9 collective-permute-done.13
  87.4 1.4 collective-permute-start.20
  88.8 1.3 constant_dynamic-update-slice_fusion.6
  90.2 1.1 slice.77
  91.6 2.0 %slice.79.rest_1_ = bf16[128,2176]{1,0:T(8,128)(2,1)} slice(bf16[128,4224]{1,0:T(8,128)(2,1)} %collective-permute-done.12), slice={[0:128], [2048:4224]} | slice | bytes 1114112 | tf_op jit(solution)/shard_map/slice | solution.py:384
  93.6 1.9 %collective-permute-start.21 = (bf16[128,1408]{1,0:T(8,128)(2,1)S(1)}, bf16[128,1408]{1,0:T(8,128)(2,1)S(1)}, u32[]{:S(2)}, u32[]{:S(2)}) collective-permute-start(bf16[128,1408]{1,0:T(8,128)(2,1)S(1)} %slice.76), channel_id=1, source_target_pairs={{0,8},{4,12},{8,0},{12,4},{1,9},{5,13},{9,1},{13,5},{2,10},{6,14},... | collective-permute-start | bytes 1081352 | tf_op jit(solution)/shard_map/ppermute | solution.py:316
  95.5 1.2 constant_dynamic-update-slice_fusion.5
  96.7 2.0 %copy-done.25 = bf16[1024,2048]{1,0:T(8,128)(2,1)} copy-done((bf16[1024,2048]{1,0:T(8,128)(2,1)}, bf16[1024,2048]{1,0:T(8,128)(2,1)S(1)}, u32[]{:S(2)}) %copy-start.25) | copy-done | bytes 4194328
  98.6 9.9 %shard_map.111 = (bf16[128,1024]{1,0:T(8,128)(2,1)S(1)}, bf16[128,1024]{1,0:T(8,128)(2,1)S(1)}, bf16[128,512]{1,0:T(8,128)(2,1)S(1)}, bf16[128,512]{1,0:T(8,128)...) custom-call(f32[1,128]{1,0:T(1,128)S(1)} %compare_convert_fusion.lane_ref, s32[1]{0:T(128)} %bitcast.7.part_ref, ...), custom_call_target="tpu_custom_call" | custom-call | flops 262144 | bytes 524288 | tf_op jit(solution)/shard_map/pallas_call | solution.py:288
  108.6 3.7 %collective-permute-done.21 = bf16[128,1408]{1,0:T(8,128)(2,1)S(1)} collective-permute-done((bf16[128,1408]{1,0:T(8,128)(2,1)S(1)}, bf16[128,1408]{1,0:T(8,128)(2,1)S(1)}, u32[]{:S(2)}, u32[]{:S(2)}) %collective-permute-start.21) | collective-permute-done | bytes 360480 | tf_op jit(solution)/shard_map/ppermute | solution.py:316
  112.4 1.3 convolution_convert_fusion.1
  113.8 1.1 copy-done.26
  115.0 1.3 constant_dynamic-update-slice_fusion.3
  116.3 1.5 collective-permute-start.24
  117.9 0.5 collective-permute-start.23
  118.6 1.3 add_convert_fusion.1
  120.1 5.7 %collective-permute-done.24 = bf16[128,768]{1,0:T(8,128)(2,1)S(1)} collective-permute-done((bf16[128,768]{1,0:T(8,128)(2,1)S(1)}, bf16[128,768]{1,0:T(8,128)(2,1)S(1)}, u32[]{:S(2)}, u32[]{:S(2)}) %collective-permute-start.24) | collective-permute-done | bytes 196640 | tf_op jit(solution)/shard_map/ppermute | solution.py:316
  125.9 3.8 %convolution_convert_fusion = bf16[2048,512]{1,0:T(8,128)(2,1)} fusion(bf16[1024,2048]{1,0:T(8,128)(2,1)S(1)} %constant_dynamic-update-slice_fusion.2, bf16[1024,1024]{1,0:T(8,128)(2,1)S(1)} %constant_dynamic-update-slice_fusion.8), kind=kOutput, calls=%fused_computation.3 | convolution fusion | flops 2148532224 | bytes 7340032 | tf_op jit(solution)/shard_map/dot_general | solution.py:336
  129.8 0.6 collective-permute-start.28
  130.4 2.9 %collective-permute-start.26 = (bf16[128,2176]{1,0:T(8,128)(2,1)}, bf16[128,2176]{1,0:T(8,128)(2,1)S(1)}, u32[]{:S(2)}, u32[]{:S(2)}) collective-permute-start(bf16[128,2176]{1,0:T(8,128)(2,1)} %get-tuple-element.116), channel_id=1, source_target_pairs={{0,4},{4,0},{8,12},{12,8},{1,5},{5,1},{9,13},{13,9},{2,6},{6,2},{1... | collective-permute-start | bytes 1671176 | tf_op jit(solution)/shard_map/ppermute | solution.py:316
  133.3 1.0 collective-permute-start.27
  134.4 5.6 %add_convert_fusion = bf16[2048,512]{1,0:T(8,128)(2,1)S(1)} fusion(bf16[2048,512]{1,0:T(8,128)(2,1)} %collective-permute-done.29, bf16[1024,2048]{1,0:T(8,128)(2,1)} %copy-done.27, bf16[1024,1024]{1,0:T(8,128)(2,1)} %copy-done.24), kind=kOutput, calls=%fused_computation | convolution fusion | flops 2150629376 | bytes 9437184 | tf_op jit(solution)/shard_map/dot_general | solution.py:336
  140.0 1.5 fusion.18
  141.4 5.5 %collective-permute-done.26 = bf16[128,2176]{1,0:T(8,128)(2,1)S(1)} collective-permute-done((bf16[128,2176]{1,0:T(8,128)(2,1)}, bf16[128,2176]{1,0:T(8,128)(2,1)S(1)}, u32[]{:S(2)}, u32[]{:S(2)}) %collective-permute-start.26) | collective-permute-done | bytes 557088 | tf_op jit(solution)/shard_map/ppermute | solution.py:316
  147.0 13.2 %collective-permute-done.27 = bf16[128,2176]{1,0:T(8,128)(2,1)S(1)} collective-permute-done((bf16[128,2176]{1,0:T(8,128)(2,1)}, bf16[128,2176]{1,0:T(8,128)(2,1)S(1)}, u32[]{:S(2)}, u32[]{:S(2)}) %collective-permute-start.27) | collective-permute-done | bytes 557088 | tf_op jit(solution)/shard_map/ppermute | solution.py:316
  160.3 1.1 add_convert_fusion.3
  161.4 1.3 fusion
  162.7 0.5 fusion.15
  (97 shorter events, 2.2 us)
Async XLA Ops:
  0.6 7.6 %copy-start.28 = (s32[128,2]{0,1:T(2,128)S(1)}, s32[128,2]{0,1:T(2,128)}, u32[]{:S(2)}) copy-start(s32[128,2]{0,1:T(2,128)} %param.9) | copy-start | bytes 3076
  0.6 7.6 %copy-start.29 = (bf16[128,2]{0,1:T(2,128)(2,1)S(1)}, bf16[128,2]{0,1:T(2,128)(2,1)}, u32[]{:S(2)}) copy-start(bf16[128,2]{0,1:T(2,128)(2,1)} %param.10) | copy-start | bytes 1540
  0.7 28.7 %collective-permute-start = (bf16[128,2048]{1,0:T(8,128)(2,1)}, bf16[128,2048]{1,0:T(8,128)(2,1)S(1)}, u32[]{:S(2)}, u32[]{:S(2)}) collective-permute-start(bf16[128,2048]{1,0:T(8,128)(2,1)} %rest_0_.1), channel_id=1, source_target_pairs={{0,8},{4,12},{8,0},{12,4},{1,9},{5,13},{9,1},{13,5},{2,10},{6,14},... | collective-permute-start | bytes 1572872 | tf_op jit(solution)/shard_map/ppermute | solution.py:316
  3.3 26.1 %collective-permute-start.1 = (bf16[128,2048]{1,0:T(8,128)(2,1)}, bf16[128,2048]{1,0:T(8,128)(2,1)S(1)}, u32[]{:S(2)}, u32[]{:S(2)}) collective-permute-start(bf16[128,2048]{1,0:T(8,128)(2,1)} %rest_0_.1), channel_id=1, source_target_pairs={{0,4},{4,0},{8,12},{12,8},{1,5},{5,1},{9,13},{13,9},{2,6},{6,2},{1... | collective-permute-start | bytes 1572872 | tf_op jit(solution)/shard_map/ppermute | solution.py:316
  3.8 4.5 %copy-start.9 = (bf16[1,2048,256]{2,1,0:T(8,128)(2,1)S(1)}, bf16[1,2048,256]{2,1,0:T(8,128)(2,1)}, u32[]{:S(2)}) copy-start(bf16[1,2048,256]{2,1,0:T(8,128)(2,1)} %param.11) | copy-start | bytes 3145732
  3.8 4.5 %copy-start.10 = (bf16[1,2048,256]{2,1,0:T(8,128)(2,1)S(1)}, bf16[1,2048,256]{2,1,0:T(8,128)(2,1)}, u32[]{:S(2)}) copy-start(bf16[1,2048,256]{2,1,0:T(8,128)(2,1)} %param.12) | copy-start | bytes 3145732
  5.0 14.9 %collective-permute-start.2 = (bf16[1024,256]{1,0:T(8,128)(2,1)S(1)}, bf16[1024,256]{1,0:T(8,128)(2,1)S(1)}, u32[]{:S(2)}, u32[]{:S(2)}) collective-permute-start(bf16[1024,256]{1,0:T(8,128)(2,1)S(1)} %dynamic-slice_bitcast_fusion.2), channel_id=1, source_target_pairs={{0,2},{1,3},{2,0},{3,1},{4,6},{5,7},{6,4},{7,5},{8,10},{9,11},{10,... | collective-permute-start | bytes 1572872 | tf_op jit(solution)/shard_map/ppermute | solution.py:320
  7.6 21.8 %collective-permute-start.3 = (bf16[1024,256]{1,0:T(8,128)(2,1)S(1)}, bf16[1024,256]{1,0:T(8,128)(2,1)S(1)}, u32[]{:S(2)}, u32[]{:S(2)}) collective-permute-start(bf16[1024,256]{1,0:T(8,128)(2,1)S(1)} %dynamic-slice_bitcast_fusion.1), channel_id=1, source_target_pairs={{0,2},{1,3},{2,0},{3,1},{4,6},{5,7},{6,4},{7,5},{8,10},{9,11},{10,... | collective-permute-start | bytes 1572872 | tf_op jit(solution)/shard_map/ppermute | solution.py:320
  8.3 12.3 %copy-start.11 = (bf16[1,2048,256]{2,1,0:T(8,128)(2,1)S(1)}, bf16[1,2048,256]{2,1,0:T(8,128)(2,1)}, u32[]{:S(2)}) copy-start(bf16[1,2048,256]{2,1,0:T(8,128)(2,1)} %param.13) | copy-start | bytes 3145732
  8.3 12.4 %copy-start.21 = (bf16[128,2048]{1,0:T(8,128)(2,1)S(1)}, bf16[128,2048]{1,0:T(8,128)(2,1)}, u32[]{:S(2)}) copy-start(bf16[128,2048]{1,0:T(8,128)(2,1)} %param.8) | copy-start | bytes 1572868
  19.9 10.4 %collective-permute-start.4 = (bf16[1024,256]{1,0:T(8,128)(2,1)S(1)}, bf16[1024,256]{1,0:T(8,128)(2,1)S(1)}, u32[]{:S(2)}, u32[]{:S(2)}) collective-permute-start(bf16[1024,256]{1,0:T(8,128)(2,1)S(1)} %collective-permute-done.2.rest_10_.rest_6_), channel_id=1, source_target_pairs={{0,16},{16,0},{1,17},{17,1},{2,18},{18,2},{3,19},{19,3},{4,20},{20... | collective-permute-start | bytes 1572872 | tf_op jit(solution)/shard_map/ppermute | solution.py:328
  20.6 25.0 %copy-start.5 = (bf16[128,2048]{1,0:T(8,128)(2,1)S(1)}, bf16[128,2048]{1,0:T(8,128)(2,1)}, u32[]{:S(2)}) copy-start(bf16[128,2048]{1,0:T(8,128)(2,1)} %rest_0_.1) | copy-start | bytes 1572868
  20.7 43.7 %copy-start.13 = (bf16[128,2176]{1,0:T(8,128)(2,1)}, bf16[128,2176]{1,0:T(8,128)(2,1)S(1)}, u32[]{:S(2)}) copy-start(bf16[128,2176]{1,0:T(8,128)(2,1)S(1)} %pad_maximum_fusion.3.rest_3_) | copy-start | bytes 1671172
  29.4 0.9 copy-start.7
  30.3 14.5 %collective-permute-start.8 = (bf16[3,2048,256]{2,1,0:T(8,128)(2,1)S(1)}, bf16[3,2048,256]{2,1,0:T(8,128)(2,1)S(1)}, u32[]{:S(2)}, u32[]{:S(2)}) collective-permute-start(bf16[3,2048,256]{2,1,0:T(8,128)(2,1)S(1)} %pad_maximum_fusion), channel_id=1, source_target_pairs={{0,1},{1,0},{2,3},{3,2},{4,5},{5,4},{6,7},{7,6},{8,9},{9,8},{10,11... | collective-permute-start | bytes 9437192 | tf_op jit(solution)/shard_map/ppermute | solution.py:324
  30.3 24.9 %collective-permute-start.5 = (bf16[128,2176]{1,0:T(8,128)(2,1)S(1)}, bf16[128,2176]{1,0:T(8,128)(2,1)S(1)}, u32[]{:S(2)}, u32[]{:S(2)}) collective-permute-start(bf16[128,2176]{1,0:T(8,128)(2,1)S(1)} %pad_maximum_fusion.3.rest_3_), channel_id=1, source_target_pairs={{0,8},{4,12},{8,0},{12,4},{1,9},{5,13},{9,1},{13,5},{2,10},{6,14},... | collective-permute-start | bytes 1671176 | tf_op jit(solution)/shard_map/ppermute | solution.py:316
  30.7 14.1 %collective-permute-start.7 = (bf16[1024,256]{1,0:T(8,128)(2,1)S(1)}, bf16[1024,256]{1,0:T(8,128)(2,1)S(1)}, u32[]{:S(2)}, u32[]{:S(2)}) collective-permute-start(bf16[1024,256]{1,0:T(8,128)(2,1)S(1)} %dynamic-slice_bitcast_fusion), channel_id=1, source_target_pairs={{0,2},{1,3},{2,0},{3,1},{4,6},{5,7},{6,4},{7,5},{8,10},{9,11},{10,... | collective-permute-start | bytes 1572872 | tf_op jit(solution)/shard_map/ppermute | solution.py:320
  32.2 25.5 %collective-permute-start.6 = (bf16[128,2176]{1,0:T(8,128)(2,1)S(1)}, bf16[128,2176]{1,0:T(8,128)(2,1)S(1)}, u32[]{:S(2)}, u32[]{:S(2)}) collective-permute-start(bf16[128,2176]{1,0:T(8,128)(2,1)S(1)} %pad_maximum_fusion.3.rest_3_), channel_id=1, source_target_pairs={{0,4},{4,0},{8,12},{12,8},{1,5},{5,1},{9,13},{13,9},{2,6},{6,2},{1... | collective-permute-start | bytes 1671176 | tf_op jit(solution)/shard_map/ppermute | solution.py:316
  33.8 22.6 %collective-permute-start.10 = (bf16[1024,256]{1,0:T(8,128)(2,1)S(1)}, bf16[1024,256]{1,0:T(8,128)(2,1)S(1)}, u32[]{:S(2)}, u32[]{:S(2)}) collective-permute-start(bf16[1024,256]{1,0:T(8,128)(2,1)S(1)} %collective-permute-done.3.rest_11_.rest_7_), channel_id=1, source_target_pairs={{0,16},{16,0},{1,17},{17,1},{2,18},{18,2},{3,19},{19,3},{4,20},{20... | collective-permute-start | bytes 1572872 | tf_op jit(solution)/shard_map/ppermute | solution.py:328
  44.8 19.7 %copy-start.12 = (bf16[3,2048,256]{2,1,0:T(8,128)(2,1)}, bf16[3,2048,256]{2,1,0:T(8,128)(2,1)S(1)}, u32[]{:S(2)}) copy-start(bf16[3,2048,256]{2,1,0:T(8,128)(2,1)S(1)} %collective-permute-done.8.rest_9_.rest_5_) | copy-start | bytes 9437188
  44.8 13.8 %collective-permute-start.11 = (bf16[1024,256]{1,0:T(8,128)(2,1)S(1)}, bf16[1024,256]{1,0:T(8,128)(2,1)}, u32[]{:S(2)}, u32[]{:S(2)}) collective-permute-start(bf16[1024,256]{1,0:T(8,128)(2,1)S(1)} %collective-permute-done.7.rest_12_.rest_8_), channel_id=1, source_target_pairs={{0,16},{16,0},{1,17},{17,1},{2,18},{18,2},{3,19},{19,3},{4,20},{20... | collective-permute-start | bytes 1572872 | tf_op jit(solution)/shard_map/ppermute | solution.py:328
  45.6 13.1 %collective-permute-start.9 = (bf16[128,2048]{1,0:T(8,128)(2,1)S(1)}, bf16[128,2048]{1,0:T(8,128)(2,1)S(1)}, u32[]{:S(2)}, u32[]{:S(2)}) collective-permute-start(bf16[128,2048]{1,0:T(8,128)(2,1)S(1)} %copy-done.5), channel_id=1, source_target_pairs={{0,2},{1,3},{2,0},{3,1},{4,6},{5,7},{6,4},{7,5},{8,10},{9,11},{10,... | collective-permute-start | bytes 1572872 | tf_op jit(solution)/shard_map/ppermute | solution.py:320
  55.3 9.2 %copy-start.14 = (bf16[128,2176]{1,0:T(8,128)(2,1)}, bf16[128,2176]{1,0:T(8,128)(2,1)S(1)}, u32[]{:S(2)}) copy-start(bf16[128,2176]{1,0:T(8,128)(2,1)S(1)} %collective-permute-done.5.rest_5_) | copy-start | bytes 1671172
  57.7 6.7 %copy-start.18 = (bf16[128,2176]{1,0:T(8,128)(2,1)}, bf16[128,2176]{1,0:T(8,128)(2,1)S(1)}, u32[]{:S(2)}) copy-start(bf16[128,2176]{1,0:T(8,128)(2,1)S(1)} %collective-permute-done.6.rest_4_) | copy-start | bytes 1671172
  58.6 5.8 %copy-start.22 = (bf16[128,2048]{1,0:T(8,128)(2,1)}, bf16[128,2048]{1,0:T(8,128)(2,1)S(1)}, u32[]{:S(2)}) copy-start(bf16[128,2048]{1,0:T(8,128)(2,1)S(1)} %collective-permute-done.9) | copy-start | bytes 1572868
  58.6 28.8 %collective-permute-start.12 = (bf16[128,4224]{1,0:T(8,128)(2,1)}, bf16[128,4224]{1,0:T(8,128)(2,1)}, u32[]{:S(2)}, u32[]{:S(2)}) collective-permute-start(bf16[128,4224]{1,0:T(8,128)(2,1)} %pad_maximum_fusion.1), channel_id=1, source_target_pairs={{0,4},{4,0},{8,12},{12,8},{1,5},{5,1},{9,13},{13,9},{2,6},{6,2},{1... | collective-permute-start | bytes 3244040 | tf_op jit(solution)/shard_map/ppermute | solution.py:316
  61.0 1.9 %collective-permute-start.14 = (bf16[1024,256]{1,0:T(8,128)(2,1)S(1)}, bf16[1024,256]{1,0:T(8,128)(2,1)S(1)}, u32[]{:S(2)}, u32[]{:S(2)}) collective-permute-start(bf16[1024,256]{1,0:T(8,128)(2,1)S(1)} %collective-permute-done.2.rest_10_.rest_6_), channel_id=1, source_target_pairs={{0,1},{1,0},{2,3},{3,2},{4,5},{5,4},{6,7},{7,6},{8,9},{9,8},{10,11... | collective-permute-start | bytes 1572872 | tf_op jit(solution)/shard_map/ppermute | solution.py:324
  61.0 2.9 %collective-permute-start.15 = (bf16[1024,256]{1,0:T(8,128)(2,1)S(1)}, bf16[1024,256]{1,0:T(8,128)(2,1)S(1)}, u32[]{:S(2)}, u32[]{:S(2)}) collective-permute-start(bf16[1024,256]{1,0:T(8,128)(2,1)S(1)} %collective-permute-done.3.rest_11_.rest_7_), channel_id=1, source_target_pairs={{0,1},{1,0},{2,3},{3,2},{4,5},{5,4},{6,7},{7,6},{8,9},{9,8},{10,11... | collective-permute-start | bytes 1572872 | tf_op jit(solution)/shard_map/ppermute | solution.py:324
  61.5 2.9 %collective-permute-start.16 = (bf16[1024,256]{1,0:T(8,128)(2,1)S(1)}, bf16[1024,256]{1,0:T(8,128)(2,1)S(1)}, u32[]{:S(2)}, u32[]{:S(2)}) collective-permute-start(bf16[1024,256]{1,0:T(8,128)(2,1)S(1)} %collective-permute-done.7.rest_12_.rest_8_), channel_id=1, source_target_pairs={{0,1},{1,0},{2,3},{3,2},{4,5},{5,4},{6,7},{7,6},{8,9},{9,8},{10,11... | collective-permute-start | bytes 1572872 | tf_op jit(solution)/shard_map/ppermute | solution.py:324
  61.5 25.9 %collective-permute-start.13 = (bf16[256,2048]{1,0:T(8,128)(2,1)}, bf16[256,2048]{1,0:T(8,128)(2,1)}, u32[]{:S(2)}, u32[]{:S(2)}) collective-permute-start(bf16[256,2048]{1,0:T(8,128)(2,1)} %pad_maximum_fusion.2), channel_id=1, source_target_pairs={{0,2},{1,3},{2,0},{3,1},{4,6},{5,7},{6,4},{7,5},{8,10},{9,11},{10,... | collective-permute-start | bytes 3145736 | tf_op jit(solution)/shard_map/ppermute | solution.py:320
  62.9 0.8 copy-start
  63.7 3.2 %collective-permute-start.17 = (bf16[1024,256]{1,0:T(8,128)(2,1)S(1)}, bf16[1024,256]{1,0:T(8,128)(2,1)}, u32[]{:S(2)}, u32[]{:S(2)}) collective-permute-start(bf16[1024,256]{1,0:T(8,128)(2,1)S(1)} %collective-permute-done.4.rest_13_.rest_9_), channel_id=1, source_target_pairs={{0,1},{1,0},{2,3},{3,2},{4,5},{5,4},{6,7},{7,6},{8,9},{9,8},{10,11... | collective-permute-start | bytes 1572872 | tf_op jit(solution)/shard_map/ppermute | solution.py:324
  64.0 0.8 copy-start.3
  64.0 3.0 %collective-permute-start.18 = (bf16[1024,256]{1,0:T(8,128)(2,1)S(1)}, bf16[1024,256]{1,0:T(8,128)(2,1)}, u32[]{:S(2)}, u32[]{:S(2)}) collective-permute-start(bf16[1024,256]{1,0:T(8,128)(2,1)S(1)} %collective-permute-done.10.rest_14_.rest_10_), channel_id=1, source_target_pairs={{0,1},{1,0},{2,3},{3,2},{4,5},{5,4},{6,7},{7,6},{8,9},{9,8},{10,11... | collective-permute-start | bytes 1572872 | tf_op jit(solution)/shard_map/ppermute | solution.py:324
  64.8 0.8 copy-start.15
  65.6 2.3 %collective-permute-start.19 = (bf16[1024,256]{1,0:T(8,128)(2,1)}, bf16[1024,256]{1,0:T(8,128)(2,1)}, u32[]{:S(2)}, u32[]{:S(2)}) collective-permute-start(bf16[1024,256]{1,0:T(8,128)(2,1)} %collective-permute-done.11.rest_15_.rest_11_), channel_id=1, source_target_pairs={{0,1},{1,0},{2,3},{3,2},{4,5},{5,4},{6,7},{7,6},{8,9},{9,8},{10,11... | collective-permute-start | bytes 1572872 | tf_op jit(solution)/shard_map/ppermute | solution.py:324
  67.8 1.0 copy-start.1
  68.9 1.0 copy-start.6
  69.9 1.0 copy-start.8
  86.5 4.9 %copy-start.16 = (bf16[384,2048]{1,0:T(8,128)(2,1)S(1)}, bf16[384,2048]{1,0:T(8,128)(2,1)}, u32[]{:S(2)}) copy-start(bf16[384,2048]{1,0:T(8,128)(2,1)} %get-tuple-element.108) | copy-start | bytes 4718596
  87.4 24.9 %collective-permute-start.20 = (bf16[384,1024]{1,0:T(8,128)(2,1)}, bf16[384,1024]{1,0:T(8,128)(2,1)S(1)}, u32[]{:S(2)}, u32[]{:S(2)}) collective-permute-start(bf16[384,1024]{1,0:T(8,128)(2,1)} %get-tuple-element.95), channel_id=1, source_target_pairs={{0,2},{1,3},{2,0},{3,1},{4,6},{5,7},{6,4},{7,5},{8,10},{9,11},{10,... | collective-permute-start | bytes 2359304 | tf_op jit(solution)/shard_map/ppermute | solution.py:320
  91.2 21.0 %collective-permute-start.22 = (bf16[128,2048]{1,0:T(8,128)(2,1)S(1)}, bf16[128,2048]{1,0:T(8,128)(2,1)S(1)}, u32[]{:S(2)}, u32[]{:S(2)}) collective-permute-start(bf16[128,2048]{1,0:T(8,128)(2,1)S(1)} %slice.77), channel_id=1, source_target_pairs={{0,4},{4,0},{8,12},{12,8},{1,5},{5,1},{9,13},{13,9},{2,6},{6,2},{1... | collective-permute-start | bytes 1572872 | tf_op jit(solution)/shard_map/ppermute | solution.py:316
  91.4 2.2 %copy-start.19 = (bf16[128,2176]{1,0:T(8,128)(2,1)S(1)}, bf16[128,2176]{1,0:T(8,128)(2,1)}, u32[]{:S(2)}) copy-start(bf16[128,2176]{1,0:T(8,128)(2,1)} %get-tuple-element.107) | copy-start | bytes 1671172
  91.6 7.1 %copy-start.2 = (bf16[1024,256]{1,0:T(8,128)(2,1)S(1)}, bf16[1024,256]{1,0:T(8,128)(2,1)}, u32[]{:S(2)}) copy-start(bf16[1024,256]{1,0:T(8,128)(2,1)} %copy-done) | copy-start | bytes 1572868
  91.6 7.1 %copy-start.4 = (bf16[1024,256]{1,0:T(8,128)(2,1)S(1)}, bf16[1024,256]{1,0:T(8,128)(2,1)}, u32[]{:S(2)}) copy-start(bf16[1024,256]{1,0:T(8,128)(2,1)} %copy-done.3) | copy-start | bytes 1572868
  93.6 18.7 %collective-permute-start.21 = (bf16[128,1408]{1,0:T(8,128)(2,1)S(1)}, bf16[128,1408]{1,0:T(8,128)(2,1)S(1)}, u32[]{:S(2)}, u32[]{:S(2)}) collective-permute-start(bf16[128,1408]{1,0:T(8,128)(2,1)S(1)} %slice.76), channel_id=1, source_target_pairs={{0,8},{4,12},{8,0},{12,4},{1,9},{5,13},{9,1},{13,5},{2,10},{6,14},... | collective-permute-start | bytes 1081352 | tf_op jit(solution)/shard_map/ppermute | solution.py:316
  96.7 2.0 %copy-start.25 = (bf16[1024,2048]{1,0:T(8,128)(2,1)}, bf16[1024,2048]{1,0:T(8,128)(2,1)S(1)}, u32[]{:S(2)}) copy-start(bf16[1024,2048]{1,0:T(8,128)(2,1)S(1)} %get-tuple-element.137) | copy-start | bytes 12582916
  112.3 1.4 copy-start.17
  112.3 1.5 copy-start.23
  112.4 2.6 %copy-start.26 = (bf16[1024,2048]{1,0:T(8,128)(2,1)S(1)}, bf16[1024,2048]{1,0:T(8,128)(2,1)}, u32[]{:S(2)}) copy-start(bf16[1024,2048]{1,0:T(8,128)(2,1)} %copy-done.25) | copy-start | bytes 12582916
  113.7 4.9 %collective-permute-start.25 = (bf16[2048,512]{1,0:T(8,128)(2,1)S(1)}, bf16[2048,512]{1,0:T(8,128)(2,1)S(1)}, u32[]{:S(2)}, u32[]{:S(2)}) collective-permute-start(bf16[2048,512]{1,0:T(8,128)(2,1)S(1)} %convolution_convert_fusion.1), channel_id=1, source_target_pairs={{0,1},{1,0},{2,3},{3,2},{4,5},{5,4},{6,7},{7,6},{8,9},{9,8},{10,11... | collective-permute-start | bytes 6291464 | tf_op jit(solution)/shard_map/ppermute | solution.py:324
  116.3 9.5 %collective-permute-start.24 = (bf16[128,768]{1,0:T(8,128)(2,1)S(1)}, bf16[128,768]{1,0:T(8,128)(2,1)S(1)}, u32[]{:S(2)}, u32[]{:S(2)}) collective-permute-start(bf16[128,768]{1,0:T(8,128)(2,1)S(1)} %slice.80), channel_id=1, source_target_pairs={{0,8},{4,12},{8,0},{12,4},{1,9},{5,13},{9,1},{13,5},{2,10},{6,14},... | collective-permute-start | bytes 589832 | tf_op jit(solution)/shard_map/ppermute | solution.py:316
  117.9 7.9 %collective-permute-start.23 = (bf16[128,1024]{1,0:T(8,128)(2,1)S(1)}, bf16[128,1024]{1,0:T(8,128)(2,1)S(1)}, u32[]{:S(2)}, u32[]{:S(2)}) collective-permute-start(bf16[128,1024]{1,0:T(8,128)(2,1)S(1)} %get-tuple-element.106), channel_id=1, source_target_pairs={{0,2},{1,3},{2,0},{3,1},{4,6},{5,7},{6,4},{7,5},{8,10},{9,11},{10,... | collective-permute-start | bytes 786440 | tf_op jit(solution)/shard_map/ppermute | solution.py:320
  118.5 7.3 %copy-start.27 = (bf16[1024,2048]{1,0:T(8,128)(2,1)}, bf16[1024,2048]{1,0:T(8,128)(2,1)S(1)}, u32[]{:S(2)}) copy-start(bf16[1024,2048]{1,0:T(8,128)(2,1)S(1)} %constant_dynamic-update-slice_fusion.2) | copy-start | bytes 12582916
  125.8 3.8 %copy-start.24 = (bf16[1024,1024]{1,0:T(8,128)(2,1)}, bf16[1024,1024]{1,0:T(8,128)(2,1)S(1)}, u32[]{:S(2)}) copy-start(bf16[1024,1024]{1,0:T(8,128)(2,1)S(1)} %constant_dynamic-update-slice_fusion.8) | copy-start | bytes 6291460
  125.8 3.8 %copy-start.20 = (bf16[128,2176]{1,0:T(8,128)(2,1)S(1)}, bf16[128,2176]{1,0:T(8,128)(2,1)}, u32[]{:S(2)}) copy-start(bf16[128,2176]{1,0:T(8,128)(2,1)} %get-tuple-element.94) | copy-start | bytes 1671172
  129.6 4.8 %collective-permute-start.29 = (bf16[2048,512]{1,0:T(8,128)(2,1)}, bf16[2048,512]{1,0:T(8,128)(2,1)}, u32[]{:S(2)}, u32[]{:S(2)}) collective-permute-start(bf16[2048,512]{1,0:T(8,128)(2,1)} %convolution_convert_fusion), channel_id=1, source_target_pairs={{0,1},{1,0},{2,3},{3,2},{4,5},{5,4},{6,7},{7,6},{8,9},{9,8},{10,11... | collective-permute-start | bytes 6291464 | tf_op jit(solution)/shard_map/ppermute | solution.py:324
  129.8 30.4 %collective-permute-start.28 = (bf16[2048,256]{1,0:T(8,128)(2,1)S(1)}, bf16[2048,256]{1,0:T(8,128)(2,1)S(1)}, u32[]{:S(2)}, u32[]{:S(2)}) collective-permute-start(bf16[2048,256]{1,0:T(8,128)(2,1)S(1)} %get-tuple-element.118), channel_id=1, source_target_pairs={{0,2},{1,3},{2,0},{3,1},{4,6},{5,7},{6,4},{7,5},{8,10},{9,11},{10,... | collective-permute-start | bytes 3145736 | tf_op jit(solution)/shard_map/ppermute | solution.py:320
  130.4 16.6 %collective-permute-start.26 = (bf16[128,2176]{1,0:T(8,128)(2,1)}, bf16[128,2176]{1,0:T(8,128)(2,1)S(1)}, u32[]{:S(2)}, u32[]{:S(2)}) collective-permute-start(bf16[128,2176]{1,0:T(8,128)(2,1)} %get-tuple-element.116), channel_id=1, source_target_pairs={{0,4},{4,0},{8,12},{12,8},{1,5},{5,1},{9,13},{13,9},{2,6},{6,2},{1... | collective-permute-start | bytes 1671176 | tf_op jit(solution)/shard_map/ppermute | solution.py:316
  133.3 26.9 %collective-permute-start.27 = (bf16[128,2176]{1,0:T(8,128)(2,1)}, bf16[128,2176]{1,0:T(8,128)(2,1)S(1)}, u32[]{:S(2)}, u32[]{:S(2)}) collective-permute-start(bf16[128,2176]{1,0:T(8,128)(2,1)} %get-tuple-element.117), channel_id=1, source_target_pairs={{0,12},{4,8},{8,4},{12,0},{1,13},{5,9},{9,5},{13,1},{2,14},{6,10},... | collective-permute-start | bytes 1671176 | tf_op jit(solution)/shard_map/ppermute | solution.py:316

commit v2 on v1

--- a/solution.py
+++ b/solution.py
@@ -187,15 +187,19 @@
 swap_part = [(0, 1), (1, 0)]
 
 
-def slot_kernel(slots, lane_ref, part_ref, *rest):
-    ins, grads, rest = rest[:slots], rest[slots : 2 * slots], rest[2 * slots :]
+def slot_kernel(slots, joined, later, cuts, splits, lane_ref, part_ref, *rest):
+    count_in = slots * (1 if joined else 2)
+    ins, rest = rest[:count_in], rest[count_in:]
     own, near, far, far_near = rest[:3], rest[3], rest[4:10], rest[10:16]
-    near_ref, far_ref, hidden_send, hidden_keep, scaled_ref = rest[16:21]
-    backs, rest = rest[21 : 21 + slots], rest[21 + slots :]
-    held, held_down, rows_in, rows_grad, acts, sems = rest
-    features = held.shape[0]
-    width = held.shape[1] // 8
-    half, quarter = features // 2, features // 4
+    rest = rest[16 + (4 if later else 0) :]
+    kept, far_refs, rest = rest[:4], rest[4 : 4 + len(splits)], rest[4 + len(splits) :]
+    backs, rest = rest[: len(cuts)], rest[len(cuts) :]
+    held, held_down, rows_in, rows_grad, acts, sems = rest[:6]
+    near_ref, hidden_send, hidden_keep, scaled_ref = rest[6:10] if later else kept
+    _, features, width = held.shape
+    half, eighth = features // 2, features // 8
+    height = ins[0].shape[0]
+    rows = slots * height
     copies = [[] for _ in range(4)]
     first = pl.multiple_of(part_ref[0] * half, half)
     second = pl.multiple_of(half - part_ref[0] * half, half)
@@ -204,16 +208,14 @@
         ((own, None), (near, None), (far, (first, second)), (far_near, (first, second)))
     ):
         for kind in range(3):
-            target = held_down if kind == 2 else held
-            column = share * width if kind == 2 else (2 * share + kind) * width
-            columns = pl.ds(column, width)
+            target = held_down.at[share] if kind == 2 else held.at[2 * share + kind]
             if share == 0:
-                pairs = [(own[kind], target.at[:, columns])]
+                pairs = [(own[kind], target)]
             elif share == 1:
-                pairs = [(near.at[kind], target.at[:, columns])]
+                pairs = [(near.at[kind], target)]
             else:
                 pairs = [
-                    (group[3 * side + kind], target.at[pl.ds(line, half), columns])
+                    (group[3 * side + kind], target.at[pl.ds(line, half), :])
                     for side, line in enumerate(lines)
                 ]
             for source, place in pairs:
@@ -222,28 +224,23 @@
     for group in copies:
         for copy in group:
             copy.start()
-    height = ins[0].shape[0]
     gates = []
-    for slot, (in_ref, grad_ref) in enumerate(zip(ins, grads)):
+    for slot in range(slots):
         lines = slice(slot * height, (slot + 1) * height)
-        rows_in[lines, :] = in_ref[...]
-        rows_grad[lines, :] = grad_ref[:, :features]
-        lanes = grad_ref[:, features:].astype(jnp.float32)
+        grad_ref, begin = (ins[slot], features) if joined else (ins[slots + slot], 0)
+        rows_in[lines, :] = ins[slot][:, :features]
+        rows_grad[lines, :] = grad_ref[:, begin : begin + features]
+        lanes = grad_ref[:, begin + features :].astype(jnp.float32)
         gates.append(jnp.sum(lanes * lane_ref[...], axis=1, keepdims=True))
     gate = jnp.concatenate(gates)
-    scaled_ref[...] = (gate * rows_grad[...].astype(jnp.float32)).astype(jnp.bfloat16)
+    scaled_ref[:rows, :] = (gate * rows_grad[...].astype(jnp.float32)).astype(jnp.bfloat16)
     gate_sum = jnp.zeros(gate.shape, jnp.float32)
     for share in range(4):
         for copy in copies[share]:
             copy.wait()
-        both = slice(2 * share * width, 2 * (share + 1) * width)
-        pre = jnp.dot(rows_in[...], held[:, both], preferred_element_type=jnp.float32)
-        pre_gate, pre_up = pre[:, :width], pre[:, width:]
-        back_proj = jnp.dot(
-            rows_grad[...],
-            held_down[:, share * width : (share + 1) * width],
-            preferred_element_type=jnp.float32,
-        )
+        pre_gate = jnp.dot(rows_in[...], held[2 * share], preferred_element_type=jnp.float32)
+        pre_up = jnp.dot(rows_in[...], held[2 * share + 1], preferred_element_type=jnp.float32)
+        back_proj = jnp.dot(rows_grad[...], held_down[share], preferred_element_type=jnp.float32)
         sigmoid_g = jax.nn.sigmoid(pre_gate)
         activated = pre_gate * sigmoid_g
         hidden_act = activated * pre_up
@@ -257,55 +254,77 @@
         acts[:, (2 * share + 1) * width : 2 * (share + 1) * width] = grad_up
         hidden = hidden_send if share % 2 else hidden_keep
         pick = share // 2
-        hidden[:, pick * width : (pick + 1) * width] = hidden_act.astype(jnp.bfloat16)
-    near_ref[...] = acts[:, : 4 * width]
-    far_ref[...] = acts[:, 4 * width :]
-    for piece in range(4):
-        lines = slice(piece * quarter, (piece + 1) * quarter)
-        part = lax.dot_general(
-            acts[...],
-            held[lines, :],
-            (((1,), (1,)), ((), ())),
-            preferred_element_type=jnp.float32,
+        hidden[:rows, pick * width : (pick + 1) * width] = hidden_act.astype(jnp.bfloat16)
+    near_ref[:rows, :] = acts[:, : 4 * width]
+    for far_ref, (begin, end) in zip(far_refs, splits):
+        far_ref[...] = acts[begin:end, 4 * width :]
+    stores = []
+    if later:
+        for place, source in enumerate((near_ref, hidden_send, hidden_keep, scaled_ref)):
+            target = kept[place].at[pl.ds(kept[place].shape[0] - rows, rows), :]
+            stores.append(pltpu.make_async_copy(source, target, sems.at[count + place]))
+        for store in stores:
+            store.start()
+    for piece in range(8):
+        lines = slice(piece * eighth, (piece + 1) * eighth)
+        part = sum(
+            lax.dot_general(
+                acts[:, k * width : (k + 1) * width],
+                held[k, lines, :],
+                (((1,), (1,)), ((), ())),
+                preferred_element_type=jnp.float32,
+            )
+            for k in range(8)
         ).astype(jnp.bfloat16)
-        for slot, back in enumerate(backs):
-            back[:, lines] = part[slot * height : (slot + 1) * height]
-    for slot, back in enumerate(backs):
-        back[:, features:] = jnp.broadcast_to(
-            gate_sum[slot * height : (slot + 1) * height], (height, 128)
-        ).astype(jnp.bfloat16)
-
-
-def slot_compute(ins, grads, lane, part, weights):
+        for back, (slot, begin, end) in zip(backs, cuts):
+            if begin <= piece * eighth < end:
+                back[:, piece * eighth - begin : (piece + 1) * eighth - begin] = part[
+                    slot * height : (slot + 1) * height
+                ]
+    for back, (slot, begin, end) in zip(backs, cuts):
+        if end > features:
+            back[:, features - begin :] = jnp.broadcast_to(
+                gate_sum[slot * height : (slot + 1) * height], (height, 128)
+            ).astype(jnp.bfloat16)
+    for store in stores:
+        store.wait()
+
+
+def slot_compute(ins, grads, lane, part, weights, total, cuts, splits, kept=()):
     slots = len(ins)
     height = ins[0].shape[0]
     rows = slots * height
     features, width = weights[0].shape
     bf = jnp.bfloat16
-    shapes = [(rows, c) for c in (4 * width, 4 * width, 2 * width, 2 * width, features)]
-    shapes += [(height, features + 128)] * slots
+    columns = [4 * width, 2 * width, 2 * width, features]
+    shapes = [(total, c) for c in columns] + [(end - begin, 4 * width) for begin, end in splits]
+    shapes += [(height, end - begin) for _, begin, end in cuts]
     vmem = pl.BlockSpec(memory_space=pltpu.VMEM)
+    anywhere = pl.BlockSpec(memory_space=pl.ANY)
+    operands = [lane, part, *ins, *grads, *weights, *kept]
     out = pl.pallas_call(
-        functools.partial(slot_kernel, slots),
+        functools.partial(slot_kernel, slots, not grads, bool(kept), cuts, splits),
         out_shape=[jax.ShapeDtypeStruct(shape, bf) for shape in shapes],
         in_specs=[vmem, pl.BlockSpec(memory_space=pltpu.SMEM)]
-        + [vmem] * (2 * slots)
-        + [pl.BlockSpec(memory_space=pl.ANY)] * 16,
-        out_specs=[vmem] * len(shapes),
+        + [vmem] * (len(ins) + len(grads))
+        + [anywhere] * (16 + len(kept)),
+        out_specs=[anywhere if kept else vmem] * 4 + [vmem] * (len(shapes) - 4),
         scratch_shapes=[
-            pltpu.VMEM((features, 8 * width), bf),
-            pltpu.VMEM((features, 4 * width), bf),
+            pltpu.VMEM((8, features, width), bf),
+            pltpu.VMEM((4, features, width), bf),
             pltpu.VMEM((rows, features), bf),
             pltpu.VMEM((rows, features), bf),
             pltpu.VMEM((rows, 8 * width), bf),
-            pltpu.SemaphoreType.DMA((18,)),
-        ],
+            pltpu.SemaphoreType.DMA((22,)),
+        ]
+        + [pltpu.VMEM((rows, c), bf) for c in columns if kept],
+        input_output_aliases={len(operands) - len(kept) + i: i for i in range(len(kept))},
         compiler_params=pltpu.CompilerParams(vmem_limit_bytes=48 * 1024 * 1024),
         cost_estimate=pl.CostEstimate(
             flops=rows * features, bytes_accessed=2 * rows * features, transcendentals=0
         ),
-    )(lane, part, *ins, *grads, *weights)
-    return (*out[:5], out[5:])
+    )(*operands)
+    return out[:4], out[4 : 4 + len(splits)], out[4 + len(splits) :]
 
 
 def tied(*values):
@@ -376,48 +395,70 @@
     three = over_z(two, apart(1))
     far_bc = over_x(in_bc)
     weights = [*own, near, *far_weights, *[over_core(w) for w in far_weights]]
-    acts_abc, crossing_abc, send_abc, keep_abc, scaled_abc, backs = slot_compute(
-        [tokens, in_one, in_two], [wide_grad, grad_one, grad_two], lane, part_index, weights
-    )
-    three, far_bc, crossing_abc, back_a, back_b, back_c = tied(three, far_bc, crossing_abc, *backs)
-
-    in_d, grad_d = three[:, :features], three[:, features:]
-    cut = features * 11 // 16
-    far_acts_abc = over_x(crossing_abc)
-    back_two_low = over_z(back_c[:, :cut], apart(2))
-    far_d = over_z(far_bc[rows:], apart(1))
-    acts_d, crossing_d, send_d, keep_d, scaled_d, (back_d,) = slot_compute(
-        [in_d], [grad_d], lane, part_index, weights
-    )
-    (far_acts_abc, back_two_low, far_d, acts_d, crossing_d, send_d, keep_d, scaled_d, back_d,
-     back_b, back_c) = tied(
-        far_acts_abc, back_two_low, far_d, acts_d, crossing_d, send_d, keep_d, scaled_d, back_d,
-        back_b, back_c,
-    )
-
-    far_acts_d = over_x(crossing_d)
-    back_two_high = over_z(back_c[:, cut:], apart(2))
-    scaled = jnp.concatenate([scaled_abc, scaled_d])
-    send = outer(scaled, jnp.concatenate([send_abc, send_d])).astype(bf)
-    keep = outer(scaled, jnp.concatenate([keep_abc, keep_d])).astype(bf)
+    slots, wide = 4, features + 128
+    kept, (crossing_ab, crossing_c), backs = slot_compute(
+        [tokens, in_one, in_two],
+        [wide_grad, grad_one, grad_two],
+        lane,
+        part_index,
+        weights,
+        slots * rows,
+        ((0, 0, wide), (1, 0, wide), (2, 0, half), (2, half, wide)),
+        ((0, 2 * rows), (2 * rows, 3 * rows)),
+    )
+    three, far_bc, crossing_ab, crossing_c, *backs = tied(
+        three, far_bc, crossing_ab, crossing_c, *backs
+    )
+    back_a, back_b, back_low, back_high = backs
+
+    far_acts_ab = over_x(crossing_ab)
+    back_two_low = over_z(back_low, apart(2))
+    far_d_low = over_z(far_bc[rows:, :half], apart(1))
+    kept, (crossing_d,), (back_d,) = slot_compute(
+        [three], [], lane, part_index, weights, slots * rows, ((0, 0, wide),), ((0, rows),), kept
+    )
+    acts, hidden_send, hidden_keep, scaled = kept
+    send = outer(scaled, hidden_send).astype(bf)
+    crossing_cd = jnp.concatenate([crossing_c, crossing_d])
+    far_acts_ab, back_two_low, far_d_low, crossing_cd, back_d, back_high, acts, send, scaled = tied(
+        far_acts_ab, back_two_low, far_d_low, crossing_cd, back_d, back_high, acts, send, scaled
+    )
+
+    far_acts_cd = over_x(crossing_cd)
+    back_two_high = over_z(back_high, apart(2))
+    far_d_high = over_z(far_bc[rows:, half:], apart(1))
+    keep = outer(scaled, hidden_keep).astype(bf)
     both = keep.astype(f32) + over_core(send).astype(f32)
     crossing, both = both[:, width:].astype(bf), both[:, :width].astype(bf)
-    far_acts_d, back_two_high, crossing, both, back_b, back_d = tied(
-        far_acts_d, back_two_high, crossing, both, back_b, back_d
-    )
+    rows_first = jnp.concatenate([tokens, in_bc, three[:, :features], far_a, far_bc[:rows]])
+    acts_first = jnp.concatenate([acts, far_acts_ab])
+    first_keep = outer(rows_first, acts_first[:, : 2 * width]).astype(bf)
+    far_acts_cd, back_two_high, far_d_high, crossing, both, back_d, back_b, first_keep = tied(
+        far_acts_cd, back_two_high, far_d_high, crossing, both, back_d, back_b, first_keep
+    )
+    first_send = outer(rows_first, acts_first[:, 2 * width :]).astype(bf)
 
     down_far = over_x(crossing)
     back_three = over_z(back_d, apart(3))
     back_one = over_z(back_b, apart(1))
-    acts = jnp.concatenate([acts_abc, acts_d, far_acts_abc, far_acts_d])
-    every_row = jnp.concatenate([tokens, in_bc, in_d, far_a, far_bc, far_d])
-    send = over_core(outer(every_row, acts[:, 2 * width :]).astype(bf))
-    pair = (outer(every_row, acts[:, : 2 * width]) + send.astype(f32)).astype(bf)
+    back_two = jnp.concatenate([back_two_low, back_two_high], axis=1)
+    rows_last = jnp.concatenate(
+        [far_bc[rows:], jnp.concatenate([far_d_low, far_d_high], axis=1)]
+    )
+    send, keep = (
+        outer(rows_last, far_acts_cd[:, cols]) + first.astype(f32)
+        for cols, first in (
+            (slice(2 * width, None), first_send),
+            (slice(0, 2 * width), first_keep),
+        )
+    )
+    send = send.astype(bf)
+    got = over_core(send)
+    pair = (keep + got.astype(f32)).astype(bf)
     gate_out, up_out = pair[:, :width], pair[:, width:]
     back_one, back_three, down_far, gate_out, up_out = tied(
         back_one, back_three, down_far, gate_out, up_out
     )
-    back_two = jnp.concatenate([back_two_low, back_two_high], axis=1)
     returned = [back_a, back_one, back_two, back_three]
     down = (both.astype(f32) + down_far.astype(f32)).astype(bf)
     token_grad = sum(r[:, :features].astype(f32) for r in returned).astype(bf)

time: 166 us -> 164 us (0.988)
  local copies, waits for them, and re-layouts: 20.6 us -> 11.8 us
  matrix products: 12 us -> 14.8 us
  starting transfers between devices: 26.9 us -> 29.4 us
    unnamed x69 -> x65, local copies, waits for them, and re-layouts: 13.5 us -> 5.2 us
    ppermute x8, waiting for transfers between devices: 27.9 us -> 31 us  [over_x(): return lax.ppermute(value, 'replica', swap_x)]
    dot_general x4 -> x6, matrix products: 12 us -> 14.8 us  [outer(): lax.dot_general(lhs, rhs, (((0,), (0,)), ((), ())), preferred_element_typ...]
    ppermute x10 -> x11, waiting for transfers between devices: 38 us -> 35.4 us  [over_z(): return lax.ppermute(value, 'expert', pairs)]
    ppermute x10 -> x11, starting transfers between devices: 15 us -> 16.7 us  [over_z(): return lax.ppermute(value, 'expert', pairs)]
  transfers between devices with their start and end apart: 30 -> 31, of which waited for: 14 -> 13; matrix products, arithmetic and copies ran while one was open for 15% -> 17% of each run, Pallas kernels for 16% -> 16%
where the time goes in v2:
time: 164 us; the launch traced here: 161 us
  waiting for transfers between devices  68.8 us (42%)
  starting transfers between devices  29.4 us (18%)
  Pallas kernels  26.2 us (16%)
  matrix products  14.8 us (9%)
  local copies, waits for them, and re-layouts  11.8 us (7%)
  other arithmetic  8.95 us (5%)
    ppermute x11, waiting for transfers between devices, over_z(): return lax.ppermute(value, 'expert', pairs)  35.4 us
    ppermute x8, waiting for transfers between devices, over_x(): return lax.ppermute(value, 'replica', swap_x)  31 us
    pallas_call x2, Pallas kernels, slot_compute(): pl.pallas_call(functools.partial(slot_kernel, slots, not grads, bool(kept...  26.2 us
    ppermute x11, starting transfers between devices, over_z(): return lax.ppermute(value, 'expert', pairs)  16.7 us
    dot_general x6, matrix products, outer(): lax.dot_general(lhs, rhs, (((0,), (0,)), ((), ())), preferred_element_typ...  14.8 us
    ppermute x8, starting transfers between devices, over_x(): return lax.ppermute(value, 'replica', swap_x)  9.66 us
    unnamed x65, local copies, waits for them, and re-layouts  5.2 us
  transfers between devices with their start and end apart: 31, of which 13 were waited for; matrix products, arithmetic and copies ran while one was open for 17% of the time, Pallas kernels for 16%

profile of v2, /device:TPU:12, one launch (start us, length us, event | category | flops | bytes accessed | tf_op | source)
XLA Modules:
  0.0 161.1 jit_solution(15084734433570483495)
XLA Ops:
  0.7 2.7 %collective-permute-start = (bf16[128,2048]{1,0:T(8,128)(2,1)}, bf16[128,2048]{1,0:T(8,128)(2,1)S(1)}, u32[]{:S(2)}, u32[]{:S(2)}) collective-permute-start(bf16[128,2048]{1,0:T(8,128)(2,1)} %rest_0_.1), channel_id=1, source_target_pairs={{0,8},{4,12},{8,0},{12,4},{1,9},{5,13},{9,1},{13,5},{2,10},{6,14},... | collective-permute-start | bytes 1572872 | tf_op jit(solution)/shard_map/ppermute | solution.py:335
  3.3 0.4 collective-permute-start.1
  3.8 1.2 dynamic-slice_bitcast_fusion.2
  5.0 1.6 collective-permute-start.2
  6.5 1.1 dynamic-slice_bitcast_fusion.1
  7.6 0.6 collective-permute-start.3
  8.3 1.7 %pad_maximum_fusion = bf16[3,2048,256]{2,1,0:T(8,128)(2,1)S(1)} fusion(bf16[1,2048,256]{2,1,0:T(8,128)(2,1)} %param.13, bf16[1,2048,256]{2,1,0:T(8,128)(2,1)S(1)} %copy-done.9, bf16[1,2048,256]{2,1,0:T(8,128)(2,1)S(1)} %copy-done.8), kind=kLoop, calls=%fused_computation.3 | loop fusion | flops 3145728 | bytes 6291456 | tf_op jit(solution)/shard_map/stack | solution.py:379
  10.0 9.9 %collective-permute-done.2.rest_10_.rest_5_ = bf16[1024,256]{1,0:T(8,128)(2,1)S(1)} collective-permute-done((bf16[1024,256]{1,0:T(8,128)(2,1)S(1)}, bf16[1024,256]{1,0:T(8,128)(2,1)S(1)}, u32[]{:S(2)}, u32[]{:S(2)}) %collective-permute-start.2) | collective-permute-done | bytes 524320 | tf_op jit(solution)/shard_map/ppermute | solution.py:339
  19.9 0.5 collective-permute-start.4
  20.7 8.7 %collective-permute-done.3.rest_11_.rest_6_ = bf16[1024,256]{1,0:T(8,128)(2,1)S(1)} collective-permute-done((bf16[1024,256]{1,0:T(8,128)(2,1)S(1)}, bf16[1024,256]{1,0:T(8,128)(2,1)S(1)}, u32[]{:S(2)}, u32[]{:S(2)}) %collective-permute-start.3) | collective-permute-done | bytes 524320 | tf_op jit(solution)/shard_map/ppermute | solution.py:339
  29.4 0.9 collective-permute-done.4.rest_13_.rest_8_
  30.3 0.4 collective-permute-start.5
  30.7 1.5 collective-permute-start.7
  32.2 1.6 collective-permute-start.6
  33.8 0.5 collective-permute-start.10
  34.3 2.1 %pad_maximum_fusion.2 = bf16[256,2048]{1,0:T(8,128)(2,1)} fusion(bf16[128,2048]{1,0:T(8,128)(2,1)S(1)} %collective-permute-done.rest_2_, bf16[128,2048]{1,0:T(8,128)(2,1)} %copy-done.6), kind=kLoop, calls=%fused_computation.11 | loop fusion | flops 2097152 | bytes 2097152 | tf_op jit(solution)/shard_map/concatenate | solution.py:389
  36.4 8.4 %collective-permute-done.7.rest_12_.rest_7_ = bf16[1024,256]{1,0:T(8,128)(2,1)S(1)} collective-permute-done((bf16[1024,256]{1,0:T(8,128)(2,1)S(1)}, bf16[1024,256]{1,0:T(8,128)(2,1)S(1)}, u32[]{:S(2)}, u32[]{:S(2)}) %collective-permute-start.7) | collective-permute-done | bytes 524320 | tf_op jit(solution)/shard_map/ppermute | solution.py:339
  44.8 0.8 collective-permute-start.11
  45.6 1.2 collective-permute-start.9
  46.8 8.5 %collective-permute-done.5.rest_5_ = bf16[128,2176]{1,0:T(8,128)(2,1)S(1)} collective-permute-done((bf16[128,2176]{1,0:T(8,128)(2,1)S(1)}, bf16[128,2176]{1,0:T(8,128)(2,1)S(1)}, u32[]{:S(2)}, u32[]{:S(2)}) %collective-permute-start.5) | collective-permute-done | bytes 557088 | tf_op jit(solution)/shard_map/ppermute | solution.py:335
  55.3 1.2 pad_maximum_fusion.1
  56.5 1.3 collective-permute-done.6.rest_4_
  57.7 0.8 collective-permute-done.11.rest_15_.rest_10_
  58.6 0.7 copy-done.2
  59.3 0.5 collective-permute-start.16
  59.8 2.5 %collective-permute-start.12 = (bf16[128,4224]{1,0:T(8,128)(2,1)}, bf16[128,4224]{1,0:T(8,128)(2,1)}, u32[]{:S(2)}, u32[]{:S(2)}) collective-permute-start(bf16[128,4224]{1,0:T(8,128)(2,1)} %pad_maximum_fusion.1), channel_id=1, source_target_pairs={{0,4},{4,0},{8,12},{12,8},{1,5},{5,1},{9,13},{13,9},{2,6},{6,2},{1... | collective-permute-start | bytes 3244040 | tf_op jit(solution)/shard_map/ppermute | solution.py:335
  62.4 1.4 collective-permute-start.13
  63.8 0.5 collective-permute-start.18
  64.4 1.1 constant_dynamic-update-slice_fusion.2
  65.5 1.3 constant_dynamic-update-slice_fusion.1
  66.8 0.4 collective-permute-done.18.rest_20_.rest_15_
  67.2 0.2 collective-permute-done.19.rest_21_.rest_16_
  67.4 0.1 copy-done.15
  67.5 0.4 copy-done.16
  68.0 0.2 copy-done.17
  68.2 15.4 %shard_map.110 = (bf16[512,1024]{1,0:T(8,128)(2,1)}, bf16[512,512]{1,0:T(8,128)(2,1)S(1)}, bf16[512,512]{1,0:T(8,128)(2,1)S(1)}, bf16[512,2048]{1,0:T(8,128)(2,1...) custom-call(f32[1,128]{1,0:T(1,128)S(1)} %compare_convert_fusion.lan, ...), custom_call_target="tpu_custom_call" | custom-call | flops 786432 | bytes 1572864 | tf_op jit(solution)/shard_map/pallas_call | solution.py:305
  83.6 4.0 %collective-permute-done.13 = bf16[256,2048]{1,0:T(8,128)(2,1)} collective-permute-done((bf16[256,2048]{1,0:T(8,128)(2,1)}, bf16[256,2048]{1,0:T(8,128)(2,1)}, u32[]{:S(2)}, u32[]{:S(2)}) %collective-permute-start.13) | collective-permute-done | bytes 1048608 | tf_op jit(solution)/shard_map/ppermute | solution.py:339
  87.6 1.1 fusion.17
  88.6 1.0 collective-permute-start.22
  89.7 1.4 collective-permute-start.20
  91.0 1.2 collective-permute-start.21
  92.2 1.1 collective-permute-start.25
  93.3 1.1 slice_dynamic-update-slice_fusion.1
  94.4 10.9 %shard_map.111 = (bf16[512,1024]{1,0:T(8,128)(2,1)}, bf16[512,512]{1,0:T(8,128)(2,1)S(1)}, bf16[512,512]{1,0:T(8,128)(2,1)S(1)}, bf16[512,2048]{1,0:T(8,128)(2,1...) custom-call(f32[1,128]{1,0:T(1,128)S(1)} %compare_convert_fusion.lan, ...), custom_call_target="tpu_custom_call", output_to_operand_aliasing={{0}: (19, {}), {1}: (20, {}), {2}: (21, {}), {3}: (22, {})} | custom-call | flops 262144 | bytes 524288 | tf_op jit(solution)/shard_map/pallas_call | solution.py:305
  105.3 2.9 %convolution_convert_fusion.3 = bf16[2048,512]{1,0:T(8,128)(2,1)S(1)} fusion(bf16[512,2048]{1,0:T(8,128)(2,1)} %get-tuple-element.118, bf16[512,512]{1,0:T(8,128)(2,1)S(1)} %get-tuple-element.115), kind=kOutput, calls=%fused_computation.7 | convolution fusion | flops 1074790400 | bytes 4718592 | tf_op jit(solution)/shard_map/dot_general | solution.py:355
  108.5 1.6 fusion.16
  110.1 0.6 collective-permute-start.23
  110.6 1.9 %collective-permute-start.24 = (bf16[128,1152]{1,0:T(8,128)(2,1)S(1)}, bf16[128,1152]{1,0:T(8,128)(2,1)S(1)}, u32[]{:S(2)}, u32[]{:S(2)}) collective-permute-start(bf16[128,1152]{1,0:T(8,128)(2,1)S(1)} %get-tuple-element.117), channel_id=1, source_target_pairs={{0,8},{4,12},{8,0},{12,4},{1,9},{5,13},{9,1},{13,5},{2,10},{6,14},... | collective-permute-start | bytes 884744 | tf_op jit(solution)/shard_map/ppermute | solution.py:335
  112.6 1.3 convolution_convert_fusion.2
  114.0 1.9 %convolution_convert_fusion = bf16[2048,512]{1,0:T(8,128)(2,1)S(1)} fusion(bf16[768,2048]{1,0:T(8,128)(2,1)S(1)} %get-tuple-element.146, bf16[768,1024]{1,0:T(8,128)(2,1)S(1)} %constant_dynamic-update-slice_fusion.3), kind=kOutput, calls=%fused_computation.4 | convolution fusion | flops 1611661312 | bytes 6029312 | tf_op jit(solution)/shard_map/dot_general | solution.py:355
  115.8 3.2 %convolution_convert_fusion.1 = bf16[2048,512]{1,0:T(8,128)(2,1)} fusion(bf16[768,2048]{1,0:T(8,128)(2,1)S(1)} %get-tuple-element.146, bf16[768,1024]{1,0:T(8,128)(2,1)S(1)} %constant_dynamic-update-slice_fusion.3), kind=kOutput, calls=%fused_computation.5 | convolution fusion | flops 1611661312 | bytes 6029312 | tf_op jit(solution)/shard_map/dot_general | solution.py:355
  119.1 0.6 add_convert_fusion.2
  119.8 5.3 %collective-permute-done.24 = bf16[128,1152]{1,0:T(8,128)(2,1)S(1)} collective-permute-done((bf16[128,1152]{1,0:T(8,128)(2,1)S(1)}, bf16[128,1152]{1,0:T(8,128)(2,1)S(1)}, u32[]{:S(2)}, u32[]{:S(2)}) %collective-permute-start.24) | collective-permute-done | bytes 294944 | tf_op jit(solution)/shard_map/ppermute | solution.py:335
  125.2 2.1 %add_convert_fusion.1 = bf16[2048,512]{1,0:T(8,128)(2,1)} fusion(bf16[2048,512]{1,0:T(8,128)(2,1)S(1)} %convolution_convert_fusion, bf16[128,1024]{1,0:T(8,128)(2,1)S(1)} %collective-permute-done.25, bf16[128,1024]{1,0:T(8,128)(2,1)S(1)} %collective-permute-done.22, bf16[128,2048]{1,0:T(8,128)(2,1)S(1)} %get-tuple-element.145, ...), kind=kOutput, calls=%fused_computation.1 | convolution fusion | flops 543162368 | bytes 5505024 | tf_op jit(solution)/shard_map/dot_general | solution.py:355
  127.4 1.4 collective-permute-start.29
  128.8 2.6 %collective-permute-start.27 = (bf16[128,2176]{1,0:T(8,128)(2,1)}, bf16[128,2176]{1,0:T(8,128)(2,1)S(1)}, u32[]{:S(2)}, u32[]{:S(2)}) collective-permute-start(bf16[128,2176]{1,0:T(8,128)(2,1)} %get-tuple-element.126), channel_id=1, source_target_pairs={{0,4},{4,0},{8,12},{12,8},{1,5},{5,1},{9,13},{13,9},{2,6},{6,2},{1... | collective-permute-start | bytes 1671176 | tf_op jit(solution)/shard_map/ppermute | solution.py:335
  131.5 1.3 collective-permute-start.28
  132.9 3.4 %add_convert_fusion = bf16[2048,512]{1,0:T(8,128)(2,1)S(1)} fusion(bf16[2048,512]{1,0:T(8,128)(2,1)} %collective-permute-done.30, bf16[2048,512]{1,0:T(8,128)(2,1)} %convolution_convert_fusion.1, bf16[128,1024]{1,0:T(8,128)(2,1)} %copy-done.29, bf16[128,1024]{1,0:T(8,128)(2,1)} %copy-done.28, bf16[128,2048]{1,0:T(8,128)(2,1)S(1)} %get-tuple-element.145, ...), kind=kOutput, calls=%fused_computation | convolution fusion | flops 545259520 | bytes 7602176 | tf_op jit(solution)/shard_map/dot_general | solution.py:355
  136.3 1.5 fusion.14
  137.8 7.3 %collective-permute-done.27 = bf16[128,2176]{1,0:T(8,128)(2,1)S(1)} collective-permute-done((bf16[128,2176]{1,0:T(8,128)(2,1)}, bf16[128,2176]{1,0:T(8,128)(2,1)S(1)}, u32[]{:S(2)}, u32[]{:S(2)}) %collective-permute-start.27) | collective-permute-done | bytes 557088 | tf_op jit(solution)/shard_map/ppermute | solution.py:335
  145.1 13.0 %collective-permute-done.28 = bf16[128,2176]{1,0:T(8,128)(2,1)S(1)} collective-permute-done((bf16[128,2176]{1,0:T(8,128)(2,1)}, bf16[128,2176]{1,0:T(8,128)(2,1)S(1)}, u32[]{:S(2)}, u32[]{:S(2)}) %collective-permute-start.28) | collective-permute-done | bytes 557088 | tf_op jit(solution)/shard_map/ppermute | solution.py:335
  158.2 1.1 add_convert_fusion.4
  159.3 1.3 fusion
  160.6 0.5 fusion.11
  (95 shorter events, 1.3 us)
Async XLA Ops:
  0.6 7.6 %copy-start.25 = (s32[128,2]{0,1:T(2,128)S(1)}, s32[128,2]{0,1:T(2,128)}, u32[]{:S(2)}) copy-start(s32[128,2]{0,1:T(2,128)} %param.9) | copy-start | bytes 3076
  0.6 7.6 %copy-start.26 = (bf16[128,2]{0,1:T(2,128)(2,1)S(1)}, bf16[128,2]{0,1:T(2,128)(2,1)}, u32[]{:S(2)}) copy-start(bf16[128,2]{0,1:T(2,128)(2,1)} %param.10) | copy-start | bytes 1540
  0.7 28.7 %collective-permute-start = (bf16[128,2048]{1,0:T(8,128)(2,1)}, bf16[128,2048]{1,0:T(8,128)(2,1)S(1)}, u32[]{:S(2)}, u32[]{:S(2)}) collective-permute-start(bf16[128,2048]{1,0:T(8,128)(2,1)} %rest_0_.1), channel_id=1, source_target_pairs={{0,8},{4,12},{8,0},{12,4},{1,9},{5,13},{9,1},{13,5},{2,10},{6,14},... | collective-permute-start | bytes 1572872 | tf_op jit(solution)/shard_map/ppermute | solution.py:335
  3.3 26.1 %collective-permute-start.1 = (bf16[128,2048]{1,0:T(8,128)(2,1)}, bf16[128,2048]{1,0:T(8,128)(2,1)S(1)}, u32[]{:S(2)}, u32[]{:S(2)}) collective-permute-start(bf16[128,2048]{1,0:T(8,128)(2,1)} %rest_0_.1), channel_id=1, source_target_pairs={{0,4},{4,0},{8,12},{12,8},{1,5},{5,1},{9,13},{13,9},{2,6},{6,2},{1... | collective-permute-start | bytes 1572872 | tf_op jit(solution)/shard_map/ppermute | solution.py:335
  3.8 4.5 %copy-start.8 = (bf16[1,2048,256]{2,1,0:T(8,128)(2,1)S(1)}, bf16[1,2048,256]{2,1,0:T(8,128)(2,1)}, u32[]{:S(2)}) copy-start(bf16[1,2048,256]{2,1,0:T(8,128)(2,1)} %param.11) | copy-start | bytes 3145732
  3.8 4.5 %copy-start.9 = (bf16[1,2048,256]{2,1,0:T(8,128)(2,1)S(1)}, bf16[1,2048,256]{2,1,0:T(8,128)(2,1)}, u32[]{:S(2)}) copy-start(bf16[1,2048,256]{2,1,0:T(8,128)(2,1)} %param.12) | copy-start | bytes 3145732
  5.0 14.9 %collective-permute-start.2 = (bf16[1024,256]{1,0:T(8,128)(2,1)S(1)}, bf16[1024,256]{1,0:T(8,128)(2,1)S(1)}, u32[]{:S(2)}, u32[]{:S(2)}) collective-permute-start(bf16[1024,256]{1,0:T(8,128)(2,1)S(1)} %dynamic-slice_bitcast_fusion.2), channel_id=1, source_target_pairs={{0,2},{1,3},{2,0},{3,1},{4,6},{5,7},{6,4},{7,5},{8,10},{9,11},{10,... | collective-permute-start | bytes 1572872 | tf_op jit(solution)/shard_map/ppermute | solution.py:339
  7.6 21.8 %collective-permute-start.3 = (bf16[1024,256]{1,0:T(8,128)(2,1)S(1)}, bf16[1024,256]{1,0:T(8,128)(2,1)S(1)}, u32[]{:S(2)}, u32[]{:S(2)}) collective-permute-start(bf16[1024,256]{1,0:T(8,128)(2,1)S(1)} %dynamic-slice_bitcast_fusion.1), channel_id=1, source_target_pairs={{0,2},{1,3},{2,0},{3,1},{4,6},{5,7},{6,4},{7,5},{8,10},{9,11},{10,... | collective-permute-start | bytes 1572872 | tf_op jit(solution)/shard_map/ppermute | solution.py:339
  8.3 12.3 %copy-start.10 = (bf16[1,2048,256]{2,1,0:T(8,128)(2,1)S(1)}, bf16[1,2048,256]{2,1,0:T(8,128)(2,1)}, u32[]{:S(2)}) copy-start(bf16[1,2048,256]{2,1,0:T(8,128)(2,1)} %param.13) | copy-start | bytes 3145732
  8.3 12.4 %copy-start.20 = (bf16[128,2048]{1,0:T(8,128)(2,1)S(1)}, bf16[128,2048]{1,0:T(8,128)(2,1)}, u32[]{:S(2)}) copy-start(bf16[128,2048]{1,0:T(8,128)(2,1)} %param.8) | copy-start | bytes 1572868
  19.9 10.4 %collective-permute-start.4 = (bf16[1024,256]{1,0:T(8,128)(2,1)S(1)}, bf16[1024,256]{1,0:T(8,128)(2,1)S(1)}, u32[]{:S(2)}, u32[]{:S(2)}) collective-permute-start(bf16[1024,256]{1,0:T(8,128)(2,1)S(1)} %collective-permute-done.2.rest_10_.rest_5_), channel_id=1, source_target_pairs={{0,16},{16,0},{1,17},{17,1},{2,18},{18,2},{3,19},{19,3},{4,20},{20... | collective-permute-start | bytes 1572872 | tf_op jit(solution)/shard_map/ppermute | solution.py:347
  20.6 25.0 %copy-start.4 = (bf16[128,2048]{1,0:T(8,128)(2,1)S(1)}, bf16[128,2048]{1,0:T(8,128)(2,1)}, u32[]{:S(2)}) copy-start(bf16[128,2048]{1,0:T(8,128)(2,1)} %rest_0_.1) | copy-start | bytes 1572868
  20.7 38.6 %copy-start.12 = (bf16[128,2176]{1,0:T(8,128)(2,1)}, bf16[128,2176]{1,0:T(8,128)(2,1)S(1)}, u32[]{:S(2)}) copy-start(bf16[128,2176]{1,0:T(8,128)(2,1)S(1)} %pad_maximum_fusion.3.rest_3_) | copy-start | bytes 1671172
  29.4 0.9 copy-start.6
  30.3 14.5 %collective-permute-start.8 = (bf16[3,2048,256]{2,1,0:T(8,128)(2,1)S(1)}, bf16[3,2048,256]{2,1,0:T(8,128)(2,1)}, u32[]{:S(2)}, u32[]{:S(2)}) collective-permute-start(bf16[3,2048,256]{2,1,0:T(8,128)(2,1)S(1)} %pad_maximum_fusion), channel_id=1, source_target_pairs={{0,1},{1,0},{2,3},{3,2},{4,5},{5,4},{6,7},{7,6},{8,9},{9,8},{10,11... | collective-permute-start | bytes 9437192 | tf_op jit(solution)/shard_map/ppermute | solution.py:343
  30.3 24.9 %collective-permute-start.5 = (bf16[128,2176]{1,0:T(8,128)(2,1)S(1)}, bf16[128,2176]{1,0:T(8,128)(2,1)S(1)}, u32[]{:S(2)}, u32[]{:S(2)}) collective-permute-start(bf16[128,2176]{1,0:T(8,128)(2,1)S(1)} %pad_maximum_fusion.3.rest_3_), channel_id=1, source_target_pairs={{0,8},{4,12},{8,0},{12,4},{1,9},{5,13},{9,1},{13,5},{2,10},{6,14},... | collective-permute-start | bytes 1671176 | tf_op jit(solution)/shard_map/ppermute | solution.py:335
  30.7 14.1 %collective-permute-start.7 = (bf16[1024,256]{1,0:T(8,128)(2,1)S(1)}, bf16[1024,256]{1,0:T(8,128)(2,1)S(1)}, u32[]{:S(2)}, u32[]{:S(2)}) collective-permute-start(bf16[1024,256]{1,0:T(8,128)(2,1)S(1)} %dynamic-slice_bitcast_fusion), channel_id=1, source_target_pairs={{0,2},{1,3},{2,0},{3,1},{4,6},{5,7},{6,4},{7,5},{8,10},{9,11},{10,... | collective-permute-start | bytes 1572872 | tf_op jit(solution)/shard_map/ppermute | solution.py:339
  32.2 25.5 %collective-permute-start.6 = (bf16[128,2176]{1,0:T(8,128)(2,1)S(1)}, bf16[128,2176]{1,0:T(8,128)(2,1)S(1)}, u32[]{:S(2)}, u32[]{:S(2)}) collective-permute-start(bf16[128,2176]{1,0:T(8,128)(2,1)S(1)} %pad_maximum_fusion.3.rest_3_), channel_id=1, source_target_pairs={{0,4},{4,0},{8,12},{12,8},{1,5},{5,1},{9,13},{13,9},{2,6},{6,2},{1... | collective-permute-start | bytes 1671176 | tf_op jit(solution)/shard_map/ppermute | solution.py:335
  33.8 22.7 %collective-permute-start.10 = (bf16[1024,256]{1,0:T(8,128)(2,1)S(1)}, bf16[1024,256]{1,0:T(8,128)(2,1)S(1)}, u32[]{:S(2)}, u32[]{:S(2)}) collective-permute-start(bf16[1024,256]{1,0:T(8,128)(2,1)S(1)} %collective-permute-done.3.rest_11_.rest_6_), channel_id=1, source_target_pairs={{0,16},{16,0},{1,17},{17,1},{2,18},{18,2},{3,19},{19,3},{4,20},{20... | collective-permute-start | bytes 1572872 | tf_op jit(solution)/shard_map/ppermute | solution.py:347
  44.8 13.7 %collective-permute-start.11 = (bf16[1024,256]{1,0:T(8,128)(2,1)S(1)}, bf16[1024,256]{1,0:T(8,128)(2,1)S(1)}, u32[]{:S(2)}, u32[]{:S(2)}) collective-permute-start(bf16[1024,256]{1,0:T(8,128)(2,1)S(1)} %collective-permute-done.7.rest_12_.rest_7_), channel_id=1, source_target_pairs={{0,16},{16,0},{1,17},{17,1},{2,18},{18,2},{3,19},{19,3},{4,20},{20... | collective-permute-start | bytes 1572872 | tf_op jit(solution)/shard_map/ppermute | solution.py:347
  45.6 13.0 %collective-permute-start.9 = (bf16[128,2048]{1,0:T(8,128)(2,1)S(1)}, bf16[128,2048]{1,0:T(8,128)(2,1)S(1)}, u32[]{:S(2)}, u32[]{:S(2)}) collective-permute-start(bf16[128,2048]{1,0:T(8,128)(2,1)S(1)} %copy-done.4), channel_id=1, source_target_pairs={{0,2},{1,3},{2,0},{3,1},{4,6},{5,7},{6,4},{7,5},{8,10},{9,11},{10,... | collective-permute-start | bytes 1572872 | tf_op jit(solution)/shard_map/ppermute | solution.py:339
  55.3 4.6 %copy-start.13 = (bf16[128,2176]{1,0:T(8,128)(2,1)}, bf16[128,2176]{1,0:T(8,128)(2,1)S(1)}, u32[]{:S(2)}) copy-start(bf16[128,2176]{1,0:T(8,128)(2,1)S(1)} %collective-permute-done.5.rest_5_) | copy-start | bytes 1671172
  56.5 10.9 %copy-start = (bf16[1024,256]{1,0:T(8,128)(2,1)}, bf16[1024,256]{1,0:T(8,128)(2,1)S(1)}, u32[]{:S(2)}) copy-start(bf16[1024,256]{1,0:T(8,128)(2,1)S(1)} %collective-permute-done.10.rest_14_.rest_9_) | copy-start | bytes 1572868
  57.7 4.6 %copy-start.18 = (bf16[128,2176]{1,0:T(8,128)(2,1)}, bf16[128,2176]{1,0:T(8,128)(2,1)S(1)}, u32[]{:S(2)}) copy-start(bf16[128,2176]{1,0:T(8,128)(2,1)S(1)} %collective-permute-done.6.rest_4_) | copy-start | bytes 1671172
  58.5 0.8 copy-start.2
  58.5 3.8 %copy-start.21 = (bf16[128,2048]{1,0:T(8,128)(2,1)}, bf16[128,2048]{1,0:T(8,128)(2,1)S(1)}, u32[]{:S(2)}) copy-start(bf16[128,2048]{1,0:T(8,128)(2,1)S(1)} %collective-permute-done.9) | copy-start | bytes 1572868
  58.5 5.2 %collective-permute-start.14 = (bf16[1024,256]{1,0:T(8,128)(2,1)S(1)}, bf16[1024,256]{1,0:T(8,128)(2,1)}, u32[]{:S(2)}, u32[]{:S(2)}) collective-permute-start(bf16[1024,256]{1,0:T(8,128)(2,1)S(1)} %collective-permute-done.2.rest_10_.rest_5_), channel_id=1, source_target_pairs={{0,1},{1,0},{2,3},{3,2},{4,5},{5,4},{6,7},{7,6},{8,9},{9,8},{10,11... | collective-permute-start | bytes 1572872 | tf_op jit(solution)/shard_map/ppermute | solution.py:343
  59.3 4.5 %collective-permute-start.15 = (bf16[1024,256]{1,0:T(8,128)(2,1)S(1)}, bf16[1024,256]{1,0:T(8,128)(2,1)}, u32[]{:S(2)}, u32[]{:S(2)}) collective-permute-start(bf16[1024,256]{1,0:T(8,128)(2,1)S(1)} %collective-permute-done.3.rest_11_.rest_6_), channel_id=1, source_target_pairs={{0,1},{1,0},{2,3},{3,2},{4,5},{5,4},{6,7},{7,6},{8,9},{9,8},{10,11... | collective-permute-start | bytes 1572872 | tf_op jit(solution)/shard_map/ppermute | solution.py:343
  59.3 5.0 %collective-permute-start.16 = (bf16[1024,256]{1,0:T(8,128)(2,1)S(1)}, bf16[1024,256]{1,0:T(8,128)(2,1)}, u32[]{:S(2)}, u32[]{:S(2)}) collective-permute-start(bf16[1024,256]{1,0:T(8,128)(2,1)S(1)} %collective-permute-done.7.rest_12_.rest_7_), channel_id=1, source_target_pairs={{0,1},{1,0},{2,3},{3,2},{4,5},{5,4},{6,7},{7,6},{8,9},{9,8},{10,11... | collective-permute-start | bytes 1572872 | tf_op jit(solution)/shard_map/ppermute | solution.py:343
  59.8 27.7 %collective-permute-start.12 = (bf16[128,4224]{1,0:T(8,128)(2,1)}, bf16[128,4224]{1,0:T(8,128)(2,1)}, u32[]{:S(2)}, u32[]{:S(2)}) collective-permute-start(bf16[128,4224]{1,0:T(8,128)(2,1)} %pad_maximum_fusion.1), channel_id=1, source_target_pairs={{0,4},{4,0},{8,12},{12,8},{1,5},{5,1},{9,13},{13,9},{2,6},{6,2},{1... | collective-permute-start | bytes 3244040 | tf_op jit(solution)/shard_map/ppermute | solution.py:335
  62.4 25.2 %collective-permute-start.13 = (bf16[256,2048]{1,0:T(8,128)(2,1)}, bf16[256,2048]{1,0:T(8,128)(2,1)}, u32[]{:S(2)}, u32[]{:S(2)}) collective-permute-start(bf16[256,2048]{1,0:T(8,128)(2,1)} %pad_maximum_fusion.2), channel_id=1, source_target_pairs={{0,2},{1,3},{2,0},{3,1},{4,6},{5,7},{6,4},{7,5},{8,10},{9,11},{10,... | collective-permute-start | bytes 3145736 | tf_op jit(solution)/shard_map/ppermute | solution.py:339
  63.8 4.4 %copy-start.5 = (bf16[128,2048]{1,0:T(8,128)(2,1)S(1)}, bf16[128,2048]{1,0:T(8,128)(2,1)}, u32[]{:S(2)}) copy-start(bf16[128,2048]{1,0:T(8,128)(2,1)} %rest_0_.1) | copy-start | bytes 1572868
  63.8 4.4 %copy-start.7 = (bf16[128,2048]{1,0:T(8,128)(2,1)S(1)}, bf16[128,2048]{1,0:T(8,128)(2,1)}, u32[]{:S(2)}) copy-start(bf16[128,2048]{1,0:T(8,128)(2,1)} %copy-done.6) | copy-start | bytes 1572868
  63.8 3.0 %collective-permute-start.17 = (bf16[1024,256]{1,0:T(8,128)(2,1)S(1)}, bf16[1024,256]{1,0:T(8,128)(2,1)S(1)}, u32[]{:S(2)}, u32[]{:S(2)}) collective-permute-start(bf16[1024,256]{1,0:T(8,128)(2,1)S(1)} %collective-permute-done.4.rest_13_.rest_8_), channel_id=1, source_target_pairs={{0,1},{1,0},{2,3},{3,2},{4,5},{5,4},{6,7},{7,6},{8,9},{9,8},{10,11... | collective-permute-start | bytes 1572872 | tf_op jit(solution)/shard_map/ppermute | solution.py:343
  63.8 3.4 %collective-permute-start.18 = (bf16[1024,256]{1,0:T(8,128)(2,1)S(1)}, bf16[1024,256]{1,0:T(8,128)(2,1)S(1)}, u32[]{:S(2)}, u32[]{:S(2)}) collective-permute-start(bf16[1024,256]{1,0:T(8,128)(2,1)S(1)} %collective-permute-done.10.rest_14_.rest_9_), channel_id=1, source_target_pairs={{0,1},{1,0},{2,3},{3,2},{4,5},{5,4},{6,7},{7,6},{8,9},{9,8},{10,11... | collective-permute-start | bytes 1572872 | tf_op jit(solution)/shard_map/ppermute | solution.py:343
  64.3 3.1 %collective-permute-start.19 = (bf16[1024,256]{1,0:T(8,128)(2,1)}, bf16[1024,256]{1,0:T(8,128)(2,1)S(1)}, u32[]{:S(2)}, u32[]{:S(2)}) collective-permute-start(bf16[1024,256]{1,0:T(8,128)(2,1)} %copy-done.2), channel_id=1, source_target_pairs={{0,1},{1,0},{2,3},{3,2},{4,5},{5,4},{6,7},{7,6},{8,9},{9,8},{10,11... | collective-permute-start | bytes 1572872 | tf_op jit(solution)/shard_map/ppermute | solution.py:343
  66.8 0.8 copy-start.15
  67.2 0.8 copy-start.16
  67.4 0.8 copy-start.17
  83.6 10.8 %copy-start.1 = (bf16[1024,256]{1,0:T(8,128)(2,1)S(1)}, bf16[1024,256]{1,0:T(8,128)(2,1)}, u32[]{:S(2)}) copy-start(bf16[1024,256]{1,0:T(8,128)(2,1)} %copy-done) | copy-start | bytes 1572868
  83.6 10.8 %copy-start.3 = (bf16[1024,256]{1,0:T(8,128)(2,1)S(1)}, bf16[1024,256]{1,0:T(8,128)(2,1)}, u32[]{:S(2)}) copy-start(bf16[1024,256]{1,0:T(8,128)(2,1)} %copy-done.2) | copy-start | bytes 1572868
  88.6 19.7 %collective-permute-start.22 = (bf16[128,1024]{1,0:T(8,128)(2,1)S(1)}, bf16[128,1024]{1,0:T(8,128)(2,1)S(1)}, u32[]{:S(2)}, u32[]{:S(2)}) collective-permute-start(bf16[128,1024]{1,0:T(8,128)(2,1)S(1)} %get-tuple-element.148), channel_id=1, source_target_pairs={{0,4},{4,0},{8,12},{12,8},{1,5},{5,1},{9,13},{13,9},{2,6},{6,2},{1... | collective-permute-start | bytes 786440 | tf_op jit(solution)/shard_map/ppermute | solution.py:335
  89.7 18.7 %collective-permute-start.20 = (bf16[256,1024]{1,0:T(8,128)(2,1)S(1)}, bf16[256,1024]{1,0:T(8,128)(2,1)S(1)}, u32[]{:S(2)}, u32[]{:S(2)}) collective-permute-start(bf16[256,1024]{1,0:T(8,128)(2,1)S(1)} %get-tuple-element.101), channel_id=1, source_target_pairs={{0,2},{1,3},{2,0},{3,1},{4,6},{5,7},{6,4},{7,5},{8,10},{9,11},{10,... | collective-permute-start | bytes 1572872 | tf_op jit(solution)/shard_map/ppermute | solution.py:339
  91.0 17.3 %collective-permute-start.21 = (bf16[128,1024]{1,0:T(8,128)(2,1)S(1)}, bf16[128,1024]{1,0:T(8,128)(2,1)S(1)}, u32[]{:S(2)}, u32[]{:S(2)}) collective-permute-start(bf16[128,1024]{1,0:T(8,128)(2,1)S(1)} %get-tuple-element.102), channel_id=1, source_target_pairs={{0,8},{4,12},{8,0},{12,4},{1,9},{5,13},{9,1},{13,5},{2,10},{6,14},... | collective-permute-start | bytes 786440 | tf_op jit(solution)/shard_map/ppermute | solution.py:335
  92.2 27.6 %collective-permute-start.25 = (bf16[128,1024]{1,0:T(8,128)(2,1)S(1)}, bf16[128,1024]{1,0:T(8,128)(2,1)S(1)}, u32[]{:S(2)}, u32[]{:S(2)}) collective-permute-start(bf16[128,1024]{1,0:T(8,128)(2,1)S(1)} %get-tuple-element.147), channel_id=1, source_target_pairs={{0,4},{4,0},{8,12},{12,8},{1,5},{5,1},{9,13},{13,9},{2,6},{6,2},{1... | collective-permute-start | bytes 786440 | tf_op jit(solution)/shard_map/ppermute | solution.py:335
  105.3 3.1 %copy-start.22 = (bf16[128,2048]{1,0:T(8,128)(2,1)S(1)}, bf16[128,2048]{1,0:T(8,128)(2,1)}, u32[]{:S(2)}) copy-start(bf16[128,2048]{1,0:T(8,128)(2,1)} %copy-done.21) | copy-start | bytes 1572868
  108.3 4.2 %copy-start.11 = (bf16[512,1024]{1,0:T(8,128)(2,1)S(1)}, bf16[512,1024]{1,0:T(8,128)(2,1)}, u32[]{:S(2)}) copy-start(bf16[512,1024]{1,0:T(8,128)(2,1)} %get-tuple-element.124) | copy-start | bytes 3145732
  108.3 16.9 %copy-start.28 = (bf16[128,1024]{1,0:T(8,128)(2,1)}, bf16[128,1024]{1,0:T(8,128)(2,1)S(1)}, u32[]{:S(2)}) copy-start(bf16[128,1024]{1,0:T(8,128)(2,1)S(1)} %collective-permute-done.22) | copy-start | bytes 786436
  108.3 4.3 %copy-start.23 = (bf16[128,1024]{1,0:T(8,128)(2,1)}, bf16[128,1024]{1,0:T(8,128)(2,1)S(1)}, u32[]{:S(2)}) copy-start(bf16[128,1024]{1,0:T(8,128)(2,1)S(1)} %collective-permute-done.21) | copy-start | bytes 786436
  108.3 10.7 %collective-permute-start.26 = (bf16[2048,512]{1,0:T(8,128)(2,1)S(1)}, bf16[2048,512]{1,0:T(8,128)(2,1)S(1)}, u32[]{:S(2)}, u32[]{:S(2)}) collective-permute-start(bf16[2048,512]{1,0:T(8,128)(2,1)S(1)} %convolution_convert_fusion.3), channel_id=1, source_target_pairs={{0,1},{1,0},{2,3},{3,2},{4,5},{5,4},{6,7},{7,6},{8,9},{9,8},{10,11... | collective-permute-start | bytes 6291464 | tf_op jit(solution)/shard_map/ppermute | solution.py:343
  110.0 2.6 %copy-start.14 = (bf16[512,2048]{1,0:T(8,128)(2,1)S(1)}, bf16[512,2048]{1,0:T(8,128)(2,1)}, u32[]{:S(2)}) copy-start(bf16[512,2048]{1,0:T(8,128)(2,1)} %get-tuple-element.118) | copy-start | bytes 6291460
  110.1 15.1 %collective-permute-start.23 = (bf16[256,1024]{1,0:T(8,128)(2,1)S(1)}, bf16[256,1024]{1,0:T(8,128)(2,1)S(1)}, u32[]{:S(2)}, u32[]{:S(2)}) collective-permute-start(bf16[256,1024]{1,0:T(8,128)(2,1)S(1)} %pad_maximum_fusion.5), channel_id=1, source_target_pairs={{0,2},{1,3},{2,0},{3,1},{4,6},{5,7},{6,4},{7,5},{8,10},{9,11},{10,... | collective-permute-start | bytes 1572872 | tf_op jit(solution)/shard_map/ppermute | solution.py:339
  110.6 14.5 %collective-permute-start.24 = (bf16[128,1152]{1,0:T(8,128)(2,1)S(1)}, bf16[128,1152]{1,0:T(8,128)(2,1)S(1)}, u32[]{:S(2)}, u32[]{:S(2)}) collective-permute-start(bf16[128,1152]{1,0:T(8,128)(2,1)S(1)} %get-tuple-element.117), channel_id=1, source_target_pairs={{0,8},{4,12},{8,0},{12,4},{1,9},{5,13},{9,1},{13,5},{2,10},{6,14},... | collective-permute-start | bytes 884744 | tf_op jit(solution)/shard_map/ppermute | solution.py:335
  119.8 7.5 %copy-start.29 = (bf16[128,1024]{1,0:T(8,128)(2,1)}, bf16[128,1024]{1,0:T(8,128)(2,1)S(1)}, u32[]{:S(2)}) copy-start(bf16[128,1024]{1,0:T(8,128)(2,1)S(1)} %collective-permute-done.25) | copy-start | bytes 786436
  125.2 2.1 %copy-start.27 = (bf16[256,1024]{1,0:T(8,128)(2,1)}, bf16[256,1024]{1,0:T(8,128)(2,1)S(1)}, u32[]{:S(2)}) copy-start(bf16[256,1024]{1,0:T(8,128)(2,1)S(1)} %collective-permute-done.23) | copy-start | bytes 1572868
  125.2 2.1 %copy-start.19 = (bf16[128,2176]{1,0:T(8,128)(2,1)S(1)}, bf16[128,2176]{1,0:T(8,128)(2,1)}, u32[]{:S(2)}) copy-start(bf16[128,2176]{1,0:T(8,128)(2,1)} %get-tuple-element.100) | copy-start | bytes 1671172
  127.3 5.6 %collective-permute-start.30 = (bf16[2048,512]{1,0:T(8,128)(2,1)}, bf16[2048,512]{1,0:T(8,128)(2,1)}, u32[]{:S(2)}, u32[]{:S(2)}) collective-permute-start(bf16[2048,512]{1,0:T(8,128)(2,1)} %add_convert_fusion.1), channel_id=1, source_target_pairs={{0,1},{1,0},{2,3},{3,2},{4,5},{5,4},{6,7},{7,6},{8,9},{9,8},{10,11... | collective-permute-start | bytes 6291464 | tf_op jit(solution)/shard_map/ppermute | solution.py:343
  127.4 30.7 %collective-permute-start.29 = (bf16[2048,256]{1,0:T(8,128)(2,1)S(1)}, bf16[2048,256]{1,0:T(8,128)(2,1)S(1)}, u32[]{:S(2)}, u32[]{:S(2)}) collective-permute-start(bf16[2048,256]{1,0:T(8,128)(2,1)S(1)} %get-tuple-element.128), channel_id=1, source_target_pairs={{0,2},{1,3},{2,0},{3,1},{4,6},{5,7},{6,4},{7,5},{8,10},{9,11},{10,... | collective-permute-start | bytes 3145736 | tf_op jit(solution)/shard_map/ppermute | solution.py:339
  128.8 16.2 %collective-permute-start.27 = (bf16[128,2176]{1,0:T(8,128)(2,1)}, bf16[128,2176]{1,0:T(8,128)(2,1)S(1)}, u32[]{:S(2)}, u32[]{:S(2)}) collective-permute-start(bf16[128,2176]{1,0:T(8,128)(2,1)} %get-tuple-element.126), channel_id=1, source_target_pairs={{0,4},{4,0},{8,12},{12,8},{1,5},{5,1},{9,13},{13,9},{2,6},{6,2},{1... | collective-permute-start | bytes 1671176 | tf_op jit(solution)/shard_map/ppermute | solution.py:335
  131.5 26.6 %collective-permute-start.28 = (bf16[128,2176]{1,0:T(8,128)(2,1)}, bf16[128,2176]{1,0:T(8,128)(2,1)S(1)}, u32[]{:S(2)}, u32[]{:S(2)}) collective-permute-start(bf16[128,2176]{1,0:T(8,128)(2,1)} %get-tuple-element.127), channel_id=1, source_target_pairs={{0,12},{4,8},{8,4},{12,0},{1,13},{5,9},{9,5},{13,1},{2,14},{6,10},... | collective-permute-start | bytes 1671176 | tf_op jit(solution)/shard_map/ppermute | solution.py:335
  136.3 21.9 %copy-start.24 = (bf16[128,1024]{1,0:T(8,128)(2,1)S(1)}, bf16[128,1024]{1,0:T(8,128)(2,1)}, u32[]{:S(2)}) copy-start(bf16[128,1024]{1,0:T(8,128)(2,1)} %copy-done.23) | copy-start | bytes 786436

commit v3 on v2

--- a/solution.py
+++ b/solution.py
@@ -395,23 +395,21 @@
     three = over_z(two, apart(1))
     far_bc = over_x(in_bc)
     weights = [*own, near, *far_weights, *[over_core(w) for w in far_weights]]
-    slots, wide = 4, features + 128
-    kept, (crossing_ab, crossing_c), backs = slot_compute(
+    slots, wide, cut = 4, features + 128, features * 5 // 8
+    kept, (crossing_abc,), backs = slot_compute(
         [tokens, in_one, in_two],
         [wide_grad, grad_one, grad_two],
         lane,
         part_index,
         weights,
         slots * rows,
-        ((0, 0, wide), (1, 0, wide), (2, 0, half), (2, half, wide)),
-        ((0, 2 * rows), (2 * rows, 3 * rows)),
-    )
-    three, far_bc, crossing_ab, crossing_c, *backs = tied(
-        three, far_bc, crossing_ab, crossing_c, *backs
-    )
+        ((0, 0, wide), (1, 0, wide), (2, 0, cut), (2, cut, wide)),
+        ((0, 3 * rows),),
+    )
+    three, far_bc, crossing_abc, *backs = tied(three, far_bc, crossing_abc, *backs)
     back_a, back_b, back_low, back_high = backs
 
-    far_acts_ab = over_x(crossing_ab)
+    far_acts_abc = over_x(crossing_abc)
     back_two_low = over_z(back_low, apart(2))
     far_d_low = over_z(far_bc[rows:, :half], apart(1))
     kept, (crossing_d,), (back_d,) = slot_compute(
@@ -419,22 +417,21 @@
     )
     acts, hidden_send, hidden_keep, scaled = kept
     send = outer(scaled, hidden_send).astype(bf)
-    crossing_cd = jnp.concatenate([crossing_c, crossing_d])
-    far_acts_ab, back_two_low, far_d_low, crossing_cd, back_d, back_high, acts, send, scaled = tied(
-        far_acts_ab, back_two_low, far_d_low, crossing_cd, back_d, back_high, acts, send, scaled
-    )
-
-    far_acts_cd = over_x(crossing_cd)
+    far_acts_abc, back_two_low, far_d_low, crossing_d, back_d, back_high, acts, send, scaled = tied(
+        far_acts_abc, back_two_low, far_d_low, crossing_d, back_d, back_high, acts, send, scaled
+    )
+
+    far_acts_d = over_x(crossing_d)
     back_two_high = over_z(back_high, apart(2))
     far_d_high = over_z(far_bc[rows:, half:], apart(1))
     keep = outer(scaled, hidden_keep).astype(bf)
     both = keep.astype(f32) + over_core(send).astype(f32)
     crossing, both = both[:, width:].astype(bf), both[:, :width].astype(bf)
     rows_first = jnp.concatenate([tokens, in_bc, three[:, :features], far_a, far_bc[:rows]])
-    acts_first = jnp.concatenate([acts, far_acts_ab])
+    acts_first = jnp.concatenate([acts, far_acts_abc[: 2 * rows]])
     first_keep = outer(rows_first, acts_first[:, : 2 * width]).astype(bf)
-    far_acts_cd, back_two_high, far_d_high, crossing, both, back_d, back_b, first_keep = tied(
-        far_acts_cd, back_two_high, far_d_high, crossing, both, back_d, back_b, first_keep
+    far_acts_d, back_two_high, far_d_high, crossing, both, back_d, back_b, first_keep = tied(
+        far_acts_d, back_two_high, far_d_high, crossing, both, back_d, back_b, first_keep
     )
     first_send = outer(rows_first, acts_first[:, 2 * width :]).astype(bf)
 
@@ -445,8 +442,9 @@
     rows_last = jnp.concatenate(
         [far_bc[rows:], jnp.concatenate([far_d_low, far_d_high], axis=1)]
     )
+    acts_last = jnp.concatenate([far_acts_abc[2 * rows :], far_acts_d])
     send, keep = (
-        outer(rows_last, far_acts_cd[:, cols]) + first.astype(f32)
+        outer(rows_last, acts_last[:, cols]) + first.astype(f32)
         for cols, first in (
             (slice(2 * width, None), first_send),
             (slice(0, 2 * width), first_keep),

time: 164 us -> 163 us (level)
  waiting for transfers between devices: 68.8 us -> 64.4 us
  other arithmetic: 8.95 us -> 13 us
  local copies, waits for them, and re-layouts: 11.8 us -> 15.6 us
  matrix products: 14.8 us -> 12.1 us
    ppermute x8, waiting for transfers between devices: 31 us -> 23.6 us  [over_x(): return lax.ppermute(value, 'replica', swap_x)]
    unnamed x65 -> x74, local copies, waits for them, and re-layouts: 5.2 us -> 8.17 us
    dot_general x6, matrix products: 14.8 us -> 12.1 us  [outer(): lax.dot_general(lhs, rhs, (((0,), (0,)), ((), ())), preferred_element_typ...]
    convert_element_type x0 -> x1, other arithmetic: none -> 2.48 us  [fast_body(): pair = (keep + got.astype(f32)).astype(bf)]
  transfers between devices with their start and end apart: 31 -> 31, of which waited for: 13 -> 17; matrix products, arithmetic and copies ran while one was open for 17% -> 19% of each run, Pallas kernels for 16% -> 16%
where the time goes in v3:
time: 163 us; the launch traced here: 161 us
  waiting for transfers between devices  64.4 us (40%)
  starting transfers between devices  28.5 us (17%)
  Pallas kernels  26.2 us (16%)
  local copies, waits for them, and re-layouts  15.6 us (10%)
  other arithmetic  13 us (8%)
  matrix products  12.1 us (7%)
    ppermute x11, waiting for transfers between devices, over_z(): return lax.ppermute(value, 'expert', pairs)  36.4 us
    pallas_call x2, Pallas kernels, slot_compute(): pl.pallas_call(functools.partial(slot_kernel, slots, not grads, bool(kept...  26.2 us
    ppermute x8, waiting for transfers between devices, over_x(): return lax.ppermute(value, 'replica', swap_x)  23.6 us
    ppermute x11, starting transfers between devices, over_z(): return lax.ppermute(value, 'expert', pairs)  15.2 us
    dot_general x6, matrix products, outer(): lax.dot_general(lhs, rhs, (((0,), (0,)), ((), ())), preferred_element_typ...  12.1 us
    ppermute x8, starting transfers between devices, over_x(): return lax.ppermute(value, 'replica', swap_x)  10.6 us
    unnamed x74, local copies, waits for them, and re-layouts  8.17 us
  transfers between devices with their start and end apart: 31, of which 17 were waited for; matrix products, arithmetic and copies ran while one was open for 19% of the time, Pallas kernels for 16%

profile of v3, /device:TPU:12, one launch (start us, length us, event | category | flops | bytes accessed | tf_op | source)
XLA Modules:
  0.0 160.9 jit_solution(11091110437590351232)
XLA Ops:
  0.7 2.7 %collective-permute-start = (bf16[128,2048]{1,0:T(8,128)(2,1)}, bf16[128,2048]{1,0:T(8,128)(2,1)S(1)}, u32[]{:S(2)}, u32[]{:S(2)}) collective-permute-start(bf16[128,2048]{1,0:T(8,128)(2,1)} %rest_0_.1), channel_id=1, source_target_pairs={{0,8},{4,12},{8,0},{12,4},{1,9},{5,13},{9,1},{13,5},{2,10},{6,14},... | collective-permute-start | bytes 1572872 | tf_op jit(solution)/shard_map/ppermute | solution.py:335
  3.8 1.2 dynamic-slice_bitcast_fusion.2
  5.0 1.6 collective-permute-start.2
  6.5 1.1 dynamic-slice_bitcast_fusion.1
  7.6 0.6 collective-permute-start.3
  8.3 1.7 %pad_maximum_fusion = bf16[3,2048,256]{2,1,0:T(8,128)(2,1)S(1)} fusion(bf16[1,2048,256]{2,1,0:T(8,128)(2,1)} %param.13, bf16[1,2048,256]{2,1,0:T(8,128)(2,1)S(1)} %copy-done.11, bf16[1,2048,256]{2,1,0:T(8,128)(2,1)S(1)} %copy-done.10), kind=kLoop, calls=%fused_computation.3 | loop fusion | flops 3145728 | bytes 6291456 | tf_op jit(solution)/shard_map/stack | solution.py:379
  10.0 9.9 %collective-permute-done.2.rest_10_.rest_5_ = bf16[1024,256]{1,0:T(8,128)(2,1)S(1)} collective-permute-done((bf16[1024,256]{1,0:T(8,128)(2,1)S(1)}, bf16[1024,256]{1,0:T(8,128)(2,1)S(1)}, u32[]{:S(2)}, u32[]{:S(2)}) %collective-permute-start.2) | collective-permute-done | bytes 524320 | tf_op jit(solution)/shard_map/ppermute | solution.py:339
  20.7 5.2 %collective-permute-done.rest_2_ = bf16[128,2048]{1,0:T(8,128)(2,1)S(1)} collective-permute-done((bf16[128,2048]{1,0:T(8,128)(2,1)}, bf16[128,2048]{1,0:T(8,128)(2,1)S(1)}, u32[]{:S(2)}, u32[]{:S(2)}) %collective-permute-start) | collective-permute-done | bytes 524320 | tf_op jit(solution)/shard_map/ppermute | solution.py:335
  25.9 1.0 collective-permute-done.1.rest_1_
  26.9 2.5 %collective-permute-done.3.rest_11_.rest_6_ = bf16[1024,256]{1,0:T(8,128)(2,1)S(1)} collective-permute-done((bf16[1024,256]{1,0:T(8,128)(2,1)S(1)}, bf16[1024,256]{1,0:T(8,128)(2,1)S(1)}, u32[]{:S(2)}, u32[]{:S(2)}) %collective-permute-start.3) | collective-permute-done | bytes 524320 | tf_op jit(solution)/shard_map/ppermute | solution.py:339
  29.4 0.9 collective-permute-done.4.rest_13_.rest_8_
  30.7 1.5 collective-permute-start.7
  32.2 1.6 collective-permute-start.6
  34.3 2.1 %pad_maximum_fusion.2 = bf16[256,2048]{1,0:T(8,128)(2,1)} fusion(bf16[128,2048]{1,0:T(8,128)(2,1)S(1)} %collective-permute-done.rest_2_, bf16[128,2048]{1,0:T(8,128)(2,1)} %copy-done.8), kind=kLoop, calls=%fused_computation.13 | loop fusion | flops 2097152 | bytes 2097152 | tf_op jit(solution)/shard_map/concatenate | solution.py:389
  36.4 8.4 %collective-permute-done.7.rest_12_.rest_7_ = bf16[1024,256]{1,0:T(8,128)(2,1)S(1)} collective-permute-done((bf16[1024,256]{1,0:T(8,128)(2,1)S(1)}, bf16[1024,256]{1,0:T(8,128)(2,1)S(1)}, u32[]{:S(2)}, u32[]{:S(2)}) %collective-permute-start.7) | collective-permute-done | bytes 524320 | tf_op jit(solution)/shard_map/ppermute | solution.py:339
  44.8 1.6 collective-permute-start.9
  46.9 8.4 %collective-permute-done.5.rest_5_ = bf16[128,2176]{1,0:T(8,128)(2,1)S(1)} collective-permute-done((bf16[128,2176]{1,0:T(8,128)(2,1)S(1)}, bf16[128,2176]{1,0:T(8,128)(2,1)S(1)}, u32[]{:S(2)}, u32[]{:S(2)}) %collective-permute-start.5) | collective-permute-done | bytes 557088 | tf_op jit(solution)/shard_map/ppermute | solution.py:335
  55.3 1.2 pad_maximum_fusion.1
  56.4 1.3 collective-permute-done.6.rest_4_
  58.1 1.3 collective-permute-done.11.rest_15_.rest_10_
  59.4 1.6 %collective-permute-start.12 = (bf16[128,4224]{1,0:T(8,128)(2,1)}, bf16[128,4224]{1,0:T(8,128)(2,1)}, u32[]{:S(2)}, u32[]{:S(2)}) collective-permute-start(bf16[128,4224]{1,0:T(8,128)(2,1)} %pad_maximum_fusion.1), channel_id=1, source_target_pairs={{0,4},{4,0},{8,12},{12,8},{1,5},{5,1},{9,13},{13,9},{2,6},{6,2},{1... | collective-permute-start | bytes 3244040 | tf_op jit(solution)/shard_map/ppermute | solution.py:335
  61.6 1.4 collective-permute-start.13
  63.2 0.5 collective-permute-done.15.rest_17_.rest_12_
  63.9 0.6 collective-permute-done.16.rest_18_.rest_13_
  64.5 0.8 copy-done.4
  65.5 1.1 constant_dynamic-update-slice_fusion.2
  66.6 1.0 collective-permute-done.19.rest_21_.rest_16_
  67.6 1.0 copy-done.7
  68.7 1.0 copy-done.9
  69.7 15.3 %shard_map.110 = (bf16[512,1024]{1,0:T(8,128)(2,1)}, bf16[512,512]{1,0:T(8,128)(2,1)S(1)}, bf16[512,512]{1,0:T(8,128)(2,1)S(1)}, bf16[512,2048]{1,0:T(8,128)(2,1...) custom-call(f32[1,128]{1,0:T(1,128)S(1)} %compare_convert_fusion.lan, ...), custom_call_target="tpu_custom_call" | custom-call | flops 786432 | bytes 1572864 | tf_op jit(solution)/shard_map/pallas_call | solution.py:305
  85.1 2.4 %collective-permute-done.13 = bf16[256,2048]{1,0:T(8,128)(2,1)} collective-permute-done((bf16[256,2048]{1,0:T(8,128)(2,1)}, bf16[256,2048]{1,0:T(8,128)(2,1)}, u32[]{:S(2)}, u32[]{:S(2)}) %collective-permute-start.13) | collective-permute-done | bytes 1048608 | tf_op jit(solution)/shard_map/ppermute | solution.py:339
  87.5 1.4 collective-permute-start.20
  88.8 1.3 constant_dynamic-update-slice_fusion.1
  90.1 1.7 %collective-permute-start.21 = (bf16[128,1280]{1,0:T(8,128)(2,1)S(1)}, bf16[128,1280]{1,0:T(8,128)(2,1)S(1)}, u32[]{:S(2)}, u32[]{:S(2)}) collective-permute-start(bf16[128,1280]{1,0:T(8,128)(2,1)S(1)} %get-tuple-element.99), channel_id=1, source_target_pairs={{0,8},{4,12},{8,0},{12,4},{1,9},{5,13},{9,1},{13,5},{2,10},{6,14},... | collective-permute-start | bytes 983048 | tf_op jit(solution)/shard_map/ppermute | solution.py:335
  91.8 1.1 fusion.22
  92.9 0.5 collective-permute-start.22
  93.4 1.6 collective-permute-start.25
  95.0 10.8 %shard_map.111 = (bf16[512,1024]{1,0:T(8,128)(2,1)}, bf16[512,512]{1,0:T(8,128)(2,1)S(1)}, bf16[512,512]{1,0:T(8,128)(2,1)S(1)}, bf16[512,2048]{1,0:T(8,128)(2,1...) custom-call(f32[1,128]{1,0:T(1,128)S(1)} %compare_convert_fusion.lan, ...), custom_call_target="tpu_custom_call", output_to_operand_aliasing={{0}: (19, {}), {1}: (20, {}), {2}: (21, {}), {3}: (22, {})} | custom-call | flops 262144 | bytes 524288 | tf_op jit(solution)/shard_map/pallas_call | solution.py:305
  105.9 2.9 %convolution_convert_fusion.3 = bf16[2048,512]{1,0:T(8,128)(2,1)S(1)} fusion(bf16[512,2048]{1,0:T(8,128)(2,1)} %get-tuple-element.114, bf16[512,512]{1,0:T(8,128)(2,1)S(1)} %get-tuple-element.111), kind=kOutput, calls=%fused_computation.7 | convolution fusion | flops 1074790400 | bytes 4718592 | tf_op jit(solution)/shard_map/dot_general | solution.py:355
  108.9 0.7 copy-done.24
  109.6 1.1 slice_dynamic-update-slice_fusion.1
  110.7 1.4 fusion.21
  112.3 1.6 collective-permute-start.23
  113.8 0.7 collective-permute-start.24
  114.6 1.3 convolution_convert_fusion.2
  115.9 0.9 copy-done.32
  116.8 1.9 %convolution_convert_fusion = bf16[2048,512]{1,0:T(8,128)(2,1)S(1)} fusion(bf16[768,2048]{1,0:T(8,128)(2,1)S(1)} %copy-done.32, bf16[256,1024]{1,0:T(8,128)(2,1)S(1)} %slice.94, bf16[512,1024]{1,0:T(8,128)(2,1)S(1)} %copy-done.18), kind=kOutput, calls=%fused_computation.4 | convolution fusion | flops 1613234176 | bytes 6815744 | tf_op jit(solution)/shard_map/dot_general | solution.py:355
  118.7 1.9 %convolution_convert_fusion.1 = bf16[2048,512]{1,0:T(8,128)(2,1)S(1)} fusion(bf16[768,2048]{1,0:T(8,128)(2,1)S(1)} %copy-done.32, bf16[512,1024]{1,0:T(8,128)(2,1)S(1)} %copy-done.18, bf16[256,1024]{1,0:T(8,128)(2,1)S(1)} %slice.94), kind=kOutput, calls=%fused_computation.5 | convolution fusion | flops 1613234176 | bytes 6815744 | tf_op jit(solution)/shard_map/dot_general | solution.py:355
  120.6 0.7 add_convert_fusion.2
  121.3 1.1 fusion.20
  122.4 1.9 %collective-permute-done.24 = bf16[128,896]{1,0:T(8,128)(2,1)S(1)} collective-permute-done((bf16[128,896]{1,0:T(8,128)(2,1)S(1)}, bf16[128,896]{1,0:T(8,128)(2,1)S(1)}, u32[]{:S(2)}, u32[]{:S(2)}) %collective-permute-start.24) | collective-permute-done | bytes 229408 | tf_op jit(solution)/shard_map/ppermute | solution.py:335
  124.3 2.1 %add_convert_fusion.1 = bf16[2048,512]{1,0:T(8,128)(2,1)} fusion(bf16[2048,512]{1,0:T(8,128)(2,1)S(1)} %convolution_convert_fusion, bf16[128,1024]{1,0:T(8,128)(2,1)S(1)} %collective-permute-done.25, bf16[128,1024]{1,0:T(8,128)(2,1)S(1)} %collective-permute-done.22, bf16[128,2048]{1,0:T(8,128)(2,1)S(1)} %get-tuple-element.141, ...), kind=kOutput, calls=%fused_computation.1 | convolution fusion | flops 543686656 | bytes 5767168 | tf_op jit(solution)/shard_map/dot_general | solution.py:355
  126.5 0.9 convert_reduce_fusion.3
  127.4 3.6 %collective-permute-start.27 = (bf16[128,2176]{1,0:T(8,128)(2,1)}, bf16[128,2176]{1,0:T(8,128)(2,1)S(1)}, u32[]{:S(2)}, u32[]{:S(2)}) collective-permute-start(bf16[128,2176]{1,0:T(8,128)(2,1)} %get-tuple-element.122), channel_id=1, source_target_pairs={{0,4},{4,0},{8,12},{12,8},{1,5},{5,1},{9,13},{13,9},{2,6},{6,2},{1... | collective-permute-start | bytes 1671176 | tf_op jit(solution)/shard_map/ppermute | solution.py:335
  131.4 1.1 collective-permute-start.29
  132.5 0.9 convert_reduce_fusion.1
  133.3 2.0 %fusion.4 = f32[2048,512]{1,0:T(8,128)S(1)} fusion(bf16[128,1024]{1,0:T(8,128)(2,1)} %copy-done.29, bf16[128,1024]{1,0:T(8,128)(2,1)} %copy-done.28, bf16[128,2048]{1,0:T(8,128)(2,1)} %copy-done.17, bf16[128,1024]{1,0:T(8,128)(2,1)S(1)} %slice.97, bf16[128,1024]{1,0:T(8,128)(2,1)} %copy-done.30), kind=kOutput, calls=%fused_computation.28 | convolution fusion | flops 540540928 | bytes 5767168 | tf_op jit(solution)/shard_map/dot_general | solution.py:355
  135.3 2.5 %add_convert_fusion = bf16[2048,512]{1,0:T(8,128)(2,1)S(1)} fusion(bf16[2048,512]{1,0:T(8,128)(2,1)} %collective-permute-done.30, f32[2048,512]{1,0:T(8,128)S(1)} %fusion.4, bf16[2048,512]{1,0:T(8,128)(2,1)S(1)} %convolution_convert_fusion.1), kind=kLoop, calls=%fused_computation | loop fusion | flops 5242880 | bytes 10485760 | tf_op jit(solution)/shard_map/convert_element_type | solution.py:455
  137.8 1.5 fusion.19
  139.3 16.5 %collective-permute-done.27 = bf16[128,2176]{1,0:T(8,128)(2,1)S(1)} collective-permute-done((bf16[128,2176]{1,0:T(8,128)(2,1)}, bf16[128,2176]{1,0:T(8,128)(2,1)S(1)}, u32[]{:S(2)}, u32[]{:S(2)}) %collective-permute-start.27) | collective-permute-done | bytes 557088 | tf_op jit(solution)/shard_map/ppermute | solution.py:335
  155.8 2.1 %collective-permute-done.28 = bf16[128,2176]{1,0:T(8,128)(2,1)S(1)} collective-permute-done((bf16[128,2176]{1,0:T(8,128)(2,1)}, bf16[128,2176]{1,0:T(8,128)(2,1)S(1)}, u32[]{:S(2)}, u32[]{:S(2)}) %collective-permute-start.28) | collective-permute-done | bytes 557088 | tf_op jit(solution)/shard_map/ppermute | solution.py:335
  158.0 1.1 add_convert_fusion.4
  159.1 1.3 fusion
  160.4 0.5 fusion.14
  (105 shorter events, 4.9 us)
Async XLA Ops:
  0.6 7.6 %copy-start.33 = (s32[128,2]{0,1:T(2,128)S(1)}, s32[128,2]{0,1:T(2,128)}, u32[]{:S(2)}) copy-start(s32[128,2]{0,1:T(2,128)} %param.9) | copy-start | bytes 3076
  0.6 7.6 %copy-start.34 = (bf16[128,2]{0,1:T(2,128)(2,1)S(1)}, bf16[128,2]{0,1:T(2,128)(2,1)}, u32[]{:S(2)}) copy-start(bf16[128,2]{0,1:T(2,128)(2,1)} %param.10) | copy-start | bytes 1540
  0.7 25.3 %collective-permute-start = (bf16[128,2048]{1,0:T(8,128)(2,1)}, bf16[128,2048]{1,0:T(8,128)(2,1)S(1)}, u32[]{:S(2)}, u32[]{:S(2)}) collective-permute-start(bf16[128,2048]{1,0:T(8,128)(2,1)} %rest_0_.1), channel_id=1, source_target_pairs={{0,8},{4,12},{8,0},{12,4},{1,9},{5,13},{9,1},{13,5},{2,10},{6,14},... | collective-permute-start | bytes 1572872 | tf_op jit(solution)/shard_map/ppermute | solution.py:335
  3.3 23.6 %collective-permute-start.1 = (bf16[128,2048]{1,0:T(8,128)(2,1)}, bf16[128,2048]{1,0:T(8,128)(2,1)S(1)}, u32[]{:S(2)}, u32[]{:S(2)}) collective-permute-start(bf16[128,2048]{1,0:T(8,128)(2,1)} %rest_0_.1), channel_id=1, source_target_pairs={{0,4},{4,0},{8,12},{12,8},{1,5},{5,1},{9,13},{13,9},{2,6},{6,2},{1... | collective-permute-start | bytes 1572872 | tf_op jit(solution)/shard_map/ppermute | solution.py:335
  3.8 4.5 %copy-start.10 = (bf16[1,2048,256]{2,1,0:T(8,128)(2,1)S(1)}, bf16[1,2048,256]{2,1,0:T(8,128)(2,1)}, u32[]{:S(2)}) copy-start(bf16[1,2048,256]{2,1,0:T(8,128)(2,1)} %param.11) | copy-start | bytes 3145732
  3.8 4.5 %copy-start.11 = (bf16[1,2048,256]{2,1,0:T(8,128)(2,1)S(1)}, bf16[1,2048,256]{2,1,0:T(8,128)(2,1)}, u32[]{:S(2)}) copy-start(bf16[1,2048,256]{2,1,0:T(8,128)(2,1)} %param.12) | copy-start | bytes 3145732
  5.0 14.9 %collective-permute-start.2 = (bf16[1024,256]{1,0:T(8,128)(2,1)S(1)}, bf16[1024,256]{1,0:T(8,128)(2,1)S(1)}, u32[]{:S(2)}, u32[]{:S(2)}) collective-permute-start(bf16[1024,256]{1,0:T(8,128)(2,1)S(1)} %dynamic-slice_bitcast_fusion.2), channel_id=1, source_target_pairs={{0,2},{1,3},{2,0},{3,1},{4,6},{5,7},{6,4},{7,5},{8,10},{9,11},{10,... | collective-permute-start | bytes 1572872 | tf_op jit(solution)/shard_map/ppermute | solution.py:339
  7.6 21.8 %collective-permute-start.3 = (bf16[1024,256]{1,0:T(8,128)(2,1)S(1)}, bf16[1024,256]{1,0:T(8,128)(2,1)S(1)}, u32[]{:S(2)}, u32[]{:S(2)}) collective-permute-start(bf16[1024,256]{1,0:T(8,128)(2,1)S(1)} %dynamic-slice_bitcast_fusion.1), channel_id=1, source_target_pairs={{0,2},{1,3},{2,0},{3,1},{4,6},{5,7},{6,4},{7,5},{8,10},{9,11},{10,... | collective-permute-start | bytes 1572872 | tf_op jit(solution)/shard_map/ppermute | solution.py:339
  8.3 12.3 %copy-start.12 = (bf16[1,2048,256]{2,1,0:T(8,128)(2,1)S(1)}, bf16[1,2048,256]{2,1,0:T(8,128)(2,1)}, u32[]{:S(2)}) copy-start(bf16[1,2048,256]{2,1,0:T(8,128)(2,1)} %param.13) | copy-start | bytes 3145732
  8.3 12.4 %copy-start.21 = (bf16[128,2048]{1,0:T(8,128)(2,1)S(1)}, bf16[128,2048]{1,0:T(8,128)(2,1)}, u32[]{:S(2)}) copy-start(bf16[128,2048]{1,0:T(8,128)(2,1)} %param.8) | copy-start | bytes 1572868
  19.9 10.4 %collective-permute-start.4 = (bf16[1024,256]{1,0:T(8,128)(2,1)S(1)}, bf16[1024,256]{1,0:T(8,128)(2,1)S(1)}, u32[]{:S(2)}, u32[]{:S(2)}) collective-permute-start(bf16[1024,256]{1,0:T(8,128)(2,1)S(1)} %collective-permute-done.2.rest_10_.rest_5_), channel_id=1, source_target_pairs={{0,16},{16,0},{1,17},{17,1},{2,18},{18,2},{3,19},{19,3},{4,20},{20... | collective-permute-start | bytes 1572872 | tf_op jit(solution)/shard_map/ppermute | solution.py:347
  20.6 24.2 %copy-start.6 = (bf16[128,2048]{1,0:T(8,128)(2,1)S(1)}, bf16[128,2048]{1,0:T(8,128)(2,1)}, u32[]{:S(2)}) copy-start(bf16[128,2048]{1,0:T(8,128)(2,1)} %rest_0_.1) | copy-start | bytes 1572868
  20.7 43.8 %copy-start.14 = (bf16[128,2176]{1,0:T(8,128)(2,1)}, bf16[128,2176]{1,0:T(8,128)(2,1)S(1)}, u32[]{:S(2)}) copy-start(bf16[128,2176]{1,0:T(8,128)(2,1)S(1)} %pad_maximum_fusion.5.rest_3_) | copy-start | bytes 1671172
  26.9 3.5 %copy-start.8 = (bf16[128,2048]{1,0:T(8,128)(2,1)}, bf16[128,2048]{1,0:T(8,128)(2,1)S(1)}, u32[]{:S(2)}) copy-start(bf16[128,2048]{1,0:T(8,128)(2,1)S(1)} %collective-permute-done.1.rest_1_) | copy-start | bytes 1572868
  30.3 14.5 %collective-permute-start.8 = (bf16[3,2048,256]{2,1,0:T(8,128)(2,1)S(1)}, bf16[3,2048,256]{2,1,0:T(8,128)(2,1)S(1)}, u32[]{:S(2)}, u32[]{:S(2)}) collective-permute-start(bf16[3,2048,256]{2,1,0:T(8,128)(2,1)S(1)} %pad_maximum_fusion), channel_id=1, source_target_pairs={{0,1},{1,0},{2,3},{3,2},{4,5},{5,4},{6,7},{7,6},{8,9},{9,8},{10,11... | collective-permute-start | bytes 9437192 | tf_op jit(solution)/shard_map/ppermute | solution.py:343
  30.3 24.9 %collective-permute-start.5 = (bf16[128,2176]{1,0:T(8,128)(2,1)S(1)}, bf16[128,2176]{1,0:T(8,128)(2,1)S(1)}, u32[]{:S(2)}, u32[]{:S(2)}) collective-permute-start(bf16[128,2176]{1,0:T(8,128)(2,1)S(1)} %pad_maximum_fusion.5.rest_3_), channel_id=1, source_target_pairs={{0,8},{4,12},{8,0},{12,4},{1,9},{5,13},{9,1},{13,5},{2,10},{6,14},... | collective-permute-start | bytes 1671176 | tf_op jit(solution)/shard_map/ppermute | solution.py:335
  30.7 14.1 %collective-permute-start.7 = (bf16[1024,256]{1,0:T(8,128)(2,1)S(1)}, bf16[1024,256]{1,0:T(8,128)(2,1)S(1)}, u32[]{:S(2)}, u32[]{:S(2)}) collective-permute-start(bf16[1024,256]{1,0:T(8,128)(2,1)S(1)} %dynamic-slice_bitcast_fusion), channel_id=1, source_target_pairs={{0,2},{1,3},{2,0},{3,1},{4,6},{5,7},{6,4},{7,5},{8,10},{9,11},{10,... | collective-permute-start | bytes 1572872 | tf_op jit(solution)/shard_map/ppermute | solution.py:339
  32.2 25.5 %collective-permute-start.6 = (bf16[128,2176]{1,0:T(8,128)(2,1)S(1)}, bf16[128,2176]{1,0:T(8,128)(2,1)S(1)}, u32[]{:S(2)}, u32[]{:S(2)}) collective-permute-start(bf16[128,2176]{1,0:T(8,128)(2,1)S(1)} %pad_maximum_fusion.5.rest_3_), channel_id=1, source_target_pairs={{0,4},{4,0},{8,12},{12,8},{1,5},{5,1},{9,13},{13,9},{2,6},{6,2},{1... | collective-permute-start | bytes 1671176 | tf_op jit(solution)/shard_map/ppermute | solution.py:335
  33.8 22.6 %collective-permute-start.10 = (bf16[1024,256]{1,0:T(8,128)(2,1)S(1)}, bf16[1024,256]{1,0:T(8,128)(2,1)S(1)}, u32[]{:S(2)}, u32[]{:S(2)}) collective-permute-start(bf16[1024,256]{1,0:T(8,128)(2,1)S(1)} %collective-permute-done.3.rest_11_.rest_6_), channel_id=1, source_target_pairs={{0,16},{16,0},{1,17},{17,1},{2,18},{18,2},{3,19},{19,3},{4,20},{20... | collective-permute-start | bytes 1572872 | tf_op jit(solution)/shard_map/ppermute | solution.py:347
  44.8 19.7 %copy-start.13 = (bf16[3,2048,256]{2,1,0:T(8,128)(2,1)}, bf16[3,2048,256]{2,1,0:T(8,128)(2,1)S(1)}, u32[]{:S(2)}) copy-start(bf16[3,2048,256]{2,1,0:T(8,128)(2,1)S(1)} %collective-permute-done.8.rest_9_.rest_4_) | copy-start | bytes 9437188
  44.8 13.3 %collective-permute-start.9 = (bf16[128,2048]{1,0:T(8,128)(2,1)S(1)}, bf16[128,2048]{1,0:T(8,128)(2,1)S(1)}, u32[]{:S(2)}, u32[]{:S(2)}) collective-permute-start(bf16[128,2048]{1,0:T(8,128)(2,1)S(1)} %copy-done.6), channel_id=1, source_target_pairs={{0,2},{1,3},{2,0},{3,1},{4,6},{5,7},{6,4},{7,5},{8,10},{9,11},{10,... | collective-permute-start | bytes 1572872 | tf_op jit(solution)/shard_map/ppermute | solution.py:339
  46.4 13.1 %collective-permute-start.11 = (bf16[1024,256]{1,0:T(8,128)(2,1)S(1)}, bf16[1024,256]{1,0:T(8,128)(2,1)}, u32[]{:S(2)}, u32[]{:S(2)}) collective-permute-start(bf16[1024,256]{1,0:T(8,128)(2,1)S(1)} %collective-permute-done.7.rest_12_.rest_7_), channel_id=1, source_target_pairs={{0,16},{16,0},{1,17},{17,1},{2,18},{18,2},{3,19},{19,3},{4,20},{20... | collective-permute-start | bytes 1572872 | tf_op jit(solution)/shard_map/ppermute | solution.py:347
  55.3 9.2 %copy-start.15 = (bf16[128,2176]{1,0:T(8,128)(2,1)}, bf16[128,2176]{1,0:T(8,128)(2,1)S(1)}, u32[]{:S(2)}) copy-start(bf16[128,2176]{1,0:T(8,128)(2,1)S(1)} %collective-permute-done.5.rest_5_) | copy-start | bytes 1671172
  57.7 6.7 %copy-start.19 = (bf16[128,2176]{1,0:T(8,128)(2,1)}, bf16[128,2176]{1,0:T(8,128)(2,1)S(1)}, u32[]{:S(2)}) copy-start(bf16[128,2176]{1,0:T(8,128)(2,1)S(1)} %collective-permute-done.6.rest_4_) | copy-start | bytes 1671172
  58.1 6.4 %copy-start.22 = (bf16[128,2048]{1,0:T(8,128)(2,1)}, bf16[128,2048]{1,0:T(8,128)(2,1)S(1)}, u32[]{:S(2)}) copy-start(bf16[128,2048]{1,0:T(8,128)(2,1)S(1)} %collective-permute-done.9) | copy-start | bytes 1572868
  59.4 28.0 %collective-permute-start.12 = (bf16[128,4224]{1,0:T(8,128)(2,1)}, bf16[128,4224]{1,0:T(8,128)(2,1)}, u32[]{:S(2)}, u32[]{:S(2)}) collective-permute-start(bf16[128,4224]{1,0:T(8,128)(2,1)} %pad_maximum_fusion.1), channel_id=1, source_target_pairs={{0,4},{4,0},{8,12},{12,8},{1,5},{5,1},{9,13},{13,9},{2,6},{6,2},{1... | collective-permute-start | bytes 3244040 | tf_op jit(solution)/shard_map/ppermute | solution.py:335
  61.1 1.9 %collective-permute-start.14 = (bf16[1024,256]{1,0:T(8,128)(2,1)S(1)}, bf16[1024,256]{1,0:T(8,128)(2,1)S(1)}, u32[]{:S(2)}, u32[]{:S(2)}) collective-permute-start(bf16[1024,256]{1,0:T(8,128)(2,1)S(1)} %collective-permute-done.2.rest_10_.rest_5_), channel_id=1, source_target_pairs={{0,1},{1,0},{2,3},{3,2},{4,5},{5,4},{6,7},{7,6},{8,9},{9,8},{10,11... | collective-permute-start | bytes 1572872 | tf_op jit(solution)/shard_map/ppermute | solution.py:343
  61.1 2.7 %collective-permute-start.15 = (bf16[1024,256]{1,0:T(8,128)(2,1)S(1)}, bf16[1024,256]{1,0:T(8,128)(2,1)S(1)}, u32[]{:S(2)}, u32[]{:S(2)}) collective-permute-start(bf16[1024,256]{1,0:T(8,128)(2,1)S(1)} %collective-permute-done.3.rest_11_.rest_6_), channel_id=1, source_target_pairs={{0,1},{1,0},{2,3},{3,2},{4,5},{5,4},{6,7},{7,6},{8,9},{9,8},{10,11... | collective-permute-start | bytes 1572872 | tf_op jit(solution)/shard_map/ppermute | solution.py:343
  61.6 2.9 %collective-permute-start.16 = (bf16[1024,256]{1,0:T(8,128)(2,1)S(1)}, bf16[1024,256]{1,0:T(8,128)(2,1)S(1)}, u32[]{:S(2)}, u32[]{:S(2)}) collective-permute-start(bf16[1024,256]{1,0:T(8,128)(2,1)S(1)} %collective-permute-done.7.rest_12_.rest_7_), channel_id=1, source_target_pairs={{0,1},{1,0},{2,3},{3,2},{4,5},{5,4},{6,7},{7,6},{8,9},{9,8},{10,11... | collective-permute-start | bytes 1572872 | tf_op jit(solution)/shard_map/ppermute | solution.py:343
  61.6 25.9 %collective-permute-start.13 = (bf16[256,2048]{1,0:T(8,128)(2,1)}, bf16[256,2048]{1,0:T(8,128)(2,1)}, u32[]{:S(2)}, u32[]{:S(2)}) collective-permute-start(bf16[256,2048]{1,0:T(8,128)(2,1)} %pad_maximum_fusion.2), channel_id=1, source_target_pairs={{0,2},{1,3},{2,0},{3,1},{4,6},{5,7},{6,4},{7,5},{8,10},{9,11},{10,... | collective-permute-start | bytes 3145736 | tf_op jit(solution)/shard_map/ppermute | solution.py:339
  63.0 1.5 copy-start
  63.0 3.6 %collective-permute-start.17 = (bf16[1024,256]{1,0:T(8,128)(2,1)S(1)}, bf16[1024,256]{1,0:T(8,128)(2,1)}, u32[]{:S(2)}, u32[]{:S(2)}) collective-permute-start(bf16[1024,256]{1,0:T(8,128)(2,1)S(1)} %collective-permute-done.4.rest_13_.rest_8_), channel_id=1, source_target_pairs={{0,1},{1,0},{2,3},{3,2},{4,5},{5,4},{6,7},{7,6},{8,9},{9,8},{10,11... | collective-permute-start | bytes 1572872 | tf_op jit(solution)/shard_map/ppermute | solution.py:343
  63.7 2.9 %collective-permute-start.18 = (bf16[1024,256]{1,0:T(8,128)(2,1)S(1)}, bf16[1024,256]{1,0:T(8,128)(2,1)}, u32[]{:S(2)}, u32[]{:S(2)}) collective-permute-start(bf16[1024,256]{1,0:T(8,128)(2,1)S(1)} %collective-permute-done.10.rest_14_.rest_9_), channel_id=1, source_target_pairs={{0,1},{1,0},{2,3},{3,2},{4,5},{5,4},{6,7},{7,6},{8,9},{9,8},{10,11... | collective-permute-start | bytes 1572872 | tf_op jit(solution)/shard_map/ppermute | solution.py:343
  64.5 0.8 copy-start.4
  65.4 2.3 %collective-permute-start.19 = (bf16[1024,256]{1,0:T(8,128)(2,1)}, bf16[1024,256]{1,0:T(8,128)(2,1)}, u32[]{:S(2)}, u32[]{:S(2)}) collective-permute-start(bf16[1024,256]{1,0:T(8,128)(2,1)} %collective-permute-done.11.rest_15_.rest_10_), channel_id=1, source_target_pairs={{0,1},{1,0},{2,3},{3,2},{4,5},{5,4},{6,7},{7,6},{8,9},{9,8},{10,11... | collective-permute-start | bytes 1572872 | tf_op jit(solution)/shard_map/ppermute | solution.py:343
  67.6 1.0 copy-start.7
  68.7 1.0 copy-start.9
  85.0 9.9 %copy-start.1 = (bf16[1024,256]{1,0:T(8,128)(2,1)S(1)}, bf16[1024,256]{1,0:T(8,128)(2,1)}, u32[]{:S(2)}) copy-start(bf16[1024,256]{1,0:T(8,128)(2,1)} %copy-done) | copy-start | bytes 1572868
  85.1 9.9 %copy-start.3 = (bf16[1024,256]{1,0:T(8,128)(2,1)S(1)}, bf16[1024,256]{1,0:T(8,128)(2,1)}, u32[]{:S(2)}) copy-start(bf16[1024,256]{1,0:T(8,128)(2,1)} %copy-done.2) | copy-start | bytes 1572868
  85.1 9.9 %copy-start.5 = (bf16[1024,256]{1,0:T(8,128)(2,1)S(1)}, bf16[1024,256]{1,0:T(8,128)(2,1)}, u32[]{:S(2)}) copy-start(bf16[1024,256]{1,0:T(8,128)(2,1)} %copy-done.4) | copy-start | bytes 1572868
  87.5 21.4 %collective-permute-start.20 = (bf16[384,1024]{1,0:T(8,128)(2,1)}, bf16[384,1024]{1,0:T(8,128)(2,1)S(1)}, u32[]{:S(2)}, u32[]{:S(2)}) collective-permute-start(bf16[384,1024]{1,0:T(8,128)(2,1)} %get-tuple-element.98), channel_id=1, source_target_pairs={{0,2},{1,3},{2,0},{3,1},{4,6},{5,7},{6,4},{7,5},{8,10},{9,11},{10,... | collective-permute-start | bytes 2359304 | tf_op jit(solution)/shard_map/ppermute | solution.py:339
  90.1 18.7 %collective-permute-start.21 = (bf16[128,1280]{1,0:T(8,128)(2,1)S(1)}, bf16[128,1280]{1,0:T(8,128)(2,1)S(1)}, u32[]{:S(2)}, u32[]{:S(2)}) collective-permute-start(bf16[128,1280]{1,0:T(8,128)(2,1)S(1)} %get-tuple-element.99), channel_id=1, source_target_pairs={{0,8},{4,12},{8,0},{12,4},{1,9},{5,13},{9,1},{13,5},{2,10},{6,14},... | collective-permute-start | bytes 983048 | tf_op jit(solution)/shard_map/ppermute | solution.py:335
  92.9 15.9 %collective-permute-start.22 = (bf16[128,1024]{1,0:T(8,128)(2,1)S(1)}, bf16[128,1024]{1,0:T(8,128)(2,1)S(1)}, u32[]{:S(2)}, u32[]{:S(2)}) collective-permute-start(bf16[128,1024]{1,0:T(8,128)(2,1)S(1)} %get-tuple-element.144), channel_id=1, source_target_pairs={{0,4},{4,0},{8,12},{12,8},{1,5},{5,1},{9,13},{13,9},{2,6},{6,2},{1... | collective-permute-start | bytes 786440 | tf_op jit(solution)/shard_map/ppermute | solution.py:335
  93.4 29.0 %collective-permute-start.25 = (bf16[128,1024]{1,0:T(8,128)(2,1)S(1)}, bf16[128,1024]{1,0:T(8,128)(2,1)S(1)}, u32[]{:S(2)}, u32[]{:S(2)}) collective-permute-start(bf16[128,1024]{1,0:T(8,128)(2,1)S(1)} %get-tuple-element.143), channel_id=1, source_target_pairs={{0,4},{4,0},{8,12},{12,8},{1,5},{5,1},{9,13},{13,9},{2,6},{6,2},{1... | collective-permute-start | bytes 786440 | tf_op jit(solution)/shard_map/ppermute | solution.py:335
  105.8 4.8 %copy-start.23 = (bf16[128,2048]{1,0:T(8,128)(2,1)S(1)}, bf16[128,2048]{1,0:T(8,128)(2,1)}, u32[]{:S(2)}) copy-start(bf16[128,2048]{1,0:T(8,128)(2,1)} %copy-done.22) | copy-start | bytes 1572868
  108.8 15.5 %copy-start.28 = (bf16[128,1024]{1,0:T(8,128)(2,1)}, bf16[128,1024]{1,0:T(8,128)(2,1)S(1)}, u32[]{:S(2)}) copy-start(bf16[128,1024]{1,0:T(8,128)(2,1)S(1)} %collective-permute-done.22) | copy-start | bytes 786436
  109.6 11.0 %collective-permute-start.26 = (bf16[2048,512]{1,0:T(8,128)(2,1)S(1)}, bf16[2048,512]{1,0:T(8,128)(2,1)S(1)}, u32[]{:S(2)}, u32[]{:S(2)}) collective-permute-start(bf16[2048,512]{1,0:T(8,128)(2,1)S(1)} %convolution_convert_fusion.3), channel_id=1, source_target_pairs={{0,1},{1,0},{2,3},{3,2},{4,5},{5,4},{6,7},{7,6},{8,9},{9,8},{10,11... | collective-permute-start | bytes 6291464 | tf_op jit(solution)/shard_map/ppermute | solution.py:343
  110.7 3.9 %copy-start.16 = (bf16[512,2048]{1,0:T(8,128)(2,1)S(1)}, bf16[512,2048]{1,0:T(8,128)(2,1)}, u32[]{:S(2)}) copy-start(bf16[512,2048]{1,0:T(8,128)(2,1)} %get-tuple-element.114) | copy-start | bytes 6291460
  112.2 2.4 %copy-start.31 = (bf16[768,2048]{1,0:T(8,128)(2,1)}, bf16[768,2048]{1,0:T(8,128)(2,1)S(1)}, u32[]{:S(2)}) copy-start(bf16[768,2048]{1,0:T(8,128)(2,1)S(1)} %get-tuple-element.142) | copy-start | bytes 9437188
  112.2 12.1 %copy-start.17 = (bf16[128,2048]{1,0:T(8,128)(2,1)}, bf16[128,2048]{1,0:T(8,128)(2,1)S(1)}, u32[]{:S(2)}) copy-start(bf16[128,2048]{1,0:T(8,128)(2,1)S(1)} %get-tuple-element.141) | copy-start | bytes 1572868
  112.3 12.0 %collective-permute-start.23 = (bf16[128,1024]{1,0:T(8,128)(2,1)S(1)}, bf16[128,1024]{1,0:T(8,128)(2,1)S(1)}, u32[]{:S(2)}, u32[]{:S(2)}) collective-permute-start(bf16[128,1024]{1,0:T(8,128)(2,1)S(1)} %get-tuple-element.112), channel_id=1, source_target_pairs={{0,2},{1,3},{2,0},{3,1},{4,6},{5,7},{6,4},{7,5},{8,10},{9,11},{10,... | collective-permute-start | bytes 786440 | tf_op jit(solution)/shard_map/ppermute | solution.py:339
  113.8 10.5 %collective-permute-start.24 = (bf16[128,896]{1,0:T(8,128)(2,1)S(1)}, bf16[128,896]{1,0:T(8,128)(2,1)S(1)}, u32[]{:S(2)}, u32[]{:S(2)}) collective-permute-start(bf16[128,896]{1,0:T(8,128)(2,1)S(1)} %get-tuple-element.113), channel_id=1, source_target_pairs={{0,8},{4,12},{8,0},{12,4},{1,9},{5,13},{9,1},{13,5},{2,10},{6,14},... | collective-permute-start | bytes 688136 | tf_op jit(solution)/shard_map/ppermute | solution.py:335
  114.6 1.3 copy-start.18
  114.6 2.2 %copy-start.32 = (bf16[768,2048]{1,0:T(8,128)(2,1)S(1)}, bf16[768,2048]{1,0:T(8,128)(2,1)}, u32[]{:S(2)}) copy-start(bf16[768,2048]{1,0:T(8,128)(2,1)} %copy-done.31) | copy-start | bytes 9437188
  122.4 4.1 %copy-start.29 = (bf16[128,1024]{1,0:T(8,128)(2,1)}, bf16[128,1024]{1,0:T(8,128)(2,1)S(1)}, u32[]{:S(2)}) copy-start(bf16[128,1024]{1,0:T(8,128)(2,1)S(1)} %collective-permute-done.25) | copy-start | bytes 786436
  124.3 2.1 %copy-start.26 = (bf16[128,896]{1,0:T(8,128)(2,1)}, bf16[128,896]{1,0:T(8,128)(2,1)S(1)}, u32[]{:S(2)}) copy-start(bf16[128,896]{1,0:T(8,128)(2,1)S(1)} %collective-permute-done.24) | copy-start | bytes 688132
  124.3 2.1 %copy-start.30 = (bf16[128,1024]{1,0:T(8,128)(2,1)}, bf16[128,1024]{1,0:T(8,128)(2,1)S(1)}, u32[]{:S(2)}) copy-start(bf16[128,1024]{1,0:T(8,128)(2,1)S(1)} %collective-permute-done.23) | copy-start | bytes 786436
  126.4 8.9 %collective-permute-start.30 = (bf16[2048,512]{1,0:T(8,128)(2,1)}, bf16[2048,512]{1,0:T(8,128)(2,1)}, u32[]{:S(2)}, u32[]{:S(2)}) collective-permute-start(bf16[2048,512]{1,0:T(8,128)(2,1)} %add_convert_fusion.1), channel_id=1, source_target_pairs={{0,1},{1,0},{2,3},{3,2},{4,5},{5,4},{6,7},{7,6},{8,9},{9,8},{10,11... | collective-permute-start | bytes 6291464 | tf_op jit(solution)/shard_map/ppermute | solution.py:343
  127.4 28.4 %collective-permute-start.27 = (bf16[128,2176]{1,0:T(8,128)(2,1)}, bf16[128,2176]{1,0:T(8,128)(2,1)S(1)}, u32[]{:S(2)}, u32[]{:S(2)}) collective-permute-start(bf16[128,2176]{1,0:T(8,128)(2,1)} %get-tuple-element.122), channel_id=1, source_target_pairs={{0,4},{4,0},{8,12},{12,8},{1,5},{5,1},{9,13},{13,9},{2,6},{6,2},{1... | collective-permute-start | bytes 1671176 | tf_op jit(solution)/shard_map/ppermute | solution.py:335
  131.0 26.9 %collective-permute-start.28 = (bf16[128,2176]{1,0:T(8,128)(2,1)}, bf16[128,2176]{1,0:T(8,128)(2,1)S(1)}, u32[]{:S(2)}, u32[]{:S(2)}) collective-permute-start(bf16[128,2176]{1,0:T(8,128)(2,1)} %get-tuple-element.123), channel_id=1, source_target_pairs={{0,12},{4,8},{8,4},{12,0},{1,13},{5,9},{9,5},{13,1},{2,14},{6,10},... | collective-permute-start | bytes 1671176 | tf_op jit(solution)/shard_map/ppermute | solution.py:335
  131.4 26.5 %collective-permute-start.29 = (bf16[2048,256]{1,0:T(8,128)(2,1)}, bf16[2048,256]{1,0:T(8,128)(2,1)S(1)}, u32[]{:S(2)}, u32[]{:S(2)}) collective-permute-start(bf16[2048,256]{1,0:T(8,128)(2,1)} %get-tuple-element.124), channel_id=1, source_target_pairs={{0,2},{1,3},{2,0},{3,1},{4,6},{5,7},{6,4},{7,5},{8,10},{9,11},{10,... | collective-permute-start | bytes 3145736 | tf_op jit(solution)/shard_map/ppermute | solution.py:339
  137.8 20.2 %copy-start.20 = (bf16[128,2176]{1,0:T(8,128)(2,1)S(1)}, bf16[128,2176]{1,0:T(8,128)(2,1)}, u32[]{:S(2)}) copy-start(bf16[128,2176]{1,0:T(8,128)(2,1)} %get-tuple-element.97) | copy-start | bytes 1671172
  137.8 20.2 %copy-start.25 = (bf16[128,1280]{1,0:T(8,128)(2,1)S(1)}, bf16[128,1280]{1,0:T(8,128)(2,1)}, u32[]{:S(2)}) copy-start(bf16[128,1280]{1,0:T(8,128)(2,1)} %copy-done.24) | copy-start | bytes 983044
  137.8 20.2 %copy-start.27 = (bf16[128,896]{1,0:T(8,128)(2,1)S(1)}, bf16[128,896]{1,0:T(8,128)(2,1)}, u32[]{:S(2)}) copy-start(bf16[128,896]{1,0:T(8,128)(2,1)} %copy-done.26) | copy-start | bytes 688132
  (2 other events, 1.6 us)

commit v4 on v3

--- a/solution.py
+++ b/solution.py
@@ -395,7 +395,7 @@
     three = over_z(two, apart(1))
     far_bc = over_x(in_bc)
     weights = [*own, near, *far_weights, *[over_core(w) for w in far_weights]]
-    slots, wide, cut = 4, features + 128, features * 5 // 8
+    slots, wide, cut = 4, features + 128, features * 3 // 4
     kept, (crossing_abc,), backs = slot_compute(
         [tokens, in_one, in_two],
         [wide_grad, grad_one, grad_two],

time: 163 us -> 161 us (0.988)
  waiting for transfers between devices: 64.4 us -> 62.3 us
    ppermute x11, waiting for transfers between devices: 36.4 us -> 34.5 us  [over_z(): return lax.ppermute(value, 'expert', pairs)]
  transfers between devices with their start and end apart: 31 -> 31, of which waited for: 17 -> 16; matrix products, arithmetic and copies ran while one was open for 19% -> 19% of each run, Pallas kernels for 16% -> 17%
where the time goes in v4:
time: 161 us; the launch traced here: 159 us
  waiting for transfers between devices  62.3 us (39%)
  starting transfers between devices  28.1 us (17%)
  Pallas kernels  26.4 us (16%)
  local copies, waits for them, and re-layouts  15.7 us (10%)
  other arithmetic  13 us (8%)
  matrix products  12.1 us (8%)
    ppermute x11, waiting for transfers between devices, over_z(): return lax.ppermute(value, 'expert', pairs)  34.5 us
    pallas_call x2, Pallas kernels, slot_compute(): pl.pallas_call(functools.partial(slot_kernel, slots, not grads, bool(kept...  26.4 us
    ppermute x8, waiting for transfers between devices, over_x(): return lax.ppermute(value, 'replica', swap_x)  23.4 us
    ppermute x11, starting transfers between devices, over_z(): return lax.ppermute(value, 'expert', pairs)  14.8 us
    dot_general x6, matrix products, outer(): lax.dot_general(lhs, rhs, (((0,), (0,)), ((), ())), preferred_element_typ...  12.1 us
    ppermute x8, starting transfers between devices, over_x(): return lax.ppermute(value, 'replica', swap_x)  10.7 us
    unnamed x74, local copies, waits for them, and re-layouts  8.2 us
  transfers between devices with their start and end apart: 31, of which 16 were waited for; matrix products, arithmetic and copies ran while one was open for 19% of the time, Pallas kernels for 17%

profile of v4, /device:TPU:12, one launch (start us, length us, event | category | flops | bytes accessed | tf_op | source)
XLA Modules:
  0.0 158.7 jit_solution(14325762538225079724)
XLA Ops:
  0.7 2.7 %collective-permute-start = (bf16[128,2048]{1,0:T(8,128)(2,1)}, bf16[128,2048]{1,0:T(8,128)(2,1)S(1)}, u32[]{:S(2)}, u32[]{:S(2)}) collective-permute-start(bf16[128,2048]{1,0:T(8,128)(2,1)} %rest_0_.1), channel_id=1, source_target_pairs={{0,8},{4,12},{8,0},{12,4},{1,9},{5,13},{9,1},{13,5},{2,10},{6,14},... | collective-permute-start | bytes 1572872 | tf_op jit(solution)/shard_map/ppermute | solution.py:335
  3.8 1.2 dynamic-slice_bitcast_fusion.2
  5.0 1.6 collective-permute-start.2
  6.5 1.1 dynamic-slice_bitcast_fusion.1
  7.6 0.6 collective-permute-start.3
  8.3 1.7 %pad_maximum_fusion = bf16[3,2048,256]{2,1,0:T(8,128)(2,1)S(1)} fusion(bf16[1,2048,256]{2,1,0:T(8,128)(2,1)} %param.13, bf16[1,2048,256]{2,1,0:T(8,128)(2,1)S(1)} %copy-done.11, bf16[1,2048,256]{2,1,0:T(8,128)(2,1)S(1)} %copy-done.10), kind=kLoop, calls=%fused_computation.3 | loop fusion | flops 3145728 | bytes 6291456 | tf_op jit(solution)/shard_map/stack | solution.py:379
  10.0 9.9 %collective-permute-done.2.rest_10_.rest_5_ = bf16[1024,256]{1,0:T(8,128)(2,1)S(1)} collective-permute-done((bf16[1024,256]{1,0:T(8,128)(2,1)S(1)}, bf16[1024,256]{1,0:T(8,128)(2,1)S(1)}, u32[]{:S(2)}, u32[]{:S(2)}) %collective-permute-start.2) | collective-permute-done | bytes 524320 | tf_op jit(solution)/shard_map/ppermute | solution.py:339
  20.7 5.2 %collective-permute-done.rest_2_ = bf16[128,2048]{1,0:T(8,128)(2,1)S(1)} collective-permute-done((bf16[128,2048]{1,0:T(8,128)(2,1)}, bf16[128,2048]{1,0:T(8,128)(2,1)S(1)}, u32[]{:S(2)}, u32[]{:S(2)}) %collective-permute-start) | collective-permute-done | bytes 524320 | tf_op jit(solution)/shard_map/ppermute | solution.py:335
  25.9 1.0 collective-permute-done.1.rest_1_
  26.9 2.5 %collective-permute-done.3.rest_11_.rest_6_ = bf16[1024,256]{1,0:T(8,128)(2,1)S(1)} collective-permute-done((bf16[1024,256]{1,0:T(8,128)(2,1)S(1)}, bf16[1024,256]{1,0:T(8,128)(2,1)S(1)}, u32[]{:S(2)}, u32[]{:S(2)}) %collective-permute-start.3) | collective-permute-done | bytes 524320 | tf_op jit(solution)/shard_map/ppermute | solution.py:339
  29.4 0.9 collective-permute-done.4.rest_13_.rest_8_
  30.7 1.5 collective-permute-start.7
  32.2 1.6 collective-permute-start.6
  34.3 2.1 %pad_maximum_fusion.2 = bf16[256,2048]{1,0:T(8,128)(2,1)} fusion(bf16[128,2048]{1,0:T(8,128)(2,1)S(1)} %collective-permute-done.rest_2_, bf16[128,2048]{1,0:T(8,128)(2,1)} %copy-done.8), kind=kLoop, calls=%fused_computation.13 | loop fusion | flops 2097152 | bytes 2097152 | tf_op jit(solution)/shard_map/concatenate | solution.py:389
  36.4 8.4 %collective-permute-done.7.rest_12_.rest_7_ = bf16[1024,256]{1,0:T(8,128)(2,1)S(1)} collective-permute-done((bf16[1024,256]{1,0:T(8,128)(2,1)S(1)}, bf16[1024,256]{1,0:T(8,128)(2,1)S(1)}, u32[]{:S(2)}, u32[]{:S(2)}) %collective-permute-start.7) | collective-permute-done | bytes 524320 | tf_op jit(solution)/shard_map/ppermute | solution.py:339
  44.8 1.6 collective-permute-start.9
  46.9 8.4 %collective-permute-done.5.rest_5_ = bf16[128,2176]{1,0:T(8,128)(2,1)S(1)} collective-permute-done((bf16[128,2176]{1,0:T(8,128)(2,1)S(1)}, bf16[128,2176]{1,0:T(8,128)(2,1)S(1)}, u32[]{:S(2)}, u32[]{:S(2)}) %collective-permute-start.5) | collective-permute-done | bytes 557088 | tf_op jit(solution)/shard_map/ppermute | solution.py:335
  55.3 1.2 pad_maximum_fusion.1
  56.4 1.3 collective-permute-done.6.rest_4_
  58.1 1.3 collective-permute-done.11.rest_15_.rest_10_
  59.4 1.6 %collective-permute-start.12 = (bf16[128,4224]{1,0:T(8,128)(2,1)}, bf16[128,4224]{1,0:T(8,128)(2,1)}, u32[]{:S(2)}, u32[]{:S(2)}) collective-permute-start(bf16[128,4224]{1,0:T(8,128)(2,1)} %pad_maximum_fusion.1), channel_id=1, source_target_pairs={{0,4},{4,0},{8,12},{12,8},{1,5},{5,1},{9,13},{13,9},{2,6},{6,2},{1... | collective-permute-start | bytes 3244040 | tf_op jit(solution)/shard_map/ppermute | solution.py:335
  61.1 0.5 collective-permute-start.15
  61.6 1.4 collective-permute-start.13
  63.2 0.5 collective-permute-done.15.rest_17_.rest_12_
  63.9 0.6 collective-permute-done.16.rest_18_.rest_13_
  64.5 0.8 copy-done.4
  65.5 1.1 constant_dynamic-update-slice_fusion.2
  66.6 1.0 collective-permute-done.19.rest_21_.rest_16_
  67.6 1.0 copy-done.7
  68.7 1.0 copy-done.9
  69.7 15.5 %shard_map.110 = (bf16[512,1024]{1,0:T(8,128)(2,1)}, bf16[512,512]{1,0:T(8,128)(2,1)S(1)}, bf16[512,512]{1,0:T(8,128)(2,1)S(1)}, bf16[512,2048]{1,0:T(8,128)(2,1...) custom-call(f32[1,128]{1,0:T(1,128)S(1)} %compare_convert_fusion.lan, ...), custom_call_target="tpu_custom_call" | custom-call | flops 786432 | bytes 1572864 | tf_op jit(solution)/shard_map/pallas_call | solution.py:305
  85.3 2.2 %collective-permute-done.13 = bf16[256,2048]{1,0:T(8,128)(2,1)} collective-permute-done((bf16[256,2048]{1,0:T(8,128)(2,1)}, bf16[256,2048]{1,0:T(8,128)(2,1)}, u32[]{:S(2)}, u32[]{:S(2)}) %collective-permute-start.13) | collective-permute-done | bytes 1048608 | tf_op jit(solution)/shard_map/ppermute | solution.py:339
  87.5 1.4 collective-permute-start.20
  88.8 1.3 constant_dynamic-update-slice_fusion.1
  90.1 1.7 %collective-permute-start.21 = (bf16[128,1536]{1,0:T(8,128)(2,1)S(1)}, bf16[128,1536]{1,0:T(8,128)(2,1)S(1)}, u32[]{:S(2)}, u32[]{:S(2)}) collective-permute-start(bf16[128,1536]{1,0:T(8,128)(2,1)S(1)} %get-tuple-element.99), channel_id=1, source_target_pairs={{0,8},{4,12},{8,0},{12,4},{1,9},{5,13},{9,1},{13,5},{2,10},{6,14},... | collective-permute-start | bytes 1179656 | tf_op jit(solution)/shard_map/ppermute | solution.py:335
  91.8 1.1 fusion.22
  92.9 0.5 collective-permute-start.22
  93.4 1.6 collective-permute-start.25
  95.0 10.8 %shard_map.111 = (bf16[512,1024]{1,0:T(8,128)(2,1)}, bf16[512,512]{1,0:T(8,128)(2,1)S(1)}, bf16[512,512]{1,0:T(8,128)(2,1)S(1)}, bf16[512,2048]{1,0:T(8,128)(2,1...) custom-call(f32[1,128]{1,0:T(1,128)S(1)} %compare_convert_fusion.lan, ...), custom_call_target="tpu_custom_call", output_to_operand_aliasing={{0}: (19, {}), {1}: (20, {}), {2}: (21, {}), {3}: (22, {})} | custom-call | flops 262144 | bytes 524288 | tf_op jit(solution)/shard_map/pallas_call | solution.py:305
  105.9 2.9 %convolution_convert_fusion.3 = bf16[2048,512]{1,0:T(8,128)(2,1)S(1)} fusion(bf16[512,2048]{1,0:T(8,128)(2,1)} %get-tuple-element.114, bf16[512,512]{1,0:T(8,128)(2,1)S(1)} %get-tuple-element.111), kind=kOutput, calls=%fused_computation.7 | convolution fusion | flops 1074790400 | bytes 4718592 | tf_op jit(solution)/shard_map/dot_general | solution.py:355
  108.9 0.8 copy-done.24
  109.6 1.1 slice_dynamic-update-slice_fusion.1
  110.8 1.4 fusion.21
  112.3 1.6 collective-permute-start.23
  113.9 2.7 %collective-permute-start.24 = (bf16[128,640]{1,0:T(8,128)(2,1)S(1)}, bf16[128,640]{1,0:T(8,128)(2,1)S(1)}, u32[]{:S(2)}, u32[]{:S(2)}) collective-permute-start(bf16[128,640]{1,0:T(8,128)(2,1)S(1)} %get-tuple-element.113), channel_id=1, source_target_pairs={{0,8},{4,12},{8,0},{12,4},{1,9},{5,13},{9,1},{13,5},{2,10},{6,14},... | collective-permute-start | bytes 491528 | tf_op jit(solution)/shard_map/ppermute | solution.py:335
  116.6 1.3 convolution_convert_fusion.2
  117.9 0.9 copy-done.32
  118.8 1.9 %convolution_convert_fusion = bf16[2048,512]{1,0:T(8,128)(2,1)S(1)} fusion(bf16[768,2048]{1,0:T(8,128)(2,1)S(1)} %copy-done.32, bf16[256,1024]{1,0:T(8,128)(2,1)S(1)} %slice.94, bf16[512,1024]{1,0:T(8,128)(2,1)S(1)} %copy-done.18), kind=kOutput, calls=%fused_computation.4 | convolution fusion | flops 1613234176 | bytes 6815744 | tf_op jit(solution)/shard_map/dot_general | solution.py:355
  120.7 1.9 %convolution_convert_fusion.1 = bf16[2048,512]{1,0:T(8,128)(2,1)S(1)} fusion(bf16[768,2048]{1,0:T(8,128)(2,1)S(1)} %copy-done.32, bf16[512,1024]{1,0:T(8,128)(2,1)S(1)} %copy-done.18, bf16[256,1024]{1,0:T(8,128)(2,1)S(1)} %slice.94), kind=kOutput, calls=%fused_computation.5 | convolution fusion | flops 1613234176 | bytes 6815744 | tf_op jit(solution)/shard_map/dot_general | solution.py:355
  122.6 0.7 add_convert_fusion.2
  123.3 1.1 fusion.20
  124.5 2.1 %add_convert_fusion.1 = bf16[2048,512]{1,0:T(8,128)(2,1)} fusion(bf16[2048,512]{1,0:T(8,128)(2,1)S(1)} %convolution_convert_fusion, bf16[128,1024]{1,0:T(8,128)(2,1)S(1)} %collective-permute-done.25, bf16[128,1024]{1,0:T(8,128)(2,1)S(1)} %collective-permute-done.22, bf16[128,2048]{1,0:T(8,128)(2,1)S(1)} %get-tuple-element.141, ...), kind=kOutput, calls=%fused_computation.1 | convolution fusion | flops 543686656 | bytes 5767168 | tf_op jit(solution)/shard_map/dot_general | solution.py:355
  126.6 0.9 convert_reduce_fusion.3
  127.5 1.3 collective-permute-start.27
  129.1 1.1 collective-permute-start.29
  130.3 0.9 convert_reduce_fusion.1
  131.1 2.0 %fusion.4 = f32[2048,512]{1,0:T(8,128)S(1)} fusion(bf16[128,1024]{1,0:T(8,128)(2,1)} %copy-done.27, bf16[128,1024]{1,0:T(8,128)(2,1)} %copy-done.26, bf16[128,2048]{1,0:T(8,128)(2,1)} %copy-done.17, bf16[128,1024]{1,0:T(8,128)(2,1)S(1)} %slice.97, bf16[128,1024]{1,0:T(8,128)(2,1)} %copy-done.28), kind=kOutput, calls=%fused_computation.28 | convolution fusion | flops 540540928 | bytes 5767168 | tf_op jit(solution)/shard_map/dot_general | solution.py:355
  133.1 2.5 %add_convert_fusion = bf16[2048,512]{1,0:T(8,128)(2,1)S(1)} fusion(bf16[2048,512]{1,0:T(8,128)(2,1)} %collective-permute-done.30, f32[2048,512]{1,0:T(8,128)S(1)} %fusion.4, bf16[2048,512]{1,0:T(8,128)(2,1)S(1)} %convolution_convert_fusion.1), kind=kLoop, calls=%fused_computation | loop fusion | flops 5242880 | bytes 10485760 | tf_op jit(solution)/shard_map/convert_element_type | solution.py:455
  135.6 1.5 fusion.19
  137.1 16.6 %collective-permute-done.27 = bf16[128,2176]{1,0:T(8,128)(2,1)S(1)} collective-permute-done((bf16[128,2176]{1,0:T(8,128)(2,1)}, bf16[128,2176]{1,0:T(8,128)(2,1)S(1)}, u32[]{:S(2)}, u32[]{:S(2)}) %collective-permute-start.27) | collective-permute-done | bytes 557088 | tf_op jit(solution)/shard_map/ppermute | solution.py:335
  153.7 2.1 %collective-permute-done.28 = bf16[128,2176]{1,0:T(8,128)(2,1)S(1)} collective-permute-done((bf16[128,2176]{1,0:T(8,128)(2,1)}, bf16[128,2176]{1,0:T(8,128)(2,1)S(1)}, u32[]{:S(2)}, u32[]{:S(2)}) %collective-permute-start.28) | collective-permute-done | bytes 557088 | tf_op jit(solution)/shard_map/ppermute | solution.py:335
  155.9 1.1 add_convert_fusion.4
  156.9 1.3 fusion
  158.2 0.5 fusion.14
  (105 shorter events, 4.2 us)
Async XLA Ops:
  0.6 7.6 %copy-start.33 = (s32[128,2]{0,1:T(2,128)S(1)}, s32[128,2]{0,1:T(2,128)}, u32[]{:S(2)}) copy-start(s32[128,2]{0,1:T(2,128)} %param.9) | copy-start | bytes 3076
  0.6 7.6 %copy-start.34 = (bf16[128,2]{0,1:T(2,128)(2,1)S(1)}, bf16[128,2]{0,1:T(2,128)(2,1)}, u32[]{:S(2)}) copy-start(bf16[128,2]{0,1:T(2,128)(2,1)} %param.10) | copy-start | bytes 1540
  0.7 25.3 %collective-permute-start = (bf16[128,2048]{1,0:T(8,128)(2,1)}, bf16[128,2048]{1,0:T(8,128)(2,1)S(1)}, u32[]{:S(2)}, u32[]{:S(2)}) collective-permute-start(bf16[128,2048]{1,0:T(8,128)(2,1)} %rest_0_.1), channel_id=1, source_target_pairs={{0,8},{4,12},{8,0},{12,4},{1,9},{5,13},{9,1},{13,5},{2,10},{6,14},... | collective-permute-start | bytes 1572872 | tf_op jit(solution)/shard_map/ppermute | solution.py:335
  3.3 23.6 %collective-permute-start.1 = (bf16[128,2048]{1,0:T(8,128)(2,1)}, bf16[128,2048]{1,0:T(8,128)(2,1)S(1)}, u32[]{:S(2)}, u32[]{:S(2)}) collective-permute-start(bf16[128,2048]{1,0:T(8,128)(2,1)} %rest_0_.1), channel_id=1, source_target_pairs={{0,4},{4,0},{8,12},{12,8},{1,5},{5,1},{9,13},{13,9},{2,6},{6,2},{1... | collective-permute-start | bytes 1572872 | tf_op jit(solution)/shard_map/ppermute | solution.py:335
  3.8 4.5 %copy-start.10 = (bf16[1,2048,256]{2,1,0:T(8,128)(2,1)S(1)}, bf16[1,2048,256]{2,1,0:T(8,128)(2,1)}, u32[]{:S(2)}) copy-start(bf16[1,2048,256]{2,1,0:T(8,128)(2,1)} %param.11) | copy-start | bytes 3145732
  3.8 4.5 %copy-start.11 = (bf16[1,2048,256]{2,1,0:T(8,128)(2,1)S(1)}, bf16[1,2048,256]{2,1,0:T(8,128)(2,1)}, u32[]{:S(2)}) copy-start(bf16[1,2048,256]{2,1,0:T(8,128)(2,1)} %param.12) | copy-start | bytes 3145732
  5.0 14.9 %collective-permute-start.2 = (bf16[1024,256]{1,0:T(8,128)(2,1)S(1)}, bf16[1024,256]{1,0:T(8,128)(2,1)S(1)}, u32[]{:S(2)}, u32[]{:S(2)}) collective-permute-start(bf16[1024,256]{1,0:T(8,128)(2,1)S(1)} %dynamic-slice_bitcast_fusion.2), channel_id=1, source_target_pairs={{0,2},{1,3},{2,0},{3,1},{4,6},{5,7},{6,4},{7,5},{8,10},{9,11},{10,... | collective-permute-start | bytes 1572872 | tf_op jit(solution)/shard_map/ppermute | solution.py:339
  7.6 21.8 %collective-permute-start.3 = (bf16[1024,256]{1,0:T(8,128)(2,1)S(1)}, bf16[1024,256]{1,0:T(8,128)(2,1)S(1)}, u32[]{:S(2)}, u32[]{:S(2)}) collective-permute-start(bf16[1024,256]{1,0:T(8,128)(2,1)S(1)} %dynamic-slice_bitcast_fusion.1), channel_id=1, source_target_pairs={{0,2},{1,3},{2,0},{3,1},{4,6},{5,7},{6,4},{7,5},{8,10},{9,11},{10,... | collective-permute-start | bytes 1572872 | tf_op jit(solution)/shard_map/ppermute | solution.py:339
  8.3 12.3 %copy-start.12 = (bf16[1,2048,256]{2,1,0:T(8,128)(2,1)S(1)}, bf16[1,2048,256]{2,1,0:T(8,128)(2,1)}, u32[]{:S(2)}) copy-start(bf16[1,2048,256]{2,1,0:T(8,128)(2,1)} %param.13) | copy-start | bytes 3145732
  8.3 12.4 %copy-start.21 = (bf16[128,2048]{1,0:T(8,128)(2,1)S(1)}, bf16[128,2048]{1,0:T(8,128)(2,1)}, u32[]{:S(2)}) copy-start(bf16[128,2048]{1,0:T(8,128)(2,1)} %param.8) | copy-start | bytes 1572868
  19.9 10.4 %collective-permute-start.4 = (bf16[1024,256]{1,0:T(8,128)(2,1)S(1)}, bf16[1024,256]{1,0:T(8,128)(2,1)S(1)}, u32[]{:S(2)}, u32[]{:S(2)}) collective-permute-start(bf16[1024,256]{1,0:T(8,128)(2,1)S(1)} %collective-permute-done.2.rest_10_.rest_5_), channel_id=1, source_target_pairs={{0,16},{16,0},{1,17},{17,1},{2,18},{18,2},{3,19},{19,3},{4,20},{20... | collective-permute-start | bytes 1572872 | tf_op jit(solution)/shard_map/ppermute | solution.py:347
  20.6 24.2 %copy-start.6 = (bf16[128,2048]{1,0:T(8,128)(2,1)S(1)}, bf16[128,2048]{1,0:T(8,128)(2,1)}, u32[]{:S(2)}) copy-start(bf16[128,2048]{1,0:T(8,128)(2,1)} %rest_0_.1) | copy-start | bytes 1572868
  20.7 43.8 %copy-start.14 = (bf16[128,2176]{1,0:T(8,128)(2,1)}, bf16[128,2176]{1,0:T(8,128)(2,1)S(1)}, u32[]{:S(2)}) copy-start(bf16[128,2176]{1,0:T(8,128)(2,1)S(1)} %pad_maximum_fusion.5.rest_3_) | copy-start | bytes 1671172
  26.9 3.5 %copy-start.8 = (bf16[128,2048]{1,0:T(8,128)(2,1)}, bf16[128,2048]{1,0:T(8,128)(2,1)S(1)}, u32[]{:S(2)}) copy-start(bf16[128,2048]{1,0:T(8,128)(2,1)S(1)} %collective-permute-done.1.rest_1_) | copy-start | bytes 1572868
  30.3 14.5 %collective-permute-start.8 = (bf16[3,2048,256]{2,1,0:T(8,128)(2,1)S(1)}, bf16[3,2048,256]{2,1,0:T(8,128)(2,1)S(1)}, u32[]{:S(2)}, u32[]{:S(2)}) collective-permute-start(bf16[3,2048,256]{2,1,0:T(8,128)(2,1)S(1)} %pad_maximum_fusion), channel_id=1, source_target_pairs={{0,1},{1,0},{2,3},{3,2},{4,5},{5,4},{6,7},{7,6},{8,9},{9,8},{10,11... | collective-permute-start | bytes 9437192 | tf_op jit(solution)/shard_map/ppermute | solution.py:343
  30.3 24.9 %collective-permute-start.5 = (bf16[128,2176]{1,0:T(8,128)(2,1)S(1)}, bf16[128,2176]{1,0:T(8,128)(2,1)S(1)}, u32[]{:S(2)}, u32[]{:S(2)}) collective-permute-start(bf16[128,2176]{1,0:T(8,128)(2,1)S(1)} %pad_maximum_fusion.5.rest_3_), channel_id=1, source_target_pairs={{0,8},{4,12},{8,0},{12,4},{1,9},{5,13},{9,1},{13,5},{2,10},{6,14},... | collective-permute-start | bytes 1671176 | tf_op jit(solution)/shard_map/ppermute | solution.py:335
  30.7 14.1 %collective-permute-start.7 = (bf16[1024,256]{1,0:T(8,128)(2,1)S(1)}, bf16[1024,256]{1,0:T(8,128)(2,1)S(1)}, u32[]{:S(2)}, u32[]{:S(2)}) collective-permute-start(bf16[1024,256]{1,0:T(8,128)(2,1)S(1)} %dynamic-slice_bitcast_fusion), channel_id=1, source_target_pairs={{0,2},{1,3},{2,0},{3,1},{4,6},{5,7},{6,4},{7,5},{8,10},{9,11},{10,... | collective-permute-start | bytes 1572872 | tf_op jit(solution)/shard_map/ppermute | solution.py:339
  32.2 25.5 %collective-permute-start.6 = (bf16[128,2176]{1,0:T(8,128)(2,1)S(1)}, bf16[128,2176]{1,0:T(8,128)(2,1)S(1)}, u32[]{:S(2)}, u32[]{:S(2)}) collective-permute-start(bf16[128,2176]{1,0:T(8,128)(2,1)S(1)} %pad_maximum_fusion.5.rest_3_), channel_id=1, source_target_pairs={{0,4},{4,0},{8,12},{12,8},{1,5},{5,1},{9,13},{13,9},{2,6},{6,2},{1... | collective-permute-start | bytes 1671176 | tf_op jit(solution)/shard_map/ppermute | solution.py:335
  33.8 22.6 %collective-permute-start.10 = (bf16[1024,256]{1,0:T(8,128)(2,1)S(1)}, bf16[1024,256]{1,0:T(8,128)(2,1)S(1)}, u32[]{:S(2)}, u32[]{:S(2)}) collective-permute-start(bf16[1024,256]{1,0:T(8,128)(2,1)S(1)} %collective-permute-done.3.rest_11_.rest_6_), channel_id=1, source_target_pairs={{0,16},{16,0},{1,17},{17,1},{2,18},{18,2},{3,19},{19,3},{4,20},{20... | collective-permute-start | bytes 1572872 | tf_op jit(solution)/shard_map/ppermute | solution.py:347
  44.8 19.7 %copy-start.13 = (bf16[3,2048,256]{2,1,0:T(8,128)(2,1)}, bf16[3,2048,256]{2,1,0:T(8,128)(2,1)S(1)}, u32[]{:S(2)}) copy-start(bf16[3,2048,256]{2,1,0:T(8,128)(2,1)S(1)} %collective-permute-done.8.rest_9_.rest_4_) | copy-start | bytes 9437188
  44.8 13.3 %collective-permute-start.9 = (bf16[128,2048]{1,0:T(8,128)(2,1)S(1)}, bf16[128,2048]{1,0:T(8,128)(2,1)S(1)}, u32[]{:S(2)}, u32[]{:S(2)}) collective-permute-start(bf16[128,2048]{1,0:T(8,128)(2,1)S(1)} %copy-done.6), channel_id=1, source_target_pairs={{0,2},{1,3},{2,0},{3,1},{4,6},{5,7},{6,4},{7,5},{8,10},{9,11},{10,... | collective-permute-start | bytes 1572872 | tf_op jit(solution)/shard_map/ppermute | solution.py:339
  46.4 13.1 %collective-permute-start.11 = (bf16[1024,256]{1,0:T(8,128)(2,1)S(1)}, bf16[1024,256]{1,0:T(8,128)(2,1)}, u32[]{:S(2)}, u32[]{:S(2)}) collective-permute-start(bf16[1024,256]{1,0:T(8,128)(2,1)S(1)} %collective-permute-done.7.rest_12_.rest_7_), channel_id=1, source_target_pairs={{0,16},{16,0},{1,17},{17,1},{2,18},{18,2},{3,19},{19,3},{4,20},{20... | collective-permute-start | bytes 1572872 | tf_op jit(solution)/shard_map/ppermute | solution.py:347
  55.3 9.2 %copy-start.15 = (bf16[128,2176]{1,0:T(8,128)(2,1)}, bf16[128,2176]{1,0:T(8,128)(2,1)S(1)}, u32[]{:S(2)}) copy-start(bf16[128,2176]{1,0:T(8,128)(2,1)S(1)} %collective-permute-done.5.rest_5_) | copy-start | bytes 1671172
  57.7 6.7 %copy-start.19 = (bf16[128,2176]{1,0:T(8,128)(2,1)}, bf16[128,2176]{1,0:T(8,128)(2,1)S(1)}, u32[]{:S(2)}) copy-start(bf16[128,2176]{1,0:T(8,128)(2,1)S(1)} %collective-permute-done.6.rest_4_) | copy-start | bytes 1671172
  58.1 6.4 %copy-start.22 = (bf16[128,2048]{1,0:T(8,128)(2,1)}, bf16[128,2048]{1,0:T(8,128)(2,1)S(1)}, u32[]{:S(2)}) copy-start(bf16[128,2048]{1,0:T(8,128)(2,1)S(1)} %collective-permute-done.9) | copy-start | bytes 1572868
  59.4 28.0 %collective-permute-start.12 = (bf16[128,4224]{1,0:T(8,128)(2,1)}, bf16[128,4224]{1,0:T(8,128)(2,1)}, u32[]{:S(2)}, u32[]{:S(2)}) collective-permute-start(bf16[128,4224]{1,0:T(8,128)(2,1)} %pad_maximum_fusion.1), channel_id=1, source_target_pairs={{0,4},{4,0},{8,12},{12,8},{1,5},{5,1},{9,13},{13,9},{2,6},{6,2},{1... | collective-permute-start | bytes 3244040 | tf_op jit(solution)/shard_map/ppermute | solution.py:335
  61.1 1.9 %collective-permute-start.14 = (bf16[1024,256]{1,0:T(8,128)(2,1)S(1)}, bf16[1024,256]{1,0:T(8,128)(2,1)S(1)}, u32[]{:S(2)}, u32[]{:S(2)}) collective-permute-start(bf16[1024,256]{1,0:T(8,128)(2,1)S(1)} %collective-permute-done.2.rest_10_.rest_5_), channel_id=1, source_target_pairs={{0,1},{1,0},{2,3},{3,2},{4,5},{5,4},{6,7},{7,6},{8,9},{9,8},{10,11... | collective-permute-start | bytes 1572872 | tf_op jit(solution)/shard_map/ppermute | solution.py:343
  61.1 2.7 %collective-permute-start.15 = (bf16[1024,256]{1,0:T(8,128)(2,1)S(1)}, bf16[1024,256]{1,0:T(8,128)(2,1)S(1)}, u32[]{:S(2)}, u32[]{:S(2)}) collective-permute-start(bf16[1024,256]{1,0:T(8,128)(2,1)S(1)} %collective-permute-done.3.rest_11_.rest_6_), channel_id=1, source_target_pairs={{0,1},{1,0},{2,3},{3,2},{4,5},{5,4},{6,7},{7,6},{8,9},{9,8},{10,11... | collective-permute-start | bytes 1572872 | tf_op jit(solution)/shard_map/ppermute | solution.py:343
  61.6 2.9 %collective-permute-start.16 = (bf16[1024,256]{1,0:T(8,128)(2,1)S(1)}, bf16[1024,256]{1,0:T(8,128)(2,1)S(1)}, u32[]{:S(2)}, u32[]{:S(2)}) collective-permute-start(bf16[1024,256]{1,0:T(8,128)(2,1)S(1)} %collective-permute-done.7.rest_12_.rest_7_), channel_id=1, source_target_pairs={{0,1},{1,0},{2,3},{3,2},{4,5},{5,4},{6,7},{7,6},{8,9},{9,8},{10,11... | collective-permute-start | bytes 1572872 | tf_op jit(solution)/shard_map/ppermute | solution.py:343
  61.6 25.9 %collective-permute-start.13 = (bf16[256,2048]{1,0:T(8,128)(2,1)}, bf16[256,2048]{1,0:T(8,128)(2,1)}, u32[]{:S(2)}, u32[]{:S(2)}) collective-permute-start(bf16[256,2048]{1,0:T(8,128)(2,1)} %pad_maximum_fusion.2), channel_id=1, source_target_pairs={{0,2},{1,3},{2,0},{3,1},{4,6},{5,7},{6,4},{7,5},{8,10},{9,11},{10,... | collective-permute-start | bytes 3145736 | tf_op jit(solution)/shard_map/ppermute | solution.py:339
  63.0 1.5 copy-start
  63.0 3.6 %collective-permute-start.17 = (bf16[1024,256]{1,0:T(8,128)(2,1)S(1)}, bf16[1024,256]{1,0:T(8,128)(2,1)}, u32[]{:S(2)}, u32[]{:S(2)}) collective-permute-start(bf16[1024,256]{1,0:T(8,128)(2,1)S(1)} %collective-permute-done.4.rest_13_.rest_8_), channel_id=1, source_target_pairs={{0,1},{1,0},{2,3},{3,2},{4,5},{5,4},{6,7},{7,6},{8,9},{9,8},{10,11... | collective-permute-start | bytes 1572872 | tf_op jit(solution)/shard_map/ppermute | solution.py:343
  63.7 2.9 %collective-permute-start.18 = (bf16[1024,256]{1,0:T(8,128)(2,1)S(1)}, bf16[1024,256]{1,0:T(8,128)(2,1)}, u32[]{:S(2)}, u32[]{:S(2)}) collective-permute-start(bf16[1024,256]{1,0:T(8,128)(2,1)S(1)} %collective-permute-done.10.rest_14_.rest_9_), channel_id=1, source_target_pairs={{0,1},{1,0},{2,3},{3,2},{4,5},{5,4},{6,7},{7,6},{8,9},{9,8},{10,11... | collective-permute-start | bytes 1572872 | tf_op jit(solution)/shard_map/ppermute | solution.py:343
  64.5 0.8 copy-start.4
  65.4 2.3 %collective-permute-start.19 = (bf16[1024,256]{1,0:T(8,128)(2,1)}, bf16[1024,256]{1,0:T(8,128)(2,1)}, u32[]{:S(2)}, u32[]{:S(2)}) collective-permute-start(bf16[1024,256]{1,0:T(8,128)(2,1)} %collective-permute-done.11.rest_15_.rest_10_), channel_id=1, source_target_pairs={{0,1},{1,0},{2,3},{3,2},{4,5},{5,4},{6,7},{7,6},{8,9},{9,8},{10,11... | collective-permute-start | bytes 1572872 | tf_op jit(solution)/shard_map/ppermute | solution.py:343
  67.6 1.0 copy-start.7
  68.7 1.0 copy-start.9
  85.3 9.7 %copy-start.1 = (bf16[1024,256]{1,0:T(8,128)(2,1)S(1)}, bf16[1024,256]{1,0:T(8,128)(2,1)}, u32[]{:S(2)}) copy-start(bf16[1024,256]{1,0:T(8,128)(2,1)} %copy-done) | copy-start | bytes 1572868
  85.3 9.7 %copy-start.3 = (bf16[1024,256]{1,0:T(8,128)(2,1)S(1)}, bf16[1024,256]{1,0:T(8,128)(2,1)}, u32[]{:S(2)}) copy-start(bf16[1024,256]{1,0:T(8,128)(2,1)} %copy-done.2) | copy-start | bytes 1572868
  85.3 9.7 %copy-start.5 = (bf16[1024,256]{1,0:T(8,128)(2,1)S(1)}, bf16[1024,256]{1,0:T(8,128)(2,1)}, u32[]{:S(2)}) copy-start(bf16[1024,256]{1,0:T(8,128)(2,1)} %copy-done.4) | copy-start | bytes 1572868
  87.5 21.4 %collective-permute-start.20 = (bf16[384,1024]{1,0:T(8,128)(2,1)}, bf16[384,1024]{1,0:T(8,128)(2,1)S(1)}, u32[]{:S(2)}, u32[]{:S(2)}) collective-permute-start(bf16[384,1024]{1,0:T(8,128)(2,1)} %get-tuple-element.98), channel_id=1, source_target_pairs={{0,2},{1,3},{2,0},{3,1},{4,6},{5,7},{6,4},{7,5},{8,10},{9,11},{10,... | collective-permute-start | bytes 2359304 | tf_op jit(solution)/shard_map/ppermute | solution.py:339
  90.1 18.7 %collective-permute-start.21 = (bf16[128,1536]{1,0:T(8,128)(2,1)S(1)}, bf16[128,1536]{1,0:T(8,128)(2,1)S(1)}, u32[]{:S(2)}, u32[]{:S(2)}) collective-permute-start(bf16[128,1536]{1,0:T(8,128)(2,1)S(1)} %get-tuple-element.99), channel_id=1, source_target_pairs={{0,8},{4,12},{8,0},{12,4},{1,9},{5,13},{9,1},{13,5},{2,10},{6,14},... | collective-permute-start | bytes 1179656 | tf_op jit(solution)/shard_map/ppermute | solution.py:335
  92.9 15.9 %collective-permute-start.22 = (bf16[128,1024]{1,0:T(8,128)(2,1)S(1)}, bf16[128,1024]{1,0:T(8,128)(2,1)S(1)}, u32[]{:S(2)}, u32[]{:S(2)}) collective-permute-start(bf16[128,1024]{1,0:T(8,128)(2,1)S(1)} %get-tuple-element.144), channel_id=1, source_target_pairs={{0,4},{4,0},{8,12},{12,8},{1,5},{5,1},{9,13},{13,9},{2,6},{6,2},{1... | collective-permute-start | bytes 786440 | tf_op jit(solution)/shard_map/ppermute | solution.py:335
  93.4 31.0 %collective-permute-start.25 = (bf16[128,1024]{1,0:T(8,128)(2,1)S(1)}, bf16[128,1024]{1,0:T(8,128)(2,1)S(1)}, u32[]{:S(2)}, u32[]{:S(2)}) collective-permute-start(bf16[128,1024]{1,0:T(8,128)(2,1)S(1)} %get-tuple-element.143), channel_id=1, source_target_pairs={{0,4},{4,0},{8,12},{12,8},{1,5},{5,1},{9,13},{13,9},{2,6},{6,2},{1... | collective-permute-start | bytes 786440 | tf_op jit(solution)/shard_map/ppermute | solution.py:335
  105.8 4.9 %copy-start.23 = (bf16[128,2048]{1,0:T(8,128)(2,1)S(1)}, bf16[128,2048]{1,0:T(8,128)(2,1)}, u32[]{:S(2)}) copy-start(bf16[128,2048]{1,0:T(8,128)(2,1)} %copy-done.22) | copy-start | bytes 1572868
  108.8 15.6 %copy-start.26 = (bf16[128,1024]{1,0:T(8,128)(2,1)}, bf16[128,1024]{1,0:T(8,128)(2,1)S(1)}, u32[]{:S(2)}) copy-start(bf16[128,1024]{1,0:T(8,128)(2,1)S(1)} %collective-permute-done.22) | copy-start | bytes 786436
  109.6 13.0 %collective-permute-start.26 = (bf16[2048,512]{1,0:T(8,128)(2,1)S(1)}, bf16[2048,512]{1,0:T(8,128)(2,1)S(1)}, u32[]{:S(2)}, u32[]{:S(2)}) collective-permute-start(bf16[2048,512]{1,0:T(8,128)(2,1)S(1)} %convolution_convert_fusion.3), channel_id=1, source_target_pairs={{0,1},{1,0},{2,3},{3,2},{4,5},{5,4},{6,7},{7,6},{8,9},{9,8},{10,11... | collective-permute-start | bytes 6291464 | tf_op jit(solution)/shard_map/ppermute | solution.py:343
  110.8 5.9 %copy-start.16 = (bf16[512,2048]{1,0:T(8,128)(2,1)S(1)}, bf16[512,2048]{1,0:T(8,128)(2,1)}, u32[]{:S(2)}) copy-start(bf16[512,2048]{1,0:T(8,128)(2,1)} %get-tuple-element.114) | copy-start | bytes 6291460
  112.2 4.4 %copy-start.31 = (bf16[768,2048]{1,0:T(8,128)(2,1)}, bf16[768,2048]{1,0:T(8,128)(2,1)S(1)}, u32[]{:S(2)}) copy-start(bf16[768,2048]{1,0:T(8,128)(2,1)S(1)} %get-tuple-element.142) | copy-start | bytes 9437188
  112.2 12.2 %copy-start.17 = (bf16[128,2048]{1,0:T(8,128)(2,1)}, bf16[128,2048]{1,0:T(8,128)(2,1)S(1)}, u32[]{:S(2)}) copy-start(bf16[128,2048]{1,0:T(8,128)(2,1)S(1)} %get-tuple-element.141) | copy-start | bytes 1572868
  112.3 12.1 %collective-permute-start.23 = (bf16[128,1024]{1,0:T(8,128)(2,1)S(1)}, bf16[128,1024]{1,0:T(8,128)(2,1)S(1)}, u32[]{:S(2)}, u32[]{:S(2)}) collective-permute-start(bf16[128,1024]{1,0:T(8,128)(2,1)S(1)} %get-tuple-element.112), channel_id=1, source_target_pairs={{0,2},{1,3},{2,0},{3,1},{4,6},{5,7},{6,4},{7,5},{8,10},{9,11},{10,... | collective-permute-start | bytes 786440 | tf_op jit(solution)/shard_map/ppermute | solution.py:339
  113.9 10.5 %collective-permute-start.24 = (bf16[128,640]{1,0:T(8,128)(2,1)S(1)}, bf16[128,640]{1,0:T(8,128)(2,1)S(1)}, u32[]{:S(2)}, u32[]{:S(2)}) collective-permute-start(bf16[128,640]{1,0:T(8,128)(2,1)S(1)} %get-tuple-element.113), channel_id=1, source_target_pairs={{0,8},{4,12},{8,0},{12,4},{1,9},{5,13},{9,1},{13,5},{2,10},{6,14},... | collective-permute-start | bytes 491528 | tf_op jit(solution)/shard_map/ppermute | solution.py:335
  116.6 1.3 copy-start.18
  116.6 2.2 %copy-start.32 = (bf16[768,2048]{1,0:T(8,128)(2,1)S(1)}, bf16[768,2048]{1,0:T(8,128)(2,1)}, u32[]{:S(2)}) copy-start(bf16[768,2048]{1,0:T(8,128)(2,1)} %copy-done.31) | copy-start | bytes 9437188
  124.4 2.2 %copy-start.27 = (bf16[128,1024]{1,0:T(8,128)(2,1)}, bf16[128,1024]{1,0:T(8,128)(2,1)S(1)}, u32[]{:S(2)}) copy-start(bf16[128,1024]{1,0:T(8,128)(2,1)S(1)} %collective-permute-done.25) | copy-start | bytes 786436
  124.4 2.2 %copy-start.29 = (bf16[128,640]{1,0:T(8,128)(2,1)}, bf16[128,640]{1,0:T(8,128)(2,1)S(1)}, u32[]{:S(2)}) copy-start(bf16[128,640]{1,0:T(8,128)(2,1)S(1)} %collective-permute-done.24) | copy-start | bytes 491524
  124.4 2.1 %copy-start.28 = (bf16[128,1024]{1,0:T(8,128)(2,1)}, bf16[128,1024]{1,0:T(8,128)(2,1)S(1)}, u32[]{:S(2)}) copy-start(bf16[128,1024]{1,0:T(8,128)(2,1)S(1)} %collective-permute-done.23) | copy-start | bytes 786436
  126.6 6.5 %collective-permute-start.30 = (bf16[2048,512]{1,0:T(8,128)(2,1)}, bf16[2048,512]{1,0:T(8,128)(2,1)}, u32[]{:S(2)}, u32[]{:S(2)}) collective-permute-start(bf16[2048,512]{1,0:T(8,128)(2,1)} %add_convert_fusion.1), channel_id=1, source_target_pairs={{0,1},{1,0},{2,3},{3,2},{4,5},{5,4},{6,7},{7,6},{8,9},{9,8},{10,11... | collective-permute-start | bytes 6291464 | tf_op jit(solution)/shard_map/ppermute | solution.py:343
  127.5 26.1 %collective-permute-start.27 = (bf16[128,2176]{1,0:T(8,128)(2,1)}, bf16[128,2176]{1,0:T(8,128)(2,1)S(1)}, u32[]{:S(2)}, u32[]{:S(2)}) collective-permute-start(bf16[128,2176]{1,0:T(8,128)(2,1)} %get-tuple-element.122), channel_id=1, source_target_pairs={{0,4},{4,0},{8,12},{12,8},{1,5},{5,1},{9,13},{13,9},{2,6},{6,2},{1... | collective-permute-start | bytes 1671176 | tf_op jit(solution)/shard_map/ppermute | solution.py:335
  128.8 26.9 %collective-permute-start.28 = (bf16[128,2176]{1,0:T(8,128)(2,1)}, bf16[128,2176]{1,0:T(8,128)(2,1)S(1)}, u32[]{:S(2)}, u32[]{:S(2)}) collective-permute-start(bf16[128,2176]{1,0:T(8,128)(2,1)} %get-tuple-element.123), channel_id=1, source_target_pairs={{0,12},{4,8},{8,4},{12,0},{1,13},{5,9},{9,5},{13,1},{2,14},{6,10},... | collective-permute-start | bytes 1671176 | tf_op jit(solution)/shard_map/ppermute | solution.py:335
  129.1 26.6 %collective-permute-start.29 = (bf16[2048,256]{1,0:T(8,128)(2,1)}, bf16[2048,256]{1,0:T(8,128)(2,1)S(1)}, u32[]{:S(2)}, u32[]{:S(2)}) collective-permute-start(bf16[2048,256]{1,0:T(8,128)(2,1)} %get-tuple-element.124), channel_id=1, source_target_pairs={{0,2},{1,3},{2,0},{3,1},{4,6},{5,7},{6,4},{7,5},{8,10},{9,11},{10,... | collective-permute-start | bytes 3145736 | tf_op jit(solution)/shard_map/ppermute | solution.py:339
  135.6 20.2 %copy-start.20 = (bf16[128,2176]{1,0:T(8,128)(2,1)S(1)}, bf16[128,2176]{1,0:T(8,128)(2,1)}, u32[]{:S(2)}) copy-start(bf16[128,2176]{1,0:T(8,128)(2,1)} %get-tuple-element.97) | copy-start | bytes 1671172
  135.6 20.2 %copy-start.25 = (bf16[128,1536]{1,0:T(8,128)(2,1)S(1)}, bf16[128,1536]{1,0:T(8,128)(2,1)}, u32[]{:S(2)}) copy-start(bf16[128,1536]{1,0:T(8,128)(2,1)} %copy-done.24) | copy-start | bytes 1179652
  135.6 20.2 %copy-start.30 = (bf16[128,640]{1,0:T(8,128)(2,1)S(1)}, bf16[128,640]{1,0:T(8,128)(2,1)}, u32[]{:S(2)}) copy-start(bf16[128,640]{1,0:T(8,128)(2,1)} %copy-done.29) | copy-start | bytes 491524
  (2 other events, 1.6 us)
